TPU v7x, 32 devices: a whole 2x2x4 slice. The times are simulated.
32 devices in a mesh: band: 4 (over y, core), slab: 8 (over z, x).
Axes of the slice: x: 2, y: 2, z: 4, core: 2. Of those that a mesh axis runs over, the one named last changes fastest.
Arguments:
- bands: float32 [8, 192, 192, 192], P('band', 'slab'), may hold values from -8 to 8
- occupied: float32 [16, 192, 192, 192], P('band', 'slab'), may hold values from -8 to 8
- occ_index: int32 [2], replicated, may hold values from 0 to 15
- band_pick: int32 [8], P('band'), may hold values from 0 to 1
Outputs:
- exchange_out: float32 [8, 192, 192, 192], P('band', 'slab')
All inputs are finite; a program needn't handle non-finite values.
Results may differ from a plain program's by a relative error of at most 0.0001.
Values sent between devices are 32-bit elements; how exact they have to be, the bound alone decides.
No kernel may reach another device: no remote copies, remote signals or barrier semaphores. Data moves between devices by JAX's collectives and lax.ppermute only.
A program may use at most 192 MiB of HBM per device.

v0:
```python
import math

import jax
import jax.numpy as jnp
from jax import lax
from jax.sharding import PartitionSpec as P

grid_step = 0.25
omega = 0.106


def broadcast(x, axis, root):
    mine = lax.axis_index(axis) == root
    return lax.psum(jnp.where(mine, x, jnp.zeros_like(x)), axis)


def wave_squared(length):
    modes = jnp.arange(length, dtype=jnp.int32)
    signed = jnp.where(modes <= length // 2, modes, modes - length)
    wave = 2.0 * math.pi / (length * grid_step) * signed.astype(jnp.float32)
    return wave * wave


def screened(squares):
    nonzero = jnp.where(squares > 0, squares, jnp.ones_like(squares))
    value = 4.0 * math.pi * (1.0 - jnp.exp(-squares / (4.0 * omega * omega))) / nonzero
    return jnp.where(squares > 0, value, jnp.full_like(squares, math.pi / (omega * omega)))


def cas_matrix(length):
    indices = jnp.arange(length, dtype=jnp.int32)
    product = indices[:, None] * indices[None, :] % length
    phases = 2.0 * math.pi / length * product.astype(jnp.float32)
    return jnp.cos(phases) + jnp.sin(phases)


def along_z(values, matrix):
    return jnp.einsum("pxyz,zk->pxyk", values, matrix, precision=lax.Precision.HIGHEST)


def along_y(values, matrix):
    return jnp.einsum("pxyz,yk->pxkz", values, matrix, precision=lax.Precision.HIGHEST)


def along_x(values, matrix):
    return jnp.einsum("pxyz,xk->pkyz", values, matrix, precision=lax.Precision.HIGHEST)


def shards(bands, occupied, occ_index, band_pick):
    points = bands.shape[2]
    planes = bands.shape[1]
    window = occ_index.shape[0]
    per_group = occupied.shape[0]
    matrix = cas_matrix(points)
    squares = wave_squared(points)
    offset = lax.axis_index("slab") * planes
    row_squares = lax.dynamic_slice_in_dim(squares, offset, planes)
    kernel = screened(squares[:, None, None] + row_squares[None, :, None] + squares[None, None, :])
    kernel = kernel / float(points * points * points)
    targets = jnp.take(bands, band_pick, axis=0)

    def fetch_orbital(turn):
        which = occ_index[turn]
        owner_group = which // per_group
        own_orbital = lax.dynamic_index_in_dim(occupied, which % per_group, 0, keepdims=False)
        return broadcast(own_orbital, "band", owner_group)

    orbitals = lax.map(fetch_orbital, jnp.arange(window, dtype=jnp.int32))
    density = (orbitals[:, None] * targets[None]).reshape((-1,) + targets.shape[1:])
    filtered = lax.all_to_all(
        along_x(
            kernel[None]
            * along_x(
                lax.all_to_all(
                    along_y(along_z(density, matrix), matrix),
                    "slab",
                    split_axis=2,
                    concat_axis=1,
                    tiled=True,
                ),
                matrix,
            ),
            matrix,
        ),
        "slab",
        split_axis=1,
        concat_axis=2,
        tiled=True,
    )
    potential_field = along_z(along_y(filtered, matrix), matrix).reshape((window,) + targets.shape)
    result = -jnp.sum(potential_field * orbitals[:, None], axis=0)
    return result


def solution(mesh):
    placed = (P("band", "slab", None, None), P("band", "slab", None, None), P(), P("band"))
    return jax.shard_map(
        shards, mesh=mesh, in_specs=placed, out_specs=P("band", "slab", None, None), check_vma=False
    )
```

profile of v0, /device:TPU:0, one launch (start us, length us, event | category | flops | bytes accessed | tf_op | source)
XLA Modules:
  0.0 1329.1 jit_solution(17676627127279975511)
XLA Ops:
  6.5 6.4 mini-gather-slice
  13.0 2.5 gather_fusion.1
  15.4 6.5 gather_fusion
  22.0 7.9 maximum_select_fusion
  29.9 222.6 %while.12 = (s32[]{:T(128)}, f32[2,24,192,192]{3,2,1,0:T(8,128)}, s32[2]{0:T(128)S(1)}, s32[2]{0:T(128)S(1)}, f32[4,24,192,192]{3,2,1,0:T(8,128)}, /*index=5*/s3...) while((s32[]{:T(128)}, f32[2,24,192,192]{3,2,1,0:T(8,128)}, ...), condition=%wide.region_2.3_spmd, body=%wide.region_0.2_spmd.sunk | while | flops 1769503 | bytes 40108524 | solution.py:68
  29.9 0.6 dynamic_slice.29
  32.4 0.6 dynamic_slice.30
  35.6 5.0 dynamic-slice_select_fusion.2
  40.6 96.9 %all-reduce.2.cloned.1.call-done = f32[1,24,192,192]{3,2,1,0:T(8,128)} async-done(((f32[1,24,192,192]{3,2,1,0:T(8,128)}), f32[1,24,192,192]{3,2,1,0:T(8,128)}) %all-reduce.2.cloned.1.call-update) | async-done | bytes 3538960 | tf_op jit(solution)/shard_map/while/body/eval_jaxpr/psum | solution.py:14
  137.5 5.0 constant_dynamic-update-slice_fusion.2
  142.4 0.6 dynamic_slice.29
  145.0 0.6 dynamic_slice.30
  148.1 5.0 dynamic-slice_select_fusion.2
  153.1 94.3 %all-reduce.2.cloned.1.call-done = f32[1,24,192,192]{3,2,1,0:T(8,128)} async-done(((f32[1,24,192,192]{3,2,1,0:T(8,128)}), f32[1,24,192,192]{3,2,1,0:T(8,128)}) %all-reduce.2.cloned.1.call-update) | async-done | bytes 3538960 | tf_op jit(solution)/shard_map/while/body/eval_jaxpr/psum | solution.py:14
  247.5 5.0 constant_dynamic-update-slice_fusion.2
  252.5 8.1 broadcast_multiply_fusion
  260.6 20.3 %fusion.21 = f32[4,24,192,192]{3,2,1,0:T(8,128)} fusion(f32[4,24,192,192]{3,2,1,0:T(8,128)S(1)} %bitcast.53), kind=kOutput, calls=%fused_computation.31 | convolution fusion | flops 8154095616 | bytes 28311552 | tf_op jit(solution)/shard_map/pxyz,zk->pxyk/dot_general | solution.py:38
  280.9 22.4 %convolution_bitcast_fusion = f32[4,24,192,192]{3,2,1,0:T(8,128)S(1)} fusion(f32[4,24,192,192]{3,2,1,0:T(8,128)} %fusion.21), kind=kOutput, calls=%fused_computation.18 | convolution fusion | flops 8154095616 | bytes 28311552 | tf_op jit(solution)/shard_map/pxyz,yk->pxkz/dot_general | solution.py:42
  303.3 22.2 %copy.19 = f32[4,24,192,192]{3,1,0,2:T(8,128)} copy(f32[4,24,192,192]{3,2,1,0:T(8,128)S(1)} %convolution_bitcast_fusion) | data formatting | bytes 28311552 | tf_op jit(solution)/shard_map/pxyz,yk->pxkz/transpose | solution.py:42
  325.5 6.4 all-to-all-start
  332.1 3.4 fusion.12
  335.5 404.3 %all-to-all-done = f32[4,24,192,192]{3,1,0,2:T(8,128)} async-done(((f32[4,24,192,192]{3,1,0,2:T(8,128)}), f32[4,24,192,192]{3,1,0,2:T(8,128)}, u32[]{:S(2)}, u32[]{:S(2)}) %all-to-all-start) | async-done | bytes 14155808 | tf_op jit(solution)/shard_map/all_to_all | solution.py:74
  739.8 17.8 %copy.21 = f32[4,8,24,24,192]{4,3,2,1,0:T(8,128)} copy(f32[4,8,24,24,192]{4,2,0,3,1:T(8,128)} %bitcast.12) | data formatting | bytes 28311552 | tf_op jit(solution)/shard_map/all_to_all | solution.py:74
  757.6 31.5 %fusion.4 = f32[192,4,24,192]{3,0,2,1:T(8,128)} fusion(f32[4,192,24,192]{3,2,1,0:T(8,128)} %bitcast.54), kind=kOutput, calls=%fused_computation.8 | convolution fusion | flops 8154095616 | bytes 28311552 | tf_op jit(solution)/shard_map/pxyz,xk->pkyz/dot_general | solution.py:46
  789.1 25.0 %fusion.8 = f32[4,192,24,192]{3,1,2,0:T(8,128)} fusion(f32[192,4,24,192]{3,0,2,1:T(8,128)} %fusion.4, f32[192,24,192]{2,0,1:T(8,128)S(1)} %bitcast.51), kind=kOutput, calls=%fused_computation.19 | convolution fusion | flops 8157634560 | bytes 31850496 | tf_op jit(solution)/shard_map/pxyz,xk->pkyz/dot_general | solution.py:46
  814.2 22.1 %copy.25 = f32[4,192,24,192]{3,2,0,1:T(8,128)S(1)} copy(f32[4,192,24,192]{3,1,2,0:T(8,128)} %fusion.8) | data formatting | bytes 28311552 | tf_op jit(solution)/shard_map/pxyz,xk->pkyz/transpose | solution.py:46
  836.2 411.5 %all_to_all.36 = f32[4,192,24,192]{3,2,0,1:T(8,128)S(1)} all-to-all(f32[4,192,24,192]{3,2,0,1:T(8,128)S(1)} %copy.25), channel_id=1, replica_groups=mesh['band'=4,'slab'=8] {'slab'}, dimensions={1} | all-to-all | bytes 28311552 | tf_op jit(solution)/shard_map/all_to_all | solution.py:70
  1247.7 7.1 copy.27
  1254.9 25.6 %fusion.26 = f32[192,4,24,192]{3,0,2,1:T(8,128)} fusion(f32[4,24,192,192]{3,2,1,0:T(8,128)} %bitcast.56), kind=kOutput, calls=%fused_computation.36 | convolution fusion | flops 8154095616 | bytes 28311552 | tf_op jit(solution)/shard_map/pxyz,yk->pxkz/dot_general | solution.py:42
  1280.5 22.0 %fusion = f32[4,24,192,192]{3,2,1,0:T(8,128)S(1)} fusion(f32[192,4,24,192]{3,0,2,1:T(8,128)} %fusion.26), kind=kOutput, calls=%fused_computation.4 | convolution fusion | flops 8154095616 | bytes 28311552 | tf_op jit(solution)/shard_map/pxyz,zk->pxyk/dot_general | solution.py:38
  1302.5 10.8 multiply_reduce_fusion
  1313.3 8.5 neg.11
  (25 shorter events, 0.2 us)
Async XLA Ops:
  6.5 6.4 slice-start.2
  6.5 6.4 copy-start.1
  15.4 6.6 copy-start
  22.0 7.9 copy-start.2
  29.9 107.6 %all-reduce.2.cloned.1.call-start = ((), (), s32[]{:S(2)}) async-start(), calls=%async_computation.2 | async-start | bytes 9437184 | tf_op jit(solution)/shard_map/while/body/eval_jaxpr/psum | solution.py:14
  142.4 105.0 %all-reduce.2.cloned.1.call-start = ((), (), s32[]{:S(2)}) async-start(), calls=%async_computation.2 | async-start | bytes 9437184 | tf_op jit(solution)/shard_map/while/body/eval_jaxpr/psum | solution.py:14
  325.5 414.3 %all-to-all-start = ((f32[4,24,192,192]{3,1,0,2:T(8,128)}), f32[4,24,192,192]{3,1,0,2:T(8,128)}, u32[]{:S(2)}, u32[]{:S(2)}) async-start(f32[4,24,192,192]{3,1,0,2:T(8,128)} %copy.19), calls=%async_computation | async-start | bytes 37748736 | tf_op jit(solution)/shard_map/all_to_all | solution.py:74
  739.8 49.4 %slice-start = ((s8[4718592]{0:T(1024)(128)(4,1)}), s8[4194304]{0:T(1024)(128)(4,1)S(1)}, s32[]{:S(2)}) async-start(s8[4718592]{0:T(1024)(128)(4,1)} %bitcast.50), calls=%async_computation.3 | async-start | bytes 8388608
  757.6 31.5 %slice-start.1 = ((s8[4718592]{0:T(1024)(128)(4,1)}), s8[524288]{0:T(1024)(128)(4,1)S(1)}, s32[]{:S(2)}) async-start(s8[4718592]{0:T(1024)(128)(4,1)} %bitcast.50), calls=%async_computation.4 | async-start | bytes 1048576
Sparse Core Ops, SparseCore 0:
  40.7 96.7 all-reduce.1
  153.3 94.1 all-reduce.1
where the time goes:
time: 1340 us; the launch traced here: 1330 us
  waiting for transfers between devices  596 us (44%)
  blocking collectives  412 us (31%)
  matrix products  147 us (11%)
  local copies, waits for them, and re-layouts  97.2 us (7%)
  other arithmetic  48.8 us (4%)
  between operations  13.9 us (1%)
    all_to_all x1, blocking collectives, shards(): lax.all_to_all(along_x(kernel[None] * along_x(lax.all_to_all(along_y(alon...  412 us
    all_to_all x1, waiting for transfers between devices, shards(): lax.all_to_all(along_y(along_z(density, matrix), matrix), 'slab', split_a...  404 us
    psum x2, waiting for transfers between devices, broadcast(): return lax.psum(jnp.where(mine, x, jnp.zeros_like(x)), axis)  191 us
    dot_general x2, matrix products, along_x(): jnp.einsum('pxyz,xk->pkyz', values, matrix, precision=lax.Precision.HIGHEST)  56.6 us
    dot_general x2, matrix products, along_y(): jnp.einsum('pxyz,yk->pxkz', values, matrix, precision=lax.Precision.HIGHEST)  48 us
    dot_general x2, matrix products, along_z(): jnp.einsum('pxyz,zk->pxyk', values, matrix, precision=lax.Precision.HIGHEST)  42.3 us
  transfers between devices with their start and end apart: 3, of which 3 were waited for; matrix products, arithmetic and copies ran while one was open for 0% of the time, Pallas kernels for 0%

commit v1 on v0

v1 whole, which is shorter than its diff:
```python
import math

import jax
import jax.numpy as jnp
from jax import lax
from jax.experimental import pallas as pl
from jax.experimental.pallas import tpu as pltpu
from jax.sharding import PartitionSpec as P

grid_step = 0.25
omega = 0.106
CORES = 2
LANES = 128
STEP = 4
SPLIT = (3, 3, 3, 3)
HALVES = ((0, 1), (2, 3))
VMEM_LIMIT = 56 * 1024 * 1024


def wave_squared(modes, length):
    signed = jnp.where(modes <= length // 2, modes, modes - length)
    wave = 2.0 * math.pi / (length * grid_step) * signed.astype(jnp.float32)
    return wave * wave


def screened(squares):
    nonzero = jnp.where(squares > 0, squares, jnp.ones_like(squares))
    value = 4.0 * math.pi * (1.0 - jnp.exp(-squares / (4.0 * omega * omega))) / nonzero
    return jnp.where(squares > 0, value, jnp.full_like(squares, math.pi / (omega * omega)))


def cas_matrix(rows, columns, length):
    product = rows[:, None] * columns[None, :] % length
    phases = 2.0 * math.pi / length * product.astype(jnp.float32)
    return jnp.cos(phases) + jnp.sin(phases)


def halves(values):
    high = values.astype(jnp.bfloat16)
    low = (values - high.astype(jnp.float32)).astype(jnp.bfloat16)
    return high, low


def multiply(left, right):
    def dot(a, b):
        return jnp.dot(a, b, preferred_element_type=jnp.float32)

    return dot(left[0], right[0]) + (dot(left[0], right[1]) + dot(left[1], right[0]))


def pack_body(scalars, keep_ref, give_ref, keep_out, give_out):
    for source, out in ((keep_ref, keep_out), (give_ref, give_out)):
        rows = jnp.swapaxes(source[0], 0, 1)
        out[0, 0, 0] = rows[:STEP, :, :LANES]
        out[0, 0, 1] = rows[STEP:, :, :LANES]
        out[0, 0, 2] = jnp.concatenate([rows[:STEP, :, LANES:], rows[STEP:, :, LANES:]], axis=-1)


def pack(stored, scalars, units):
    count = scalars.shape[0] - 2
    planes, points = stored.shape[1], stored.shape[3]
    block = (1, 1, 3, STEP, planes, LANES)
    shape = jax.ShapeDtypeStruct((count, units) + block[2:], jnp.float32)
    spec = pl.BlockSpec(block, lambda i, u, s: (i, u, 0, 0, 0, 0))
    return pl.pallas_call(
        pack_body,
        grid_spec=pltpu.PrefetchScalarGridSpec(
            num_scalar_prefetch=1,
            grid=(count, units),
            in_specs=[
                pl.BlockSpec((1, planes, 2 * STEP, points), lambda i, u, s: (s[i], 0, s[count] + u, 0)),
                pl.BlockSpec((1, planes, 2 * STEP, points), lambda i, u, s: (s[i], 0, s[count + 1] + u, 0)),
            ],
            out_specs=[spec, spec],
        ),
        out_shape=[shape, shape],
        compiler_params=pltpu.CompilerParams(vmem_limit_bytes=VMEM_LIMIT),
        name="pack",
    )(scalars, stored, stored)


def unpack_body(scalars, keep_ref, got_ref, *rest):
    out = rest[-1]

    def place(source):
        lower = jnp.concatenate([source[0, 0, 0], source[0, 0, 2][:, :, : LANES // 2]], axis=-1)
        upper = jnp.concatenate([source[0, 0, 1], source[0, 0, 2][:, :, LANES // 2 :]], axis=-1)
        out[0] = jnp.swapaxes(jnp.concatenate([lower, upper], axis=0), 0, 1)

    pl.when(pl.program_id(1) == 0)(lambda: place(keep_ref))
    pl.when(pl.program_id(1) == 1)(lambda: place(got_ref))


def unpack(keep, got, scalars, shape, earlier):
    count, units = keep.shape[:2]
    planes, points = shape[1], shape[3]
    block = (1, 1, 3, STEP, planes, LANES)
    kept = pl.BlockSpec(block, lambda i, k, u, s: (i, jnp.where(k == 0, u, units - 1), 0, 0, 0, 0))
    other = pl.BlockSpec(block, lambda i, k, u, s: (i, jnp.where(k == 0, 0, u), 0, 0, 0, 0))
    held = [] if earlier is None else [earlier]
    return pl.pallas_call(
        unpack_body,
        grid_spec=pltpu.PrefetchScalarGridSpec(
            num_scalar_prefetch=1,
            grid=(count, 2, units),
            in_specs=[kept, other] + [pl.BlockSpec(memory_space=pl.ANY) for _ in held],
            out_specs=pl.BlockSpec(
                (1, planes, 2 * STEP, points), lambda i, k, u, s: (s[i], 0, s[count + k] + u, 0)
            ),
        ),
        out_shape=jax.ShapeDtypeStruct(shape, jnp.float32),
        input_output_aliases={3: 0} if held else {},
        compiler_params=pltpu.CompilerParams(vmem_limit_bytes=VMEM_LIMIT),
        name="unpack",
    )(scalars, keep, got, *held)


def orbital_parts(same, first, second):
    pieces = range(first.shape[0])
    near = [jnp.where(same, first[d, 0], second[d, 0]) for d in pieces]
    far = [jnp.where(same, second[d, 0], first[d, 0]) for d in pieces]
    return near + far


def forward_body(scalars, near, far, first, second, lower_ref, upper_ref, planes_ref, keep_out, give_out):
    orbitals = orbital_parts(scalars[0] == 1, first, second)
    targets = [part[d, 0] for part in (near, far) for d in range(part.shape[0])]
    density = jnp.concatenate([t * o for t, o in zip(targets, orbitals)], axis=2)
    step, points = density.shape[1], density.shape[2]
    matrix = halves(planes_ref[...])
    results = []
    for part, weights in ((0, lower_ref), (1, upper_ref)):
        packed = jnp.concatenate([density[part], density[2]], axis=-1).reshape(step * points, 2 * LANES)
        lines = multiply(halves(packed), halves(weights[...]))
        high, low = halves(lines)
        for row in range(step):
            where = slice(row * points, (row + 1) * points)
            results.append(multiply(matrix, (high[where], low[where])))
    spectrum = jnp.swapaxes(jnp.stack(results), 0, 1)
    keep_out[...] = spectrum[: points // 2]
    give_out[...] = spectrum[points // 2 :]


def stacked(array, offset):
    return pl.BlockSpec((array.shape[0], 1) + array.shape[2:], lambda u, s: (0, u + offset, 0, 0, 0, 0))


def forward(near, far, first, second, offset, scalars, lower, upper, planes_matrix):
    units, points = near.shape[1], planes_matrix.shape[0]
    whole = lambda a: pl.BlockSpec(a.shape, lambda u, s: (0, 0))
    out = pl.BlockSpec((points // 2, 2 * STEP, points), lambda u, s: (0, u, 0))
    shape = jax.ShapeDtypeStruct((points // 2, 2 * STEP * units, points), jnp.float32)
    return pl.pallas_call(
        forward_body,
        grid_spec=pltpu.PrefetchScalarGridSpec(
            num_scalar_prefetch=1,
            grid=(units,),
            in_specs=[stacked(near, 0), stacked(far, 0), stacked(first, offset), stacked(second, offset)]
            + [whole(lower), whole(upper), whole(planes_matrix)],
            out_specs=[out, out],
        ),
        out_shape=[shape, shape],
        compiler_params=pltpu.CompilerParams(vmem_limit_bytes=VMEM_LIMIT),
        name="forward",
    )(scalars, near, far, first, second, lower, upper, planes_matrix)


def middle_body(count, kernel_ref, forth_ref, back_ref, *refs):
    ins, outs = refs[:count], refs[count:]
    forth, back = halves(forth_ref[...]), halves(back_ref[...])
    for k in range(kernel_ref.shape[0]):
        rows = jnp.concatenate([r[k] for r in ins], axis=0)
        spectrum = multiply(forth, halves(rows)) * kernel_ref[k]
        filtered = multiply(back, halves(spectrum))
        start = 0
        for out in outs:
            out[k] = filtered[start : start + out.shape[1]]
            start += out.shape[1]


def middle(spectra, kernel, forth, back):
    count = len(spectra)
    deep, _, points = spectra[0].shape
    block = 4
    parts = [pl.BlockSpec((block,) + a.shape[1:], lambda k: (k, 0, 0)) for a in spectra]
    whole = pl.BlockSpec((points, points), lambda k: (0, 0))
    return pl.pallas_call(
        lambda *refs: middle_body(count, *refs),
        grid=(deep // block,),
        in_specs=[pl.BlockSpec((block, points, points), lambda k: (k, 0, 0)), whole, whole] + parts,
        out_specs=parts,
        out_shape=[jax.ShapeDtypeStruct(a.shape, jnp.float32) for a in spectra],
        compiler_params=pltpu.CompilerParams(vmem_limit_bytes=VMEM_LIMIT),
        name="middle",
    )(kernel, forth, back, *spectra)


def inverse_body(scalars, keep_ref, got_ref, first, second, lower_ref, upper_ref, planes_ref, near, far):
    spectrum = jnp.swapaxes(jnp.concatenate([keep_ref[...], got_ref[...]], axis=0), 0, 1)
    points = spectrum.shape[1]
    step = spectrum.shape[0] // 2
    matrix = halves(planes_ref[...])
    packed = []
    for part, weights in ((0, lower_ref), (1, upper_ref)):
        lines = jnp.concatenate(
            [multiply(matrix, halves(spectrum[part * step + row])) for row in range(step)], axis=0
        )
        packed.append(multiply(halves(lines), halves(weights[...])).reshape(step, points, 2 * LANES))
    low, high = packed
    field = [low[:, :, :LANES], high[:, :, :LANES], low[:, :, LANES:] + high[:, :, LANES:]]
    orbitals = orbital_parts(scalars[0] == 1, first, second)
    outs = [(part, d) for part in (near, far) for d in range(part.shape[0])]
    planes = points // len(outs)
    for i, (orbital, (out, d)) in enumerate(zip(orbitals, outs)):
        for part in range(3):
            out[d, 0, part] = -field[part][:, i * planes : (i + 1) * planes] * orbital[part]


def inverse(keep, got, first, second, offset, scalars, lower, upper, planes_matrix):
    deep, rows, points = keep.shape
    units = rows // (2 * STEP)
    whole = lambda a: pl.BlockSpec(a.shape, lambda u, s: (0, 0))
    part = pl.BlockSpec((deep, 2 * STEP, points), lambda u, s: (0, u, 0))
    shape = jax.ShapeDtypeStruct(first.shape[:1] + (units,) + first.shape[2:], jnp.float32)
    return pl.pallas_call(
        inverse_body,
        grid_spec=pltpu.PrefetchScalarGridSpec(
            num_scalar_prefetch=1,
            grid=(units,),
            in_specs=[part, part, stacked(first, offset), stacked(second, offset)]
            + [whole(lower), whole(upper), whole(planes_matrix)],
            out_specs=[stacked(shape, 0)] * 2,
        ),
        out_shape=[shape] * 2,
        compiler_params=pltpu.CompilerParams(vmem_limit_bytes=VMEM_LIMIT),
        name="inverse",
    )(scalars, keep, got, first, second, lower, upper, planes_matrix)


def by_layers(bands, occupied, occ_index, band_pick, groups, slabs):
    picks, window = band_pick.shape[0], occ_index.shape[0]
    per_group, planes, points = occupied.shape[0], bands.shape[1], bands.shape[2]
    sides = window
    layers = slabs // sides
    half_rows = points // CORES
    units = half_rows // (2 * STEP)
    chunks = len(SPLIT)
    starts = [sum(SPLIT[:j]) for j in range(chunks)]

    band, slab = lax.axis_index("band"), lax.axis_index("slab")
    y, c = band // CORES, band % CORES
    z, x = slab // sides, slab % sides

    def swap(values, axis, size, flip):
        return lax.ppermute(values, axis, [(i, flip(i)) for i in range(size)])

    def over_core(values):
        return swap(values, "band", groups, lambda i: i ^ 1)

    def over_y(values):
        return swap(values, "band", groups, lambda i: i ^ CORES)

    def over_x(values):
        return swap(values, "slab", slabs, lambda i: i ^ 1)

    def over_z(values, d):
        return swap(values, "slab", slabs, lambda i: i ^ (d * sides))

    layer_of = z ^ jnp.arange(layers, dtype=jnp.int32)
    side_of = x ^ jnp.arange(sides, dtype=jnp.int32)
    slab_of = (side_of[:, None] + sides * layer_of[None, :]).reshape(-1)
    plane_of = (slab_of[:, None] * planes + jnp.arange(planes, dtype=jnp.int32)).reshape(-1)
    core_of = c ^ jnp.arange(CORES, dtype=jnp.int32)
    all_modes = jnp.arange(points, dtype=jnp.int32)
    mode_of = (core_of[:, None] * half_rows + jnp.arange(half_rows, dtype=jnp.int32)).reshape(-1)

    columns = cas_matrix(all_modes, all_modes, points)
    empty = jnp.zeros((points - LANES, points), jnp.float32)
    lower = jnp.concatenate([columns, empty], axis=0)
    upper = jnp.concatenate([columns[:LANES], empty, columns[LANES:]], axis=0)
    lower_back = jnp.concatenate([columns, empty.T], axis=1)
    upper_back = jnp.concatenate([columns[:, :LANES], empty.T, columns[:, LANES:]], axis=1)
    to_modes = cas_matrix(mode_of, plane_of, points)
    to_planes = cas_matrix(plane_of, mode_of, points)
    forth = cas_matrix(all_modes, mode_of, points)
    back = cas_matrix(mode_of, all_modes, points)
    squares = wave_squared(all_modes, points)
    own_squares = wave_squared(c * half_rows + jnp.arange(half_rows, dtype=jnp.int32), points)
    kernel = screened(own_squares[:, None, None] + squares[None, :, None] + squares[None, None, :])
    kernel = kernel / float(points * points * points)

    first_bit = z % picks
    target_index = band_pick[jnp.arange(picks, dtype=jnp.int32) ^ first_bit]
    which = occ_index[side_of]
    owner = which // per_group
    owner_y, owner_core = owner // CORES, owner % CORES
    here = z // picks == c
    same = x == y
    flag = same.astype(jnp.int32)[None]

    def row_blocks(start):
        return jnp.stack([c * units + start, (1 - c) * units + start])

    def sync(*values):
        return lax.optimization_barrier(values)

    def pack_orbital(h):
        chosen = HALVES[h]
        size = sum(SPLIT[j] for j in chosen)
        return pack(occupied, jnp.concatenate([which % per_group, row_blocks(starts[chosen[0]])]), size)

    def pack_target(j):
        return pack(bands, jnp.concatenate([target_index, row_blocks(starts[j])]), SPLIT[j])

    def prepare_orbital(keep, got):
        mine = jnp.where(owner_core[0] == c, keep[0], got[0])
        theirs = jnp.where(owner_core[1] == c, keep[1], got[1])
        other = over_x(theirs)
        send = jnp.where(same, other, mine)
        stay = jnp.where(same, mine, other)
        return jnp.where(owner_y[0] == y, stay, over_y(send))

    def choose_targets(keep, got):
        pieces = []
        for d in range(layers):
            a, b = (keep, got) if d < picks else (got, keep)
            pieces.append(jnp.where(here, a[d % picks], b[d % picks]))
        return pieces

    def along_layers(pieces, carried):
        got, reached, size = [], [], pieces[0].shape[0]
        for d, piece in enumerate(pieces):
            if d == 0:
                got.append(piece)
                reached.append(carried)
            elif carried is None:
                got.append(over_z(piece, d))
            elif d & (d - 1):
                reach = d & -d
                got.append(over_z(piece, d))
                reached.append(over_z(reached[d - reach], reach))
            else:
                both = over_z(jnp.concatenate([piece, carried], axis=0), d)
                got.append(both[:size])
                reached.append(both[size:])
        return jnp.stack(got), None if carried is None else jnp.stack(reached)

    constants = sync(kernel, lower, upper, to_modes, to_planes, forth, back, lower_back, upper_back)
    orbital_give, target_give = {}, {}
    orbital_keep, orbital_got, target_keep, target_got = {}, {}, {}, {}
    orbital_keep[0], orbital_give[0] = pack_orbital(0)
    target_keep[0], target_give[0] = pack_target(0)
    orbital_got[0] = over_core(orbital_give[0])
    target_got[0] = over_core(target_give[0])
    orbital_keep[1], orbital_give[1] = pack_orbital(1)
    target_keep[1], target_give[1] = pack_target(1)
    orbital_got[0], target_got[0], orbital_give[1], target_give[1] = sync(
        orbital_got[0], target_got[0], orbital_give[1], target_give[1]
    )
    carried0 = prepare_orbital(orbital_keep[0], orbital_got[0])
    near0, _ = along_layers(choose_targets(target_keep[0], target_got[0]), None)
    orbital_got[1] = over_core(orbital_give[1])
    target_got[1] = over_core(target_give[1])
    target_keep[2], target_give[2] = pack_target(2)
    carried0, near0, orbital_got[1], target_got[1], target_give[2], constants = sync(
        carried0, near0, orbital_got[1], target_got[1], target_give[2], constants
    )
    kernel, lower, upper, to_modes, to_planes, forth, back, lower_back, upper_back = constants
    near1, first0 = along_layers(choose_targets(target_keep[1], target_got[1]), carried0)
    far0 = over_x(near0)
    carried1 = prepare_orbital(orbital_keep[1], orbital_got[1])
    target_got[2] = over_core(target_give[2])
    target_keep[3], target_give[3] = pack_target(3)
    near1, first0, far0, carried1, target_got[2], target_give[3] = sync(
        near1, first0, far0, carried1, target_got[2], target_give[3]
    )
    near2, first1 = along_layers(choose_targets(target_keep[2], target_got[2]), carried1)
    far1 = over_x(near1)
    second0 = over_y(first0)
    target_got[3] = over_core(target_give[3])
    near2, first1, far1, second0, target_got[3] = sync(near2, first1, far1, second0, target_got[3])
    near3, _ = along_layers(choose_targets(target_keep[3], target_got[3]), None)
    far2 = over_x(near2)
    second1 = over_y(first1)
    keep0, give0 = forward(near0, far0, first0, second0, 0, flag, lower, upper, to_modes)
    near3, far2, keep0, give0 = sync(near3, far2, keep0, give0)
    far3 = over_x(near3)
    spectra_got = {0: over_core(give0)}
    keep1, give1 = forward(near1, far1, first0, second0, SPLIT[0], flag, lower, upper, to_modes)
    spectra_got[1] = over_core(give1)
    keep2, give2 = forward(near2, far2, first1, second1, 0, flag, lower, upper, to_modes)
    spectra_got[2] = over_core(give2)
    keep3, give3 = forward(near3, far3, first1, second1, SPLIT[2], flag, lower, upper, to_modes)
    spectra_got[3] = over_core(give3)

    order = range(chunks)
    filtered = middle([keep0, keep1, keep2, keep3] + [spectra_got[j] for j in order], kernel, forth, back)

    orbit = [(first0, second0, 0), (first0, second0, SPLIT[0]), (first1, second1, 0), (first1, second1, SPLIT[2])]
    result = None
    queue = list(reversed(order))
    back_got = {j: over_core(filtered[chunks + j]) for j in queue}
    fields, home = {}, {}
    for turn in range(chunks + 2):
        if turn < chunks:
            j = queue[turn]
            fields[j] = inverse(filtered[j], back_got[j], *orbit[j], flag, lower_back, upper_back, to_planes)
        if turn:
            fields, home, result = sync(fields, home, result)
            fields, home = dict(fields), dict(home)
        if turn < chunks:
            near, far = fields[j]
            fields[j] = near, over_x(far)
        if 0 <= turn - 1 < chunks:
            j = queue[turn - 1]
            near, got = fields.pop(j)
            home[j] = [near[d] + got[d] for d in range(layers)]
            home[j] = [piece if d == 0 else over_z(piece, d) for d, piece in enumerate(home[j])]
        if 0 <= turn - 2:
            j = queue[turn - 2]
            pieces = home.pop(j)
            near, far = jnp.stack(pieces[:picks]), jnp.stack(pieces[picks:])
            keep = jnp.where(here, near, far)
            got = over_core(jnp.where(here, far, near))
            index = jnp.arange(picks, dtype=jnp.int32) ^ first_bit
            shape = (picks,) + bands.shape[1:]
            result = unpack(keep, got, jnp.concatenate([index, row_blocks(starts[j])]), shape, result)
    return result


def broadcast(x, axis, root):
    mine = lax.axis_index(axis) == root
    return lax.psum(jnp.where(mine, x, jnp.zeros_like(x)), axis)


def by_lines(bands, occupied, occ_index, band_pick):
    points, planes = bands.shape[2], bands.shape[1]
    window, per_group = occ_index.shape[0], occupied.shape[0]
    modes = jnp.arange(points, dtype=jnp.int32)
    matrix = cas_matrix(modes, modes, points)
    squares = wave_squared(modes, points)

    def transform(pattern, values):
        return jnp.einsum(pattern, values, matrix, precision=lax.Precision.HIGHEST)

    along_z, along_y, along_x = "pxyz,zk->pxyk", "pxyz,yk->pxkz", "pxyz,xk->pkyz"
    offset = lax.axis_index("slab") * planes
    row_squares = lax.dynamic_slice_in_dim(squares, offset, planes)
    kernel = screened(squares[:, None, None] + row_squares[None, :, None] + squares[None, None, :])
    kernel = kernel / float(points * points * points)
    targets = jnp.take(bands, band_pick, axis=0)

    def fetch_orbital(turn):
        which = occ_index[turn]
        own_orbital = lax.dynamic_index_in_dim(occupied, which % per_group, 0, keepdims=False)
        return broadcast(own_orbital, "band", which // per_group)

    orbitals = lax.map(fetch_orbital, jnp.arange(window, dtype=jnp.int32))
    density = (orbitals[:, None] * targets[None]).reshape((-1,) + targets.shape[1:])
    lines = transform(along_y, transform(along_z, density))
    lines = lax.all_to_all(lines, "slab", split_axis=2, concat_axis=1, tiled=True)
    lines = transform(along_x, kernel[None] * transform(along_x, lines))
    lines = lax.all_to_all(lines, "slab", split_axis=1, concat_axis=2, tiled=True)
    field = transform(along_z, transform(along_y, lines)).reshape((window,) + targets.shape)
    return -jnp.sum(field * orbitals[:, None], axis=0)


def solution(mesh):
    groups, slabs = mesh.shape["band"], mesh.shape["slab"]

    def shards(bands, occupied, occ_index, band_pick):
        picks, window = band_pick.shape[0], occ_index.shape[0]
        planes, points = bands.shape[1], bands.shape[2]
        fits = (
            window == 2
            and picks == 2
            and bands.shape[0] == picks
            and groups == 2 * CORES
            and slabs == CORES * picks * window
            and planes % 8 == 0
            and 2 * (points - LANES) == LANES
            and points == CORES * 2 * STEP * sum(SPLIT)
        )
        if fits:
            return by_layers(bands, occupied, occ_index, band_pick, groups, slabs)
        return by_lines(bands, occupied, occ_index, band_pick)

    placed = (P("band", "slab", None, None), P("band", "slab", None, None), P(), P("band"))
    return jax.shard_map(
        shards, mesh=mesh, in_specs=placed, out_specs=P("band", "slab", None, None), check_vma=False
    )
```

time: 1340 us -> 688 us (0.51)
  blocking collectives: 412 us -> 0 us
  waiting for transfers between devices: 596 us -> 356 us
  Pallas kernels: 0 us -> 194 us
  matrix products: 147 us -> 0 us
  local copies, waits for them, and re-layouts: 97.2 us -> 24.5 us
  starting transfers between devices: 6.37 us -> 56.5 us
    all_to_all x1 -> x0, blocking collectives: 412 us -> none  [shards(): lax.all_to_all(along_x(kernel[None] * along_x(lax.all_to_all(along_y(alon...]
    all_to_all x1 -> x0, waiting for transfers between devices: 404 us -> none  [shards(): lax.all_to_all(along_y(along_z(density, matrix), matrix), 'slab', split_a...]
    ppermute x0 -> x58, waiting for transfers between devices: none -> 356 us  [swap(): return lax.ppermute(values, axis, [(i, flip(i)) for i in range(size)])]
    pallas_call x0 -> x19, Pallas kernels: none -> 194 us  [the longest x4 45.1 us: forward(): pl.pallas_call(forward_body, grid_spec=pltpu.PrefetchScalarGridSpec(num_s...]
    psum x2 -> x0, waiting for transfers between devices: 191 us -> none  [broadcast(): return lax.psum(jnp.where(mine, x, jnp.zeros_like(x)), axis)]
    dot_general x6 -> x0, matrix products: 147 us -> none  [the longest x2 56.6 us: along_x(): jnp.einsum('pxyz,xk->pkyz', values, matrix, precision=lax.Precision.HIGHEST)]
    ppermute x0 -> x58, starting transfers between devices: none -> 56.5 us  [swap(): return lax.ppermute(values, axis, [(i, flip(i)) for i in range(size)])]
    transpose x2 -> x0, local copies, waits for them, and re-layouts: 44.3 us -> none  [the longest x1 22.2 us: along_y(): jnp.einsum('pxyz,yk->pxkz', values, matrix, precision=lax.Precision.HIGHEST)]
  transfers between devices with their start and end apart: 3 -> 58, of which waited for: 3 -> 25; matrix products, arithmetic and copies ran while one was open for 0% -> 8% of each run, Pallas kernels for 0% -> 21%
where the time goes in v1:
time: 688 us; the launch traced here: 685 us
  waiting for transfers between devices  356 us (52%)
  Pallas kernels  194 us (28%)
  starting transfers between devices  56.5 us (8%)
  other arithmetic  52 us (8%)
  local copies, waits for them, and re-layouts  24.5 us (4%)
    ppermute x58, waiting for transfers between devices, swap(): return lax.ppermute(values, axis, [(i, flip(i)) for i in range(size)])  356 us
    ppermute x58, starting transfers between devices, swap(): return lax.ppermute(values, axis, [(i, flip(i)) for i in range(size)])  56.5 us
    pallas_call x4, Pallas kernels, forward(): pl.pallas_call(forward_body, grid_spec=pltpu.PrefetchScalarGridSpec(num_s...  45.1 us
    pallas_call x6, Pallas kernels, pack(): pl.pallas_call(pack_body, grid_spec=pltpu.PrefetchScalarGridSpec(num_scal...  42.5 us
    pallas_call x4, Pallas kernels, inverse(): pl.pallas_call(inverse_body, grid_spec=pltpu.PrefetchScalarGridSpec(num_s...  37.6 us
    pallas_call x4, Pallas kernels, unpack(): pl.pallas_call(unpack_body, grid_spec=pltpu.PrefetchScalarGridSpec(num_sc...  34.7 us
    pallas_call x1, Pallas kernels, middle(): pl.pallas_call(lambda *refs: middle_body(count, *refs), grid=(deep // blo...  34.4 us
    unnamed x84, local copies, waits for them, and re-layouts  15.5 us
  transfers between devices with their start and end apart: 58, of which 25 were waited for; matrix products, arithmetic and copies ran while one was open for 8% of the time, Pallas kernels for 21%

profile of v1, /device:TPU:0, one launch (start us, length us, event | category | flops | bytes accessed | tf_op | source)
XLA Modules:
  0.0 684.8 jit_solution(17557595927818723836)
XLA Ops:
  9.0 9.6 %pack.6 = (f32[2,6,3,4,24,128]{5,4,3,2,1,0:T(8,128)}, f32[2,6,3,4,24,128]{5,4,3,2,1,0:T(8,128)}) custom-call(s32[4]{0:T(128)} %get-tuple-element.295.scalars, f32[4,24,192,192]{3,2,1,0:T(8,128)} %give_ref.8, f32[4,24,192,192]{3,2,1,0:T(8,128)} %give_ref.8), custom_call_target="tpu_custom_call" | custom-call | tf_op jit(solution)/shard_map/pack/pallas_call | solution.py:65
  18.7 9.5 %fusion.1.refs_0_ = f32[96,192,192]{2,1,0:T(8,128)} fusion(f32[192]{0:T(256)S(1)} %fusion.44, f32[96,192]{1,0:T(8,128)S(1)} %broadcast_add_fusion), kind=kLoop, calls=%fused_computation.6 | loop fusion | flops 35389440 | bytes 14230272 | tf_op jit(solution)/shard_map/div | solution.py:290
  35.1 9.7 %pack.8 = (f32[2,6,3,4,24,128]{5,4,3,2,1,0:T(8,128)}, f32[2,6,3,4,24,128]{5,4,3,2,1,0:T(8,128)}) custom-call(s32[4]{0:T(128)} %get-tuple-element.294.scalars, f32[4,24,192,192]{3,2,1,0:T(8,128)} %give_ref.8, f32[4,24,192,192]{3,2,1,0:T(8,128)} %give_ref.8), custom_call_target="tpu_custom_call" | custom-call | tf_op jit(solution)/shard_map/pack/pallas_call | solution.py:65
  55.1 13.8 %collective-permute-done.2 = f32[6,3,4,24,128]{4,3,2,1,0:T(8,128)} collective-permute-done((f32[6,3,4,24,128]{4,3,2,1,0:T(8,128)}, f32[6,3,4,24,128]{4,3,2,1,0:T(8,128)}, u32[]{:S(2)}, u32[]{:S(2)}) %collective-permute-start.2) | collective-permute-done | bytes 884768 | tf_op jit(solution)/shard_map/ppermute | solution.py:255
  92.8 6.5 collective-permute-done.6
  99.3 7.4 %collective-permute-done.4 = f32[3,3,4,24,128]{4,3,2,1,0:T(8,128)S(1)} collective-permute-done((f32[3,3,4,24,128]{4,3,2,1,0:T(8,128)S(1)}, f32[3,3,4,24,128]{4,3,2,1,0:T(8,128)S(1)}, u32[]{:S(2)}, u32[]{:S(2)}) %collective-permute-start.4) | collective-permute-done | bytes 442400 | tf_op jit(solution)/shard_map/ppermute | solution.py:255
  127.3 9.7 %collective-permute-done.14 = f32[6,3,4,24,128]{4,3,2,1,0:T(8,128)S(1)} collective-permute-done((f32[6,3,4,24,128]{4,3,2,1,0:T(8,128)S(1)}, f32[6,3,4,24,128]{4,3,2,1,0:T(8,128)S(1)}, u32[]{:S(2)}, u32[]{:S(2)}) %collective-permute-start.14) | collective-permute-done | bytes 884768 | tf_op jit(solution)/shard_map/ppermute | solution.py:255
  140.1 35.4 %collective-permute-done.10 = f32[9,3,4,24,128]{4,3,2,1,0:T(8,128)} collective-permute-done((f32[9,3,4,24,128]{4,3,2,1,0:T(8,128)}, f32[9,3,4,24,128]{4,3,2,1,0:T(8,128)}, u32[]{:S(2)}, u32[]{:S(2)}) %collective-permute-start.10) | collective-permute-done | bytes 1327136 | tf_op jit(solution)/shard_map/ppermute | solution.py:255
  186.2 10.8 %collective-permute-done.15 = f32[6,3,4,24,128]{4,3,2,1,0:T(8,128)S(1)} collective-permute-done((f32[6,3,4,24,128]{4,3,2,1,0:T(8,128)S(1)}, f32[6,3,4,24,128]{4,3,2,1,0:T(8,128)S(1)}, u32[]{:S(2)}, u32[]{:S(2)}) %collective-permute-start.15) | collective-permute-done | bytes 884768 | tf_op jit(solution)/shard_map/ppermute | solution.py:255
  198.5 7.2 %collective-permute-done.12 = f32[6,3,4,24,128]{4,3,2,1,0:T(8,128)S(1)} collective-permute-done((f32[6,3,4,24,128]{4,3,2,1,0:T(8,128)S(1)}, f32[6,3,4,24,128]{4,3,2,1,0:T(8,128)S(1)}, u32[]{:S(2)}, u32[]{:S(2)}) %collective-permute-start.12) | collective-permute-done | bytes 884768 | tf_op jit(solution)/shard_map/ppermute | solution.py:255
  213.1 56.8 %collective-permute-done.18 = f32[9,3,4,24,128]{4,3,2,1,0:T(8,128)S(1)} collective-permute-done((f32[9,3,4,24,128]{4,3,2,1,0:T(8,128)S(1)}, f32[9,3,4,24,128]{4,3,2,1,0:T(8,128)S(1)}, u32[]{:S(2)}, u32[]{:S(2)}) %collective-permute-start.18) | collective-permute-done | bytes 1327136 | tf_op jit(solution)/shard_map/ppermute | solution.py:255
  277.4 17.5 %collective-permute-done.20 = f32[6,3,4,24,128]{4,3,2,1,0:T(8,128)S(1)} collective-permute-done((f32[6,3,4,24,128]{4,3,2,1,0:T(8,128)S(1)}, f32[6,3,4,24,128]{4,3,2,1,0:T(8,128)S(1)}, u32[]{:S(2)}, u32[]{:S(2)}) %collective-permute-start.20) | collective-permute-done | bytes 884768 | tf_op jit(solution)/shard_map/ppermute | solution.py:255
  303.7 11.4 %forward.4 = (f32[96,24,192]{2,1,0:T(8,128)}, f32[96,24,192]{2,1,0:T(8,128)}) custom-call(s32[1]{0:T(128)} %bitcast.2.scalars, f32[4,3,3,4,24,128]{5,4,3,2,1,0:T(8,128)} %copy-done.6, f32[4,3,3,4,24,128]{5,4,3,2,1,0:T(8,128)} %copy-done.22, f32[4,6,3,4,24,128]{5,4,3,2,1,0:T(8,128)} %copy-done.3, f32[4,6,3,4,24,128]{5,4,3,2,1,0:T(8,128)} %copy-done.4, ...), custom_call_target="tpu_custom_call" | custom-call | tf_op jit(solution)/shard_map/forward/pallas_call | solution.py:153
  315.0 17.5 %collective-permute-done.25 = f32[3,3,4,24,128]{4,3,2,1,0:T(8,128)} collective-permute-done((f32[3,3,4,24,128]{4,3,2,1,0:T(8,128)}, f32[3,3,4,24,128]{4,3,2,1,0:T(8,128)}, u32[]{:S(2)}, u32[]{:S(2)}) %collective-permute-start.25) | collective-permute-done | bytes 442400 | tf_op jit(solution)/shard_map/ppermute | solution.py:255
  338.4 11.3 %forward.5 = (f32[96,24,192]{2,1,0:T(8,128)}, f32[96,24,192]{2,1,0:T(8,128)}) custom-call(s32[1]{0:T(128)} %bitcast.2.scalars, f32[4,3,3,4,24,128]{5,4,3,2,1,0:T(8,128)} %copy-done.7, f32[4,3,3,4,24,128]{5,4,3,2,1,0:T(8,128)} %copy-done.23, f32[4,6,3,4,24,128]{5,4,3,2,1,0:T(8,128)} %copy-done.3, f32[4,6,3,4,24,128]{5,4,3,2,1,0:T(8,128)} %copy-done.4, ...), custom_call_target="tpu_custom_call" | custom-call | tf_op jit(solution)/shard_map/forward/pallas_call | solution.py:153
  350.2 25.8 %collective-permute-done.28.second = f32[4,6,3,4,24,128]{5,4,3,2,1,0:T(8,128)S(1)} collective-permute-done((f32[4,6,3,4,24,128]{5,4,3,2,1,0:T(8,128)}, f32[4,6,3,4,24,128]{5,4,3,2,1,0:T(8,128)S(1)}, u32[]{:S(2)}, u32[]{:S(2)}) %collective-permute-start.28) | collective-permute-done | bytes 3538976 | tf_op jit(solution)/shard_map/ppermute | solution.py:255
  377.8 11.2 %forward.6 = (f32[96,24,192]{2,1,0:T(8,128)}, f32[96,24,192]{2,1,0:T(8,128)}) custom-call(s32[1]{0:T(128)} %bitcast.2.scalars, f32[4,3,3,4,24,128]{5,4,3,2,1,0:T(8,128)} %pad_maximum_fusion.4.near, f32[4,3,3,4,24,128]{5,4,3,2,1,0:T(8,128)} %collective-permute-done.27.far, f32[4,6,3,4,24,128]{5,4,3,2,1,0:T(8,128)} %pad_maximum_fusion.1.first, ...), custom_call_target="tpu_custom_call" | custom-call | tf_op jit(solution)/shard_map/forward/pallas_call | solution.py:153
  389.1 11.3 %forward.7 = (f32[96,24,192]{2,1,0:T(8,128)}, f32[96,24,192]{2,1,0:T(8,128)}) custom-call(s32[1]{0:T(128)} %bitcast.2.scalars, f32[4,3,3,4,24,128]{5,4,3,2,1,0:T(8,128)} %copy-done.8, f32[4,3,3,4,24,128]{5,4,3,2,1,0:T(8,128)} %collective-permute-done.29.far, f32[4,6,3,4,24,128]{5,4,3,2,1,0:T(8,128)} %pad_maximum_fusion.1.first, ...), custom_call_target="tpu_custom_call" | custom-call | tf_op jit(solution)/shard_map/forward/pallas_call | solution.py:153
  405.3 34.4 %middle.1 = (f32[96,24,192]{2,1,0:T(8,128)}, f32[96,24,192]{2,1,0:T(8,128)}, f32[96,24,192]{2,1,0:T(8,128)}, f32[96,24,192]{2,1,0:T(8,128)}, f32[96,24,192]{2,1,...) custom-call(f32[96,192,192]{2,1,0:T(8,128)} %fusion.1.refs_0_, ...), custom_call_target="tpu_custom_call" | custom-call | tf_op jit(solution)/shard_map/middle/pallas_call | solution.py:187
  446.0 9.3 %inverse.7 = (f32[4,3,3,4,24,128]{5,4,3,2,1,0:T(8,128)}, f32[4,3,3,4,24,128]{5,4,3,2,1,0:T(8,128)}) custom-call(s32[1]{0:T(128)} %bitcast.2.scalars, f32[96,24,192]{2,1,0:T(8,128)} %get-tuple-element.190.keep_ref, f32[96,24,192]{2,1,0:T(8,128)} %copy-done.16, f32[4,6,3,4,24,128]{5,4,3,2,1,0:T(8,128)} %pad_maximum_fusion.1.first, ...), custom_call_target="tpu_custom_call" | custom-call | tf_op jit(solution)/shard_map/inverse/pallas_call | solution.py:225
  458.5 9.7 %inverse.6 = (f32[4,3,3,4,24,128]{5,4,3,2,1,0:T(8,128)}, f32[4,3,3,4,24,128]{5,4,3,2,1,0:T(8,128)}) custom-call(s32[1]{0:T(128)} %bitcast.2.scalars, f32[96,24,192]{2,1,0:T(8,128)} %get-tuple-element.186.keep_ref, f32[96,24,192]{2,1,0:T(8,128)} %copy-done.15, f32[4,6,3,4,24,128]{5,4,3,2,1,0:T(8,128)} %pad_maximum_fusion.1.first, ...), custom_call_target="tpu_custom_call" | custom-call | tf_op jit(solution)/shard_map/inverse/pallas_call | solution.py:225
  468.2 28.2 %collective-permute-done.38 = f32[4,3,3,4,24,128]{5,4,3,2,1,0:T(8,128)S(1)} collective-permute-done((f32[4,3,3,4,24,128]{5,4,3,2,1,0:T(8,128)}, f32[4,3,3,4,24,128]{5,4,3,2,1,0:T(8,128)S(1)}, u32[]{:S(2)}, u32[]{:S(2)}) %collective-permute-start.38) | collective-permute-done | bytes 1769504 | tf_op jit(solution)/shard_map/ppermute | solution.py:255
  507.7 9.3 %inverse.5 = (f32[4,3,3,4,24,128]{5,4,3,2,1,0:T(8,128)}, f32[4,3,3,4,24,128]{5,4,3,2,1,0:T(8,128)}) custom-call(s32[1]{0:T(128)} %bitcast.2.scalars, f32[96,24,192]{2,1,0:T(8,128)} %get-tuple-element.182.keep_ref, f32[96,24,192]{2,1,0:T(8,128)} %copy-done.14, f32[4,6,3,4,24,128]{5,4,3,2,1,0:T(8,128)} %copy-done.3, f32[4,6,3,4,24,128]{5,4,3,2,1,0:T(8,128)} %copy-done.4, ...), custom_call_target="tpu_custom_call" | custom-call | tf_op jit(solution)/shard_map/inverse/pallas_call | solution.py:225
  517.0 24.8 %collective-permute-done.41 = f32[3,3,4,24,128]{4,3,2,1,0:T(8,128)} collective-permute-done((f32[3,3,4,24,128]{4,3,2,1,0:T(8,128)S(1)}, f32[3,3,4,24,128]{4,3,2,1,0:T(8,128)}, u32[]{:S(2)}, u32[]{:S(2)}) %collective-permute-start.41) | collective-permute-done | bytes 442400 | tf_op jit(solution)/shard_map/ppermute | solution.py:255
  551.1 9.3 %inverse.4 = (f32[4,3,3,4,24,128]{5,4,3,2,1,0:T(8,128)}, f32[4,3,3,4,24,128]{5,4,3,2,1,0:T(8,128)}) custom-call(s32[1]{0:T(128)} %bitcast.2.scalars, f32[96,24,192]{2,1,0:T(8,128)} %get-tuple-element.175.keep_ref, f32[96,24,192]{2,1,0:T(8,128)} %copy-done.13, f32[4,6,3,4,24,128]{5,4,3,2,1,0:T(8,128)} %copy-done.3, f32[4,6,3,4,24,128]{5,4,3,2,1,0:T(8,128)} %copy-done.4, ...), custom_call_target="tpu_custom_call" | custom-call | tf_op jit(solution)/shard_map/inverse/pallas_call | solution.py:225
  561.4 8.7 %unpack.4.rest_0_ = f32[2,24,192,192]{3,2,1,0:T(8,128)} custom-call(s32[4]{0:T(128)} %get-tuple-element.284.scalars, f32[2,3,3,4,24,128]{5,4,3,2,1,0:T(8,128)} %get-tuple-element.252.keep_ref, f32[2,3,3,4,24,128]{5,4,3,2,1,0:T(8,128)} %copy-done.26), custom_call_target="tpu_custom_call" | custom-call | tf_op jit(solution)/shard_map/unpack/pallas_call | solution.py:101
  570.1 16.4 %collective-permute-done.45 = f32[3,3,4,24,128]{4,3,2,1,0:T(8,128)S(1)} collective-permute-done((f32[3,3,4,24,128]{4,3,2,1,0:T(8,128)}, f32[3,3,4,24,128]{4,3,2,1,0:T(8,128)S(1)}, u32[]{:S(2)}, u32[]{:S(2)}) %collective-permute-start.45) | collective-permute-done | bytes 442400 | tf_op jit(solution)/shard_map/ppermute | solution.py:255
  596.2 8.7 %unpack.5.rest_0_ = f32[2,24,192,192]{3,2,1,0:T(8,128)} custom-call(s32[4]{0:T(128)} %get-tuple-element.285.scalars, f32[2,3,3,4,24,128]{5,4,3,2,1,0:T(8,128)} %get-tuple-element.250.keep_ref, f32[2,3,3,4,24,128]{5,4,3,2,1,0:T(8,128)} %copy-done.30, f32[2,24,192,192]{3,2,1,0:T(8,128)} %unpack.4.rest_0_), custom_call_target="tpu_custom_call", output_to_operand_aliasing={{}: (3, {})} | custom-call | tf_op jit(solution)/shard_map/unpack/pallas_call | solution.py:101
  605.8 24.0 %collective-permute-done.50 = f32[3,3,4,24,128]{4,3,2,1,0:T(8,128)S(1)} collective-permute-done((f32[3,3,4,24,128]{4,3,2,1,0:T(8,128)S(1)}, f32[3,3,4,24,128]{4,3,2,1,0:T(8,128)S(1)}, u32[]{:S(2)}, u32[]{:S(2)}) %collective-permute-start.50) | collective-permute-done | bytes 442400 | tf_op jit(solution)/shard_map/ppermute | solution.py:255
  637.3 8.7 %unpack.6.rest_0_ = f32[2,24,192,192]{3,2,1,0:T(8,128)} custom-call(s32[4]{0:T(128)} %get-tuple-element.283.scalars, f32[2,3,3,4,24,128]{5,4,3,2,1,0:T(8,128)} %get-tuple-element.248.keep_ref, f32[2,3,3,4,24,128]{5,4,3,2,1,0:T(8,128)} %copy-done.31, f32[2,24,192,192]{3,2,1,0:T(8,128)} %unpack.5.rest_0_), custom_call_target="tpu_custom_call", output_to_operand_aliasing={{}: (3, {})} | custom-call | tf_op jit(solution)/shard_map/unpack/pallas_call | solution.py:101
  646.9 24.7 %collective-permute-done.54 = f32[3,3,4,24,128]{4,3,2,1,0:T(8,128)S(1)} collective-permute-done((f32[3,3,4,24,128]{4,3,2,1,0:T(8,128)S(1)}, f32[3,3,4,24,128]{4,3,2,1,0:T(8,128)S(1)}, u32[]{:S(2)}, u32[]{:S(2)}) %collective-permute-start.54) | collective-permute-done | bytes 442400 | tf_op jit(solution)/shard_map/ppermute | solution.py:255
  676.0 8.8 %unpack.7 = f32[2,24,192,192]{3,2,1,0:T(8,128)} custom-call(s32[4]{0:T(128)} %get-tuple-element.286.scalars, f32[2,3,3,4,24,128]{5,4,3,2,1,0:T(8,128)} %get-tuple-element.246.keep_ref, f32[2,3,3,4,24,128]{5,4,3,2,1,0:T(8,128)} %copy-done.32, f32[2,24,192,192]{3,2,1,0:T(8,128)} %unpack.6.rest_0_), custom_call_target="tpu_custom_call", output_to_operand_aliasing={{}: (3, {})} | custom-call | tf_op jit(solution)/shard_map/unpack/pallas_call | solution.py:101
  (259 shorter events, 175.9 us)
Async XLA Ops:
  7.2 37.6 %collective-permute-start.1 = (f32[2,3,3,4,24,128]{5,4,3,2,1,0:T(8,128)}, f32[2,3,3,4,24,128]{5,4,3,2,1,0:T(8,128)}, u32[]{:S(2)}, u32[]{:S(2)}) collective-permute-start(f32[2,3,3,4,24,128]{5,4,3,2,1,0:T(8,128)} %get-tuple-element.118), channel_id=1, source_target_pairs={{0,8},{8,0},{16,24},{24,16},{1,9},{9,1},{17,25},{25,17},{2,10},{10... | collective-permute-start | bytes 2654216 | tf_op jit(solution)/shard_map/ppermute | solution.py:255
  49.8 58.6 %collective-permute-start.7 = (f32[2,6,3,4,24,128]{5,4,3,2,1,0:T(8,128)}, f32[2,6,3,4,24,128]{5,4,3,2,1,0:T(8,128)}, u32[]{:S(2)}, u32[]{:S(2)}) collective-permute-start(f32[2,6,3,4,24,128]{5,4,3,2,1,0:T(8,128)} %get-tuple-element.124), channel_id=1, source_target_pairs={{0,8},{8,0},{16,24},{24,16},{1,9},{9,1},{17,25},{25,17},{2,10},{10... | collective-permute-start | bytes 5308424 | tf_op jit(solution)/shard_map/ppermute | solution.py:255
  71.3 36.7 %collective-permute-start.3 = (f32[6,3,4,24,128]{4,3,2,1,0:T(8,128)}, f32[6,3,4,24,128]{4,3,2,1,0:T(8,128)}, u32[]{:S(2)}, u32[]{:S(2)}) collective-permute-start(f32[6,3,4,24,128]{4,3,2,1,0:T(8,128)} %bitcast_select_fusion.2), channel_id=1, source_target_pairs={{0,16},{8,24},{16,0},{24,8},{1,17},{9,25},{17,1},{25,9},{2,18},{10... | collective-permute-start | bytes 2654216 | tf_op jit(solution)/shard_map/ppermute | solution.py:255
  112.6 62.9 %collective-permute-start.10 = (f32[9,3,4,24,128]{4,3,2,1,0:T(8,128)}, f32[9,3,4,24,128]{4,3,2,1,0:T(8,128)}, u32[]{:S(2)}, u32[]{:S(2)}) collective-permute-start(f32[9,3,4,24,128]{4,3,2,1,0:T(8,128)} %get-tuple-element.276), channel_id=1, source_target_pairs={{0,4},{1,5},{2,6},{3,7},{4,0},{5,1},{6,2},{7,3},{8,12},{9,13},{10,... | collective-permute-start | bytes 3981320 | tf_op jit(solution)/shard_map/ppermute | solution.py:255
  117.8 68.2 %collective-permute-start.9 = (f32[9,3,4,24,128]{4,3,2,1,0:T(8,128)}, f32[9,3,4,24,128]{4,3,2,1,0:T(8,128)S(1)}, u32[]{:S(2)}, u32[]{:S(2)}) collective-permute-start(f32[9,3,4,24,128]{4,3,2,1,0:T(8,128)} %get-tuple-element.275), channel_id=1, source_target_pairs={{0,2},{1,3},{2,0},{3,1},{4,6},{5,7},{6,4},{7,5},{8,10},{9,11},{10,... | collective-permute-start | bytes 3981320 | tf_op jit(solution)/shard_map/ppermute | solution.py:255
  125.2 60.8 %collective-permute-start.11 = (f32[3,3,4,24,128]{4,3,2,1,0:T(8,128)}, f32[3,3,4,24,128]{4,3,2,1,0:T(8,128)S(1)}, u32[]{:S(2)}, u32[]{:S(2)}) collective-permute-start(f32[3,3,4,24,128]{4,3,2,1,0:T(8,128)} %get-tuple-element.263), channel_id=1, source_target_pairs={{0,6},{1,7},{2,4},{3,5},{4,2},{5,3},{6,0},{7,1},{8,14},{9,15},{10,... | collective-permute-start | bytes 1327112 | tf_op jit(solution)/shard_map/ppermute | solution.py:255
  127.3 78.8 %collective-permute-start.16 = (f32[2,3,3,4,24,128]{5,4,3,2,1,0:T(8,128)}, f32[2,3,3,4,24,128]{5,4,3,2,1,0:T(8,128)S(1)}, u32[]{:S(2)}, u32[]{:S(2)}) collective-permute-start(f32[2,3,3,4,24,128]{5,4,3,2,1,0:T(8,128)} %get-tuple-element.147), channel_id=1, source_target_pairs={{0,8},{8,0},{16,24},{24,16},{1,9},{9,1},{17,25},{25,17},{2,10},{10... | collective-permute-start | bytes 2654216 | tf_op jit(solution)/shard_map/ppermute | solution.py:255
  137.0 69.1 %collective-permute-start.13 = (f32[4,3,3,4,24,128]{5,4,3,2,1,0:T(8,128)S(1)}, f32[4,3,3,4,24,128]{5,4,3,2,1,0:T(8,128)S(1)}, u32[]{:S(2)}, u32[]{:S(2)}) collective-permute-start(f32[4,3,3,4,24,128]{5,4,3,2,1,0:T(8,128)S(1)} %pad_maximum_fusion.2.near), channel_id=1, source_target_pairs={{0,1},{1,0},{2,3},{3,2},{4,5},{5,4},{6,7},{7,6},{8,9},{9,8},{10,11... | collective-permute-start | bytes 5308424 | tf_op jit(solution)/shard_map/ppermute | solution.py:255
  207.4 89.7 %collective-permute-start.22 = (f32[4,6,3,4,24,128]{5,4,3,2,1,0:T(8,128)S(1)}, f32[4,6,3,4,24,128]{5,4,3,2,1,0:T(8,128)S(1)}, u32[]{:S(2)}, u32[]{:S(2)}) collective-permute-start(f32[4,6,3,4,24,128]{5,4,3,2,1,0:T(8,128)S(1)} %pad_maximum_fusion.first), channel_id=1, source_target_pairs={{0,16},{8,24},{16,0},{24,8},{1,17},{9,25},{17,1},{25,9},{2,18},{10... | collective-permute-start | bytes 10616840 | tf_op jit(solution)/shard_map/ppermute | solution.py:255
  208.6 61.2 %collective-permute-start.18 = (f32[9,3,4,24,128]{4,3,2,1,0:T(8,128)S(1)}, f32[9,3,4,24,128]{4,3,2,1,0:T(8,128)S(1)}, u32[]{:S(2)}, u32[]{:S(2)}) collective-permute-start(f32[9,3,4,24,128]{4,3,2,1,0:T(8,128)S(1)} %get-tuple-element.274), channel_id=1, source_target_pairs={{0,4},{1,5},{2,6},{3,7},{4,0},{5,1},{6,2},{7,3},{8,12},{9,13},{10,... | collective-permute-start | bytes 3981320 | tf_op jit(solution)/shard_map/ppermute | solution.py:255
  208.7 61.4 %collective-permute-start.17 = (f32[9,3,4,24,128]{4,3,2,1,0:T(8,128)S(1)}, f32[9,3,4,24,128]{4,3,2,1,0:T(8,128)S(1)}, u32[]{:S(2)}, u32[]{:S(2)}) collective-permute-start(f32[9,3,4,24,128]{4,3,2,1,0:T(8,128)S(1)} %get-tuple-element.273), channel_id=1, source_target_pairs={{0,2},{1,3},{2,0},{3,1},{4,6},{5,7},{6,4},{7,5},{8,10},{9,11},{10,... | collective-permute-start | bytes 3981320 | tf_op jit(solution)/shard_map/ppermute | solution.py:255
  209.5 87.6 %collective-permute-start.21 = (f32[4,3,3,4,24,128]{5,4,3,2,1,0:T(8,128)S(1)}, f32[4,3,3,4,24,128]{5,4,3,2,1,0:T(8,128)S(1)}, u32[]{:S(2)}, u32[]{:S(2)}) collective-permute-start(f32[4,3,3,4,24,128]{5,4,3,2,1,0:T(8,128)S(1)} %pad_maximum_fusion.3.near), channel_id=1, source_target_pairs={{0,1},{1,0},{2,3},{3,2},{4,5},{5,4},{6,7},{7,6},{8,9},{9,8},{10,11... | collective-permute-start | bytes 5308424 | tf_op jit(solution)/shard_map/ppermute | solution.py:255
  209.9 66.2 %collective-permute-start.19 = (f32[3,3,4,24,128]{4,3,2,1,0:T(8,128)S(1)}, f32[3,3,4,24,128]{4,3,2,1,0:T(8,128)S(1)}, u32[]{:S(2)}, u32[]{:S(2)}) collective-permute-start(f32[3,3,4,24,128]{4,3,2,1,0:T(8,128)S(1)} %get-tuple-element.259), channel_id=1, source_target_pairs={{0,6},{1,7},{2,4},{3,5},{4,2},{5,3},{6,0},{7,1},{8,14},{9,15},{10,... | collective-permute-start | bytes 1327112 | tf_op jit(solution)/shard_map/ppermute | solution.py:255
  297.1 41.0 %collective-permute-start.27 = (f32[4,3,3,4,24,128]{5,4,3,2,1,0:T(8,128)}, f32[4,3,3,4,24,128]{5,4,3,2,1,0:T(8,128)}, u32[]{:S(2)}, u32[]{:S(2)}) collective-permute-start(f32[4,3,3,4,24,128]{5,4,3,2,1,0:T(8,128)} %pad_maximum_fusion.4.near), channel_id=1, source_target_pairs={{0,1},{1,0},{2,3},{3,2},{4,5},{5,4},{6,7},{7,6},{8,9},{9,8},{10,11... | collective-permute-start | bytes 5308424 | tf_op jit(solution)/shard_map/ppermute | solution.py:255
  297.2 78.8 %collective-permute-start.28 = (f32[4,6,3,4,24,128]{5,4,3,2,1,0:T(8,128)}, f32[4,6,3,4,24,128]{5,4,3,2,1,0:T(8,128)S(1)}, u32[]{:S(2)}, u32[]{:S(2)}) collective-permute-start(f32[4,6,3,4,24,128]{5,4,3,2,1,0:T(8,128)} %pad_maximum_fusion.1.first), channel_id=1, source_target_pairs={{0,16},{8,24},{16,0},{24,8},{1,17},{9,25},{17,1},{25,9},{2,18},{10... | collective-permute-start | bytes 10616840 | tf_op jit(solution)/shard_map/ppermute | solution.py:255
  338.1 51.0 %collective-permute-start.29 = (f32[4,3,3,4,24,128]{5,4,3,2,1,0:T(8,128)S(1)}, f32[4,3,3,4,24,128]{5,4,3,2,1,0:T(8,128)}, u32[]{:S(2)}, u32[]{:S(2)}) collective-permute-start(f32[4,3,3,4,24,128]{5,4,3,2,1,0:T(8,128)S(1)} %pad_maximum_fusion.5.near), channel_id=1, source_target_pairs={{0,1},{1,0},{2,3},{3,2},{4,5},{5,4},{6,7},{7,6},{8,9},{9,8},{10,11... | collective-permute-start | bytes 5308424 | tf_op jit(solution)/shard_map/ppermute | solution.py:255
  349.6 51.2 %collective-permute-start.31 = (f32[96,24,192]{2,1,0:T(8,128)}, f32[96,24,192]{2,1,0:T(8,128)S(1)}, u32[]{:S(2)}, u32[]{:S(2)}) collective-permute-start(f32[96,24,192]{2,1,0:T(8,128)} %get-tuple-element.172), channel_id=1, source_target_pairs={{0,8},{8,0},{16,24},{24,16},{1,9},{9,1},{17,25},{25,17},{2,10},{10... | collective-permute-start | bytes 5308424 | tf_op jit(solution)/shard_map/ppermute | solution.py:255
  349.7 51.1 %collective-permute-start.30 = (f32[96,24,192]{2,1,0:T(8,128)}, f32[96,24,192]{2,1,0:T(8,128)}, u32[]{:S(2)}, u32[]{:S(2)}) collective-permute-start(f32[96,24,192]{2,1,0:T(8,128)} %get-tuple-element.171), channel_id=1, source_target_pairs={{0,8},{8,0},{16,24},{24,16},{1,9},{9,1},{17,25},{25,17},{2,10},{10... | collective-permute-start | bytes 5308424 | tf_op jit(solution)/shard_map/ppermute | solution.py:255
  455.3 41.1 %collective-permute-start.38 = (f32[4,3,3,4,24,128]{5,4,3,2,1,0:T(8,128)}, f32[4,3,3,4,24,128]{5,4,3,2,1,0:T(8,128)S(1)}, u32[]{:S(2)}, u32[]{:S(2)}) collective-permute-start(f32[4,3,3,4,24,128]{5,4,3,2,1,0:T(8,128)} %get-tuple-element.193), channel_id=1, source_target_pairs={{0,1},{1,0},{2,3},{3,2},{4,5},{5,4},{6,7},{7,6},{8,9},{9,8},{10,11... | collective-permute-start | bytes 5308424 | tf_op jit(solution)/shard_map/ppermute | solution.py:255
  457.0 49.3 %collective-permute-start.35 = (f32[96,24,192]{2,1,0:T(8,128)}, f32[96,24,192]{2,1,0:T(8,128)S(1)}, u32[]{:S(2)}, u32[]{:S(2)}) collective-permute-start(f32[96,24,192]{2,1,0:T(8,128)} %get-tuple-element.183), channel_id=1, source_target_pairs={{0,8},{8,0},{16,24},{24,16},{1,9},{9,1},{17,25},{25,17},{2,10},{10... | collective-permute-start | bytes 5308424 | tf_op jit(solution)/shard_map/ppermute | solution.py:255
  497.7 44.2 %collective-permute-start.39 = (f32[4,3,3,4,24,128]{5,4,3,2,1,0:T(8,128)}, f32[4,3,3,4,24,128]{5,4,3,2,1,0:T(8,128)S(1)}, u32[]{:S(2)}, u32[]{:S(2)}) collective-permute-start(f32[4,3,3,4,24,128]{5,4,3,2,1,0:T(8,128)} %get-tuple-element.195), channel_id=1, source_target_pairs={{0,1},{1,0},{2,3},{3,2},{4,5},{5,4},{6,7},{7,6},{8,9},{9,8},{10,11... | collective-permute-start | bytes 5308424 | tf_op jit(solution)/shard_map/ppermute | solution.py:255
  504.6 37.2 %collective-permute-start.41 = (f32[3,3,4,24,128]{4,3,2,1,0:T(8,128)S(1)}, f32[3,3,4,24,128]{4,3,2,1,0:T(8,128)}, u32[]{:S(2)}, u32[]{:S(2)}) collective-permute-start(f32[3,3,4,24,128]{4,3,2,1,0:T(8,128)S(1)} %get-tuple-element.242), channel_id=1, source_target_pairs={{0,4},{1,5},{2,6},{3,7},{4,0},{5,1},{6,2},{7,3},{8,12},{9,13},{10,... | collective-permute-start | bytes 1327112 | tf_op jit(solution)/shard_map/ppermute | solution.py:255
  504.6 37.2 %collective-permute-start.40 = (f32[3,3,4,24,128]{4,3,2,1,0:T(8,128)S(1)}, f32[3,3,4,24,128]{4,3,2,1,0:T(8,128)}, u32[]{:S(2)}, u32[]{:S(2)}) collective-permute-start(f32[3,3,4,24,128]{4,3,2,1,0:T(8,128)S(1)} %get-tuple-element.243), channel_id=1, source_target_pairs={{0,2},{1,3},{2,0},{3,1},{4,6},{5,7},{6,4},{7,5},{8,10},{9,11},{10,... | collective-permute-start | bytes 1327112 | tf_op jit(solution)/shard_map/ppermute | solution.py:255
  506.3 42.5 %collective-permute-start.34 = (f32[96,24,192]{2,1,0:T(8,128)}, f32[96,24,192]{2,1,0:T(8,128)S(1)}, u32[]{:S(2)}, u32[]{:S(2)}) collective-permute-start(f32[96,24,192]{2,1,0:T(8,128)} %get-tuple-element.176), channel_id=1, source_target_pairs={{0,8},{8,0},{16,24},{24,16},{1,9},{9,1},{17,25},{25,17},{2,10},{10... | collective-permute-start | bytes 5308424 | tf_op jit(solution)/shard_map/ppermute | solution.py:255
  541.8 44.6 %collective-permute-start.43 = (f32[4,3,3,4,24,128]{5,4,3,2,1,0:T(8,128)}, f32[4,3,3,4,24,128]{5,4,3,2,1,0:T(8,128)S(1)}, u32[]{:S(2)}, u32[]{:S(2)}) collective-permute-start(f32[4,3,3,4,24,128]{5,4,3,2,1,0:T(8,128)} %get-tuple-element.199), channel_id=1, source_target_pairs={{0,1},{1,0},{2,3},{3,2},{4,5},{5,4},{6,7},{7,6},{8,9},{9,8},{10,11... | collective-permute-start | bytes 5308424 | tf_op jit(solution)/shard_map/ppermute | solution.py:255
  548.7 37.7 %collective-permute-start.45 = (f32[3,3,4,24,128]{4,3,2,1,0:T(8,128)}, f32[3,3,4,24,128]{4,3,2,1,0:T(8,128)S(1)}, u32[]{:S(2)}, u32[]{:S(2)}) collective-permute-start(f32[3,3,4,24,128]{4,3,2,1,0:T(8,128)} %get-tuple-element.238), channel_id=1, source_target_pairs={{0,4},{1,5},{2,6},{3,7},{4,0},{5,1},{6,2},{7,3},{8,12},{9,13},{10,... | collective-permute-start | bytes 1327112 | tf_op jit(solution)/shard_map/ppermute | solution.py:255
  548.7 37.7 %collective-permute-start.44 = (f32[3,3,4,24,128]{4,3,2,1,0:T(8,128)}, f32[3,3,4,24,128]{4,3,2,1,0:T(8,128)S(1)}, u32[]{:S(2)}, u32[]{:S(2)}) collective-permute-start(f32[3,3,4,24,128]{4,3,2,1,0:T(8,128)} %get-tuple-element.239), channel_id=1, source_target_pairs={{0,2},{1,3},{2,0},{3,1},{4,6},{5,7},{6,4},{7,5},{8,10},{9,11},{10,... | collective-permute-start | bytes 1327112 | tf_op jit(solution)/shard_map/ppermute | solution.py:255
  586.5 43.3 %collective-permute-start.48 = (f32[4,3,3,4,24,128]{5,4,3,2,1,0:T(8,128)}, f32[4,3,3,4,24,128]{5,4,3,2,1,0:T(8,128)S(1)}, u32[]{:S(2)}, u32[]{:S(2)}) collective-permute-start(f32[4,3,3,4,24,128]{5,4,3,2,1,0:T(8,128)} %get-tuple-element.207), channel_id=1, source_target_pairs={{0,1},{1,0},{2,3},{3,2},{4,5},{5,4},{6,7},{7,6},{8,9},{9,8},{10,11... | collective-permute-start | bytes 5308424 | tf_op jit(solution)/shard_map/ppermute | solution.py:255
  592.0 37.7 %collective-permute-start.50 = (f32[3,3,4,24,128]{4,3,2,1,0:T(8,128)S(1)}, f32[3,3,4,24,128]{4,3,2,1,0:T(8,128)S(1)}, u32[]{:S(2)}, u32[]{:S(2)}) collective-permute-start(f32[3,3,4,24,128]{4,3,2,1,0:T(8,128)S(1)} %get-tuple-element.234), channel_id=1, source_target_pairs={{0,4},{1,5},{2,6},{3,7},{4,0},{5,1},{6,2},{7,3},{8,12},{9,13},{10,... | collective-permute-start | bytes 1327112 | tf_op jit(solution)/shard_map/ppermute | solution.py:255
  592.0 37.7 %collective-permute-start.49 = (f32[3,3,4,24,128]{4,3,2,1,0:T(8,128)S(1)}, f32[3,3,4,24,128]{4,3,2,1,0:T(8,128)S(1)}, u32[]{:S(2)}, u32[]{:S(2)}) collective-permute-start(f32[3,3,4,24,128]{4,3,2,1,0:T(8,128)S(1)} %get-tuple-element.235), channel_id=1, source_target_pairs={{0,2},{1,3},{2,0},{3,1},{4,6},{5,7},{6,4},{7,5},{8,10},{9,11},{10,... | collective-permute-start | bytes 1327112 | tf_op jit(solution)/shard_map/ppermute | solution.py:255
  634.6 37.0 %collective-permute-start.54 = (f32[3,3,4,24,128]{4,3,2,1,0:T(8,128)S(1)}, f32[3,3,4,24,128]{4,3,2,1,0:T(8,128)S(1)}, u32[]{:S(2)}, u32[]{:S(2)}) collective-permute-start(f32[3,3,4,24,128]{4,3,2,1,0:T(8,128)S(1)} %get-tuple-element.230), channel_id=1, source_target_pairs={{0,4},{1,5},{2,6},{3,7},{4,0},{5,1},{6,2},{7,3},{8,12},{9,13},{10,... | collective-permute-start | bytes 1327112 | tf_op jit(solution)/shard_map/ppermute | solution.py:255
  634.6 37.0 %collective-permute-start.53 = (f32[3,3,4,24,128]{4,3,2,1,0:T(8,128)S(1)}, f32[3,3,4,24,128]{4,3,2,1,0:T(8,128)S(1)}, u32[]{:S(2)}, u32[]{:S(2)}) collective-permute-start(f32[3,3,4,24,128]{4,3,2,1,0:T(8,128)S(1)} %get-tuple-element.231), channel_id=1, source_target_pairs={{0,2},{1,3},{2,0},{3,1},{4,6},{5,7},{6,4},{7,5},{8,10},{9,11},{10,... | collective-permute-start | bytes 1327112 | tf_op jit(solution)/shard_map/ppermute | solution.py:255
  (68 other events, 855.8 us)

commit v2 on v1

v2 whole, which is shorter than its diff:
```python
import math

import jax
import jax.numpy as jnp
from jax import lax
from jax.experimental import pallas as pl
from jax.experimental.pallas import tpu as pltpu
from jax.sharding import PartitionSpec as P

grid_step = 0.25
omega = 0.106
CORES = 2
LANES = 128
STEP = 4
SPLIT = (4, 2, 2, 2, 2)
PARTS = ((0,), (1, 2), (3, 4))
BACK = 2
VMEM_LIMIT = 56 * 1024 * 1024


def wave_squared(modes, length):
    signed = jnp.where(modes <= length // 2, modes, modes - length)
    wave = 2.0 * math.pi / (length * grid_step) * signed.astype(jnp.float32)
    return wave * wave


def screened(squares):
    nonzero = jnp.where(squares > 0, squares, jnp.ones_like(squares))
    value = 4.0 * math.pi * (1.0 - jnp.exp(-squares / (4.0 * omega * omega))) / nonzero
    return jnp.where(squares > 0, value, jnp.full_like(squares, math.pi / (omega * omega)))


def cas_matrix(rows, columns, length):
    product = rows[:, None] * columns[None, :] % length
    phases = 2.0 * math.pi / length * product.astype(jnp.float32)
    return jnp.cos(phases) + jnp.sin(phases)


def halves(values):
    high = values.astype(jnp.bfloat16)
    low = (values - high.astype(jnp.float32)).astype(jnp.bfloat16)
    return high, low


def multiply(left, right):
    def dot(a, b):
        return jnp.dot(a, b, preferred_element_type=jnp.float32)

    return dot(left[0], right[0]) + (dot(left[0], right[1]) + dot(left[1], right[0]))


def multiply_deep(left, right):
    wide = jnp.concatenate([left[0], left[0], left[1]], axis=1)
    deep = jnp.concatenate([right[0], right[1], right[0]], axis=0)
    return jnp.dot(wide, deep, preferred_element_type=jnp.float32)


def pack_body(scalars, keep_ref, give_ref, keep_out, give_out):
    for source, out in ((keep_ref, keep_out), (give_ref, give_out)):
        rows = jnp.swapaxes(source[0], 0, 1)
        rows = rows.reshape((out.shape[1], 2, STEP) + rows.shape[1:])
        out[0, :, 0] = rows[:, 0, :, :, :LANES]
        out[0, :, 1] = rows[:, 1, :, :, :LANES]
        out[0, :, 2] = jnp.concatenate([rows[:, 0, :, :, LANES:], rows[:, 1, :, :, LANES:]], axis=-1)


def pack(stored, scalars, units, parts=1):
    count = scalars.shape[0] - 2
    planes, points = stored.shape[1], stored.shape[3]
    block = (1, units, 3, STEP, planes, LANES)
    rows = (1, planes, 2 * STEP * units, points)
    shape = jax.ShapeDtypeStruct((count, units * parts) + block[2:], jnp.float32)
    spec = pl.BlockSpec(block, lambda i, k, s: (i, k, 0, 0, 0, 0))
    return pl.pallas_call(
        pack_body,
        grid_spec=pltpu.PrefetchScalarGridSpec(
            num_scalar_prefetch=1,
            grid=(count, parts),
            in_specs=[
                pl.BlockSpec(rows, lambda i, k, s: (s[i], 0, s[count] + k, 0)),
                pl.BlockSpec(rows, lambda i, k, s: (s[i], 0, s[count + 1] + k, 0)),
            ],
            out_specs=[spec, spec],
        ),
        out_shape=[shape, shape],
        compiler_params=pltpu.CompilerParams(vmem_limit_bytes=VMEM_LIMIT),
        name="pack",
    )(scalars, stored, stored)


def unpack_body(scalars, keep_ref, got_ref, *rest):
    out = rest[-1]

    def place(source):
        tails = source[0, :, 2]
        lower = jnp.concatenate([source[0, :, 0], tails[..., : LANES // 2]], axis=-1)
        upper = jnp.concatenate([source[0, :, 1], tails[..., LANES // 2 :]], axis=-1)
        rows = jnp.stack([lower, upper], axis=1)
        out[0] = jnp.swapaxes(rows.reshape((-1,) + rows.shape[3:]), 0, 1)

    pl.when(pl.program_id(1) == 0)(lambda: place(keep_ref))
    pl.when(pl.program_id(1) == 1)(lambda: place(got_ref))


def unpack(keep, got, scalars, shape, earlier):
    count, units = keep.shape[:2]
    planes, points = shape[1], shape[3]
    spec = pl.BlockSpec((1,) + keep.shape[1:], lambda i, k, s: (i, 0, 0, 0, 0, 0))
    held = [] if earlier is None else [earlier]
    return pl.pallas_call(
        unpack_body,
        grid_spec=pltpu.PrefetchScalarGridSpec(
            num_scalar_prefetch=1,
            grid=(count, 2),
            in_specs=[spec, spec] + [pl.BlockSpec(memory_space=pl.ANY) for _ in held],
            out_specs=pl.BlockSpec(
                (1, planes, 2 * STEP * units, points), lambda i, k, s: (s[i], 0, s[count + k], 0)
            ),
        ),
        out_shape=jax.ShapeDtypeStruct(shape, jnp.float32),
        input_output_aliases={3: 0} if held else {},
        compiler_params=pltpu.CompilerParams(vmem_limit_bytes=VMEM_LIMIT),
        name="unpack",
    )(scalars, keep, got, *held)


def orbital_parts(same, first, second):
    pieces = range(first.shape[0])
    near = [jnp.where(same, first[d, 0], second[d, 0]) for d in pieces]
    far = [jnp.where(same, second[d, 0], first[d, 0]) for d in pieces]
    return near + far


def forward_body(scalars, near, far, first, second, lower_ref, upper_ref, planes_ref, keep_out, give_out):
    orbitals = orbital_parts(scalars[0] == 1, first, second)
    targets = [part[d, 0] for part in (near, far) for d in range(part.shape[0])]
    density = jnp.concatenate([t * o for t, o in zip(targets, orbitals)], axis=2)
    step, points = density.shape[1], density.shape[2]
    matrix = halves(planes_ref[...])
    results = []
    for part, weights in ((0, lower_ref), (1, upper_ref)):
        packed = jnp.concatenate([density[part], density[2]], axis=-1).reshape(step * points, 2 * LANES)
        lines = multiply_deep(halves(packed), halves(weights[...]))
        high, low = halves(lines)
        for row in range(step):
            where = slice(row * points, (row + 1) * points)
            results.append(multiply_deep(matrix, (high[where], low[where])))
    spectrum = jnp.swapaxes(jnp.stack(results), 0, 1)
    keep_out[...] = spectrum[: points // 2]
    give_out[...] = spectrum[points // 2 :]


def stacked(array, offset, layers):
    return pl.BlockSpec((layers, 1) + array.shape[2:], lambda u, s: (0, u + offset, 0, 0, 0, 0))


def forward(near, far, first, at, second, there, scalars, lower, upper, planes_matrix):
    units, points = near.shape[1], planes_matrix.shape[0]
    whole = lambda a: pl.BlockSpec(a.shape, lambda u, s: (0, 0))
    out = pl.BlockSpec((points // 2, 2 * STEP, points), lambda u, s: (0, u, 0))
    shape = jax.ShapeDtypeStruct((points // 2, 2 * STEP * units, points), jnp.float32)
    return pl.pallas_call(
        forward_body,
        grid_spec=pltpu.PrefetchScalarGridSpec(
            num_scalar_prefetch=1,
            grid=(units,),
            in_specs=[stacked(a, at, near.shape[0]) for a, at in ((near, 0), (far, 0), (first, at), (second, there))]
            + [whole(lower), whole(upper), whole(planes_matrix)],
            out_specs=[out, out],
        ),
        out_shape=[shape, shape],
        compiler_params=pltpu.CompilerParams(vmem_limit_bytes=VMEM_LIMIT),
        name="forward",
    )(scalars, near, far, first, second, lower, upper, planes_matrix)


def middle_body(count, kernel_ref, forth_ref, back_ref, *refs):
    ins, outs = refs[:count], refs[count:]
    forth, back = halves(forth_ref[...]), halves(back_ref[...])
    for k in range(kernel_ref.shape[0]):
        rows = jnp.concatenate([r[k] for r in ins], axis=0)
        spectrum = multiply(forth, halves(rows)) * kernel_ref[k]
        filtered = multiply(back, halves(spectrum))
        start = 0
        for out in outs:
            out[k] = filtered[start : start + out.shape[1]]
            start += out.shape[1]


def middle(spectra, kernel, forth, back):
    count = len(spectra)
    deep, _, points = spectra[0].shape
    block = 16
    parts = [pl.BlockSpec((block,) + a.shape[1:], lambda k: (k, 0, 0)) for a in spectra]
    whole = pl.BlockSpec((points, points), lambda k: (0, 0))
    return pl.pallas_call(
        lambda *refs: middle_body(count, *refs),
        grid=(deep // block,),
        in_specs=[pl.BlockSpec((block, points, points), lambda k: (k, 0, 0)), whole, whole] + parts,
        out_specs=parts,
        out_shape=[jax.ShapeDtypeStruct(a.shape, jnp.float32) for a in spectra],
        compiler_params=pltpu.CompilerParams(vmem_limit_bytes=VMEM_LIMIT),
        name="middle",
    )(kernel, forth, back, *spectra)


def inverse_body(scalars, keep_ref, got_ref, first, second, lower_ref, upper_ref, planes_ref, near, far):
    spectrum = jnp.swapaxes(jnp.concatenate([keep_ref[...], got_ref[...]], axis=0), 0, 1)
    points = spectrum.shape[1]
    step = spectrum.shape[0] // 2
    matrix = halves(planes_ref[...])
    packed = []
    for part, weights in ((0, lower_ref), (1, upper_ref)):
        lines = jnp.concatenate(
            [multiply(matrix, halves(spectrum[part * step + row])) for row in range(step)], axis=0
        )
        packed.append(multiply(halves(lines), halves(weights[...])).reshape(step, points, 2 * LANES))
    low, high = packed
    field = [low[:, :, :LANES], high[:, :, :LANES], low[:, :, LANES:] + high[:, :, LANES:]]
    orbitals = orbital_parts(scalars[0] == 1, first, second)
    outs = [(part, d) for part in (near, far) for d in range(part.shape[0])]
    planes = points // len(outs)
    for i, (orbital, (out, d)) in enumerate(zip(orbitals, outs)):
        for part in range(3):
            out[d, 0, part] = -field[part][:, i * planes : (i + 1) * planes] * orbital[part]


def inverse(keep, got, skip, units, first, at, second, there, scalars, lower, upper, planes_matrix):
    deep, _, points = keep.shape
    whole = lambda a: pl.BlockSpec(a.shape, lambda u, s: (0, 0))
    part = pl.BlockSpec((deep, 2 * STEP, points), lambda u, s: (0, u + skip, 0))
    layers = first.shape[0]
    shape = jax.ShapeDtypeStruct((layers, units) + first.shape[2:], jnp.float32)
    return pl.pallas_call(
        inverse_body,
        grid_spec=pltpu.PrefetchScalarGridSpec(
            num_scalar_prefetch=1,
            grid=(units,),
            in_specs=[part, part, stacked(first, at, layers), stacked(second, there, layers)]
            + [whole(lower), whole(upper), whole(planes_matrix)],
            out_specs=[stacked(shape, 0, layers)] * 2,
        ),
        out_shape=[shape] * 2,
        compiler_params=pltpu.CompilerParams(vmem_limit_bytes=VMEM_LIMIT),
        name="inverse",
    )(scalars, keep, got, first, second, lower, upper, planes_matrix)


def by_layers(bands, occupied, occ_index, band_pick, groups, slabs):
    picks, window = band_pick.shape[0], occ_index.shape[0]
    per_group, planes, points = occupied.shape[0], bands.shape[1], bands.shape[2]
    sides = window
    layers = slabs // sides
    half_rows = points // CORES
    units = half_rows // (2 * STEP)
    chunks = len(SPLIT)
    starts = [sum(SPLIT[:j]) for j in range(chunks)]

    band, slab = lax.axis_index("band"), lax.axis_index("slab")
    y, c = band // CORES, band % CORES
    z, x = slab // sides, slab % sides

    def swap(values, axis, size, flip):
        return lax.ppermute(values, axis, [(i, flip(i)) for i in range(size)])

    def over_core(values):
        return swap(values, "band", groups, lambda i: i ^ 1)

    def over_y(values):
        return swap(values, "band", groups, lambda i: i ^ CORES)

    def over_x(values):
        return swap(values, "slab", slabs, lambda i: i ^ 1)

    def over_z(values, d):
        return swap(values, "slab", slabs, lambda i: i ^ (d * sides))

    layer_of = z ^ jnp.arange(layers, dtype=jnp.int32)
    side_of = x ^ jnp.arange(sides, dtype=jnp.int32)
    slab_of = (side_of[:, None] + sides * layer_of[None, :]).reshape(-1)
    plane_of = (slab_of[:, None] * planes + jnp.arange(planes, dtype=jnp.int32)).reshape(-1)
    core_of = c ^ jnp.arange(CORES, dtype=jnp.int32)
    all_modes = jnp.arange(points, dtype=jnp.int32)
    mode_of = (core_of[:, None] * half_rows + jnp.arange(half_rows, dtype=jnp.int32)).reshape(-1)

    squares = wave_squared(all_modes, points)
    own_squares = wave_squared(c * half_rows + jnp.arange(half_rows, dtype=jnp.int32), points)

    first_bit = z % picks
    target_index = band_pick[jnp.arange(picks, dtype=jnp.int32) ^ first_bit]
    which = occ_index[side_of]
    owner = which // per_group
    owner_y, owner_core = owner // CORES, owner % CORES
    here = z // picks == c
    same = x == y
    flag = same.astype(jnp.int32)[None]

    def row_blocks(start, size):
        return jnp.stack([c * (units // size) + start // size, (1 - c) * (units // size) + start // size])

    def sync(*values):
        return lax.optimization_barrier(values)

    def after(value, *others):
        return lax.optimization_barrier((value,) + others)[0]

    def pack_orbital(h, parts, *earlier):
        start, size = starts[PARTS[h][0]], sum(SPLIT[j] for j in PARTS[h])
        scalars = jnp.concatenate([which % per_group, row_blocks(start, size)])
        return pack(occupied, after(scalars, *earlier), size, parts)

    def pack_target(j, parts, *earlier):
        scalars = jnp.concatenate([target_index, row_blocks(starts[j], SPLIT[j])])
        return pack(bands, after(scalars, *earlier), SPLIT[j], parts)


    def choose_orbital(keep, got):
        mine = jnp.where(owner_core[0] == c, keep[0], got[0])
        theirs = jnp.where(owner_core[1] == c, keep[1], got[1])
        return mine, theirs

    def choose_side(mine, other):
        return jnp.where(same, mine, other), jnp.where(same, other, mine)

    def choose_group(stay, got):
        return jnp.where(owner_y[0] == y, stay, got)

    def choose_targets(j, keep, got, carried=None):
        pieces = []
        begin = starts[j] - (starts[1] if j else 0)
        for d in range(layers):
            a, b = (keep, got) if d < picks else (got, keep)
            piece = jnp.where(here, a[d % picks], b[d % picks])[begin : begin + SPLIT[j]]
            if carried is not None and d and not d & (d - 1):
                piece = jnp.concatenate([piece, carried], axis=0)
            pieces.append(piece)
        return pieces

    def along_layers(pieces, carried=None):
        got, reached, size = [], [carried], pieces[0].shape[0]
        for d, piece in enumerate(pieces):
            moved = over_z(piece, d) if d else piece
            got.append(moved[:size])
            if carried is not None and d:
                reach = d & -d
                reached.append(over_z(reached[d - reach], reach) if d & (d - 1) else moved[size:])
        return got, reached

    size = SPLIT[0]
    keep, give = pack_target(0, 1)
    got = over_core(give)
    ready = choose_targets(0, keep, got)
    ready = sync(ready)[0]
    near0, _ = along_layers(ready)
    keep, give = pack_orbital(0, 1, ready)
    got = over_core(give)
    mine, theirs = choose_orbital(keep, got)
    other = over_x(theirs)
    stay, send = choose_side(mine, other)
    carried0 = choose_group(stay, over_y(send))
    keep, give = pack_orbital(1, 2, keep)
    mine, theirs = choose_orbital(keep, over_core(give))
    stay, send = choose_side(mine, over_x(theirs))
    keep, give = pack_target(1, chunks - 1, keep)
    got = over_core(give)
    ready = choose_targets(1, keep, got, carried0)
    ready, carried0, near0, stay, send, keep, got = sync(ready, carried0, near0, stay, send, keep, got)
    near1, first0 = along_layers(ready, carried0)
    near0 = jnp.stack(near0)
    far0 = over_x(near0)
    carried = choose_group(stay, over_y(send))
    carried1, carried2 = carried[:size], carried[size:]
    ready = choose_targets(2, keep, got, carried1)
    ready, carried1, carried2, near1, first0, far0 = sync(ready, carried1, carried2, near1, first0, far0)
    near2, first1 = along_layers(ready, carried1)
    first0, near1 = jnp.stack(first0), jnp.stack(near1)
    second0 = over_y(first0)
    far1 = over_x(near1)
    ready = choose_targets(3, keep, got, carried2)
    own_squares, squares, all_modes, mode_of, plane_of = after(
        (own_squares, squares, all_modes, mode_of, plane_of), near2[1]
    )
    kernel = screened(own_squares[:, None, None] + squares[None, :, None] + squares[None, None, :])
    kernel = kernel / float(points * points * points)
    columns = cas_matrix(all_modes, all_modes, points)
    empty = jnp.zeros((points - LANES, points), jnp.float32)
    lower = jnp.concatenate([columns, empty], axis=0)
    upper = jnp.concatenate([columns[:LANES], empty, columns[LANES:]], axis=0)
    lower_back = jnp.concatenate([columns, empty.T], axis=1)
    upper_back = jnp.concatenate([columns[:, :LANES], empty.T, columns[:, LANES:]], axis=1)
    to_modes = cas_matrix(mode_of, plane_of, points)
    to_planes = cas_matrix(plane_of, mode_of, points)
    forth = cas_matrix(all_modes, mode_of, points)
    back = cas_matrix(mode_of, all_modes, points)
    matrices = lower, upper, lower_back, upper_back, to_modes, to_planes, forth, back
    ready, carried2, near2, first1, far1, second0, kernel, matrices = sync(
        ready, carried2, near2, first1, far1, second0, kernel, matrices
    )
    lower, upper, lower_back, upper_back, to_modes, to_planes, forth, back = matrices
    near3, first2 = along_layers(ready, carried2)
    first1, near2 = jnp.stack(first1), jnp.stack(near2)
    second1 = over_y(first1)
    far2 = over_x(near2)
    ready = choose_targets(4, keep, got)
    keep0, give0 = forward(near0, far0, first0, 0, second0, 0, flag, lower, upper, to_modes)
    ready, near3, first2, second1, far2, keep0, give0 = sync(ready, near3, first2, second1, far2, keep0, give0)
    near4, _ = along_layers(ready)
    split = SPLIT[PARTS[2][0]]
    first3 = jnp.stack([piece[split:] for piece in first2])
    first2, near3 = jnp.stack([piece[:split] for piece in first2]), jnp.stack(near3)
    second2 = over_y(first2)
    far3 = over_x(near3)
    got0 = over_core(give0)
    keep1, give1 = forward(near1, far1, first1, 0, second1, 0, flag, lower, upper, to_modes)
    near4, far3, second2, first3, got0, keep1, give1 = sync(near4, far3, second2, first3, got0, keep1, give1)
    near4 = jnp.stack(near4)
    far4 = over_x(near4)
    second3 = over_y(first3)
    got1 = over_core(give1)
    keep2, give2 = forward(near2, far2, first1, SPLIT[1], second1, SPLIT[1], flag, lower, upper, to_modes)
    got2 = over_core(give2)
    keep3, give3 = forward(near3, far3, first2, 0, second2, 0, flag, lower, upper, to_modes)
    got3 = over_core(give3)
    keep4, give4 = forward(near4, far4, first3, 0, second3, 0, flag, lower, upper, to_modes)
    got4 = over_core(give4)

    spectra = [keep0, keep1, keep2, keep3, keep4, got0, got1, got2, got3, got4]
    filtered = middle(spectra, kernel, forth, back)

    orbit = [
        (first0, 0, second0, 0),
        (first1, 0, second1, 0),
        (first1, SPLIT[1], second1, SPLIT[1]),
        (first2, 0, second2, 0),
        (first3, 0, second3, 0),
    ]
    back_got = [over_core(values) for values in filtered[chunks:]]
    queue = [(j, skip) for j in range(chunks) for skip in range(0, SPLIT[j], BACK)]
    queue.reverse()
    result, home, sums = None, None, None
    for turn in range(len(queue) + 2):
        near = far = got = pieces = None
        if turn < len(queue):
            j, skip = queue[turn]
            first, at, second, there = orbit[j]
            orbitals = first, at + skip, second, there + skip
            near, far = inverse(
                filtered[j], back_got[j], skip, BACK, *orbitals, flag, lower_back, upper_back, to_planes
            )
        if turn:
            near, far, sums, home, result = sync(near, far, sums, home, result)
        if far is not None:
            got = over_x(far)
        if sums is not None:
            pieces = [sums[0][d] + sums[1][d] for d in range(layers)]
            pieces = [over_z(piece, d) if d else piece for d, piece in enumerate(pieces)]
        if home is not None:
            j, skip = queue[turn - 2]
            kept, sent = jnp.stack(home[:picks]), jnp.stack(home[picks:])
            own = jnp.where(here, kept, sent)
            other = over_core(jnp.where(here, sent, kept))
            index = jnp.arange(picks, dtype=jnp.int32) ^ first_bit
            place = jnp.concatenate([index, row_blocks(starts[j] + skip, BACK)])
            result = unpack(own, other, place, (picks,) + bands.shape[1:], result)
        sums = None if far is None else (near, got)
        home = pieces
    return result


def broadcast(x, axis, root):
    mine = lax.axis_index(axis) == root
    return lax.psum(jnp.where(mine, x, jnp.zeros_like(x)), axis)


def by_lines(bands, occupied, occ_index, band_pick):
    points, planes = bands.shape[2], bands.shape[1]
    window, per_group = occ_index.shape[0], occupied.shape[0]
    modes = jnp.arange(points, dtype=jnp.int32)
    matrix = cas_matrix(modes, modes, points)
    squares = wave_squared(modes, points)

    def transform(pattern, values):
        return jnp.einsum(pattern, values, matrix, precision=lax.Precision.HIGHEST)

    along_z, along_y, along_x = "pxyz,zk->pxyk", "pxyz,yk->pxkz", "pxyz,xk->pkyz"
    offset = lax.axis_index("slab") * planes
    row_squares = lax.dynamic_slice_in_dim(squares, offset, planes)
    kernel = screened(squares[:, None, None] + row_squares[None, :, None] + squares[None, None, :])
    kernel = kernel / float(points * points * points)
    targets = jnp.take(bands, band_pick, axis=0)

    def fetch_orbital(turn):
        which = occ_index[turn]
        own_orbital = lax.dynamic_index_in_dim(occupied, which % per_group, 0, keepdims=False)
        return broadcast(own_orbital, "band", which // per_group)

    orbitals = lax.map(fetch_orbital, jnp.arange(window, dtype=jnp.int32))
    density = (orbitals[:, None] * targets[None]).reshape((-1,) + targets.shape[1:])
    lines = transform(along_y, transform(along_z, density))
    lines = lax.all_to_all(lines, "slab", split_axis=2, concat_axis=1, tiled=True)
    lines = transform(along_x, kernel[None] * transform(along_x, lines))
    lines = lax.all_to_all(lines, "slab", split_axis=1, concat_axis=2, tiled=True)
    field = transform(along_z, transform(along_y, lines)).reshape((window,) + targets.shape)
    return -jnp.sum(field * orbitals[:, None], axis=0)


def solution(mesh):
    groups, slabs = mesh.shape["band"], mesh.shape["slab"]

    def shards(bands, occupied, occ_index, band_pick):
        picks, window = band_pick.shape[0], occ_index.shape[0]
        planes, points = bands.shape[1], bands.shape[2]
        fits = (
            window == 2
            and picks == 2
            and bands.shape[0] == picks
            and groups == 2 * CORES
            and slabs == CORES * picks * window
            and planes % 8 == 0
            and 2 * (points - LANES) == LANES
            and points == CORES * 2 * STEP * sum(SPLIT)
        )
        if fits:
            return by_layers(bands, occupied, occ_index, band_pick, groups, slabs)
        return by_lines(bands, occupied, occ_index, band_pick)

    placed = (P("band", "slab", None, None), P("band", "slab", None, None), P(), P("band"))
    return jax.shard_map(
        shards, mesh=mesh, in_specs=placed, out_specs=P("band", "slab", None, None), check_vma=False
    )
```

time: 688 us -> 632 us (0.919)
  the two profiles are of different devices: /device:TPU:0 before, /device:TPU:9 now
where the time goes in v2:
time: 632 us; the launch traced here: 622 us
  waiting for transfers between devices  291 us (46%)
  Pallas kernels  157 us (25%)
  starting transfers between devices  84.9 us (13%)
  other arithmetic  55.5 us (9%)
  local copies, waits for them, and re-layouts  31.8 us (5%)
    ppermute x75, waiting for transfers between devices, swap(): return lax.ppermute(values, axis, [(i, flip(i)) for i in range(size)])  291 us
    ppermute x75, starting transfers between devices, swap(): return lax.ppermute(values, axis, [(i, flip(i)) for i in range(size)])  84.9 us
    pallas_call x6, Pallas kernels, inverse(): pl.pallas_call(inverse_body, grid_spec=pltpu.PrefetchScalarGridSpec(num_s...  43.2 us
    pallas_call x5, Pallas kernels, forward(): pl.pallas_call(forward_body, grid_spec=pltpu.PrefetchScalarGridSpec(num_s...  41 us
    pallas_call x6, Pallas kernels, unpack(): pl.pallas_call(unpack_body, grid_spec=pltpu.PrefetchScalarGridSpec(num_sc...  25.5 us
    pallas_call x1, Pallas kernels, middle(): pl.pallas_call(lambda *refs: middle_body(count, *refs), grid=(deep // blo...  24.7 us
    pallas_call x4, Pallas kernels, pack(): pl.pallas_call(pack_body, grid_spec=pltpu.PrefetchScalarGridSpec(num_scal...  22.3 us
    unnamed x130, local copies, waits for them, and re-layouts  16.2 us
  transfers between devices with their start and end apart: 75, of which 32 were waited for; matrix products, arithmetic and copies ran while one was open for 10% of the time, Pallas kernels for 19%

profile of v2, /device:TPU:9, one launch (start us, length us, event | category | flops | bytes accessed | tf_op | source)
XLA Modules:
  0.0 622.1 jit_solution(7959346968432237897)
XLA Ops:
  24.0 8.3 %pack.7 = (f32[2,8,3,4,24,128]{5,4,3,2,1,0:T(8,128)}, f32[2,8,3,4,24,128]{5,4,3,2,1,0:T(8,128)}) custom-call(s32[4]{0:T(128)} %get-tuple-element.196.scalars, f32[2,24,192,192]{3,2,1,0:T(8,128)} %give_ref.7, f32[2,24,192,192]{3,2,1,0:T(8,128)} %give_ref.7), custom_call_target="tpu_custom_call" | custom-call | tf_op jit(solution)/shard_map/pack/pallas_call | solution.py:74
  42.4 8.6 %collective-permute-done.3 = f32[4,3,4,24,128]{4,3,2,1,0:T(8,128)} collective-permute-done((f32[4,3,4,24,128]{4,3,2,1,0:T(8,128)}, f32[4,3,4,24,128]{4,3,2,1,0:T(8,128)}, u32[]{:S(2)}, u32[]{:S(2)}) %collective-permute-start.3) | collective-permute-done | bytes 589856 | tf_op jit(solution)/shard_map/ppermute | solution.py:264
  58.7 8.7 %collective-permute-done.4 = f32[4,3,4,24,128]{4,3,2,1,0:T(8,128)S(1)} collective-permute-done((f32[4,3,4,24,128]{4,3,2,1,0:T(8,128)S(1)}, f32[4,3,4,24,128]{4,3,2,1,0:T(8,128)S(1)}, u32[]{:S(2)}, u32[]{:S(2)}) %collective-permute-start.4) | collective-permute-done | bytes 589856 | tf_op jit(solution)/shard_map/ppermute | solution.py:264
  70.9 11.5 %collective-permute-done.9 = f32[8,3,4,24,128]{4,3,2,1,0:T(8,128)S(1)} collective-permute-done((f32[8,3,4,24,128]{4,3,2,1,0:T(8,128)S(1)}, f32[8,3,4,24,128]{4,3,2,1,0:T(8,128)S(1)}, u32[]{:S(2)}, u32[]{:S(2)}) %collective-permute-start.9) | collective-permute-done | bytes 1179680 | tf_op jit(solution)/shard_map/ppermute | solution.py:264
  103.7 27.5 %collective-permute-done.12 = f32[6,3,4,24,128]{4,3,2,1,0:T(8,128)S(1)} collective-permute-done((f32[6,3,4,24,128]{4,3,2,1,0:T(8,128)}, f32[6,3,4,24,128]{4,3,2,1,0:T(8,128)S(1)}, u32[]{:S(2)}, u32[]{:S(2)}) %collective-permute-start.12) | collective-permute-done | bytes 884768 | tf_op jit(solution)/shard_map/ppermute | solution.py:264
  137.2 8.0 %collective-permute-done.13 = f32[2,3,4,24,128]{4,3,2,1,0:T(8,128)S(1)} collective-permute-done((f32[2,3,4,24,128]{4,3,2,1,0:T(8,128)S(1)}, f32[2,3,4,24,128]{4,3,2,1,0:T(8,128)S(1)}, u32[]{:S(2)}, u32[]{:S(2)}) %collective-permute-start.13) | collective-permute-done | bytes 294944 | tf_op jit(solution)/shard_map/ppermute | solution.py:264
  145.2 6.7 %collective-permute-done.14 = f32[4,3,4,24,128]{4,3,2,1,0:T(8,128)S(1)} collective-permute-done((f32[4,3,4,24,128]{4,3,2,1,0:T(8,128)S(1)}, f32[4,3,4,24,128]{4,3,2,1,0:T(8,128)S(1)}, u32[]{:S(2)}, u32[]{:S(2)}) %collective-permute-start.14) | collective-permute-done | bytes 589856 | tf_op jit(solution)/shard_map/ppermute | solution.py:264
  161.1 23.3 %collective-permute-done.16 = f32[6,3,4,24,128]{4,3,2,1,0:T(8,128)S(1)} collective-permute-done((f32[6,3,4,24,128]{4,3,2,1,0:T(8,128)}, f32[6,3,4,24,128]{4,3,2,1,0:T(8,128)S(1)}, u32[]{:S(2)}, u32[]{:S(2)}) %collective-permute-start.16) | collective-permute-done | bytes 884768 | tf_op jit(solution)/shard_map/ppermute | solution.py:264
  184.5 9.4 %fusion.1.refs_0_ = f32[96,192,192]{2,1,0:T(8,128)} fusion(f32[192]{0:T(256)S(1)} %fusion.50, f32[96,192]{1,0:T(8,128)S(1)} %broadcast_add_fusion), kind=kLoop, calls=%fused_computation.6 | loop fusion | flops 35389440 | bytes 14230272 | tf_op jit(solution)/shard_map/div | solution.py:384
  219.5 35.9 %collective-permute-done.23 = f32[6,3,4,24,128]{4,3,2,1,0:T(8,128)S(1)} collective-permute-done((f32[6,3,4,24,128]{4,3,2,1,0:T(8,128)S(1)}, f32[6,3,4,24,128]{4,3,2,1,0:T(8,128)S(1)}, u32[]{:S(2)}, u32[]{:S(2)}) %collective-permute-start.23) | collective-permute-done | bytes 884768 | tf_op jit(solution)/shard_map/ppermute | solution.py:264
  259.9 12.0 %forward.5 = (f32[96,32,192]{2,1,0:T(8,128)}, f32[96,32,192]{2,1,0:T(8,128)}) custom-call(s32[1]{0:T(128)} %bitcast.2.scalars, f32[4,4,3,4,24,128]{5,4,3,2,1,0:T(8,128)} %copy-done.8, f32[4,4,3,4,24,128]{5,4,3,2,1,0:T(8,128)} %collective-permute-done.15.far, f32[4,4,3,4,24,128]{5,4,3,2,1,0:T(8,128)} %copy-done.3, f32[4,4,3,4,24,128]{5,4,3,2,1,0:T(8,128)} %copy-done.4, ...), custom_call_target="tpu_custom_call" | custom-call | tf_op jit(solution)/shard_map/forward/pallas_call | solution.py:162
  286.5 11.1 %collective-permute-done.28 = f32[2,3,4,24,128]{4,3,2,1,0:T(8,128)S(1)} collective-permute-done((f32[2,3,4,24,128]{4,3,2,1,0:T(8,128)S(1)}, f32[2,3,4,24,128]{4,3,2,1,0:T(8,128)S(1)}, u32[]{:S(2)}, u32[]{:S(2)}) %collective-permute-start.28) | collective-permute-done | bytes 294944 | tf_op jit(solution)/shard_map/ppermute | solution.py:264
  298.1 7.3 %forward.6 = (f32[96,16,192]{2,1,0:T(8,128)}, f32[96,16,192]{2,1,0:T(8,128)}) custom-call(s32[1]{0:T(128)} %bitcast.2.scalars, f32[4,2,3,4,24,128]{5,4,3,2,1,0:T(8,128)} %copy-done.11, f32[4,2,3,4,24,128]{5,4,3,2,1,0:T(8,128)} %copy-done.46, f32[4,4,3,4,24,128]{5,4,3,2,1,0:T(8,128)} %copy-done.2, f32[4,4,3,4,24,128]{5,4,3,2,1,0:T(8,128)} %collective-permute-done.26.second, ...), custom_call_target="tpu_custom_call" | custom-call | tf_op jit(solution)/shard_map/forward/pallas_call | solution.py:162
  305.5 7.4 %collective-permute-done.30 = f32[2,3,4,24,128]{4,3,2,1,0:T(8,128)S(1)} collective-permute-done((f32[2,3,4,24,128]{4,3,2,1,0:T(8,128)}, f32[2,3,4,24,128]{4,3,2,1,0:T(8,128)S(1)}, u32[]{:S(2)}, u32[]{:S(2)}) %collective-permute-start.30) | collective-permute-done | bytes 294944 | tf_op jit(solution)/shard_map/ppermute | solution.py:264
  315.2 7.3 %forward.7 = (f32[96,16,192]{2,1,0:T(8,128)}, f32[96,16,192]{2,1,0:T(8,128)}) custom-call(s32[1]{0:T(128)} %bitcast.2.scalars, f32[4,2,3,4,24,128]{5,4,3,2,1,0:T(8,128)} %pad_maximum_fusion.4.near, f32[4,2,3,4,24,128]{5,4,3,2,1,0:T(8,128)} %collective-permute-done.27.far, f32[4,4,3,4,24,128]{5,4,3,2,1,0:T(8,128)} %copy-done.2, ...), custom_call_target="tpu_custom_call" | custom-call | tf_op jit(solution)/shard_map/forward/pallas_call | solution.py:162
  324.6 7.2 %forward.8 = (f32[96,16,192]{2,1,0:T(8,128)}, f32[96,16,192]{2,1,0:T(8,128)}) custom-call(s32[1]{0:T(128)} %bitcast.2.scalars, f32[4,2,3,4,24,128]{5,4,3,2,1,0:T(8,128)} %copy-done.12, f32[4,2,3,4,24,128]{5,4,3,2,1,0:T(8,128)} %copy-done.47, f32[4,2,3,4,24,128]{5,4,3,2,1,0:T(8,128)} %copy-done.6, f32[4,2,3,4,24,128]{5,4,3,2,1,0:T(8,128)} %copy-done.14, ...), custom_call_target="tpu_custom_call" | custom-call | tf_op jit(solution)/shard_map/forward/pallas_call | solution.py:162
  332.4 7.8 %collective-permute-done.34.far = f32[4,2,3,4,24,128]{5,4,3,2,1,0:T(8,128)} collective-permute-done((f32[4,2,3,4,24,128]{5,4,3,2,1,0:T(8,128)S(1)}, f32[4,2,3,4,24,128]{5,4,3,2,1,0:T(8,128)}, u32[]{:S(2)}, u32[]{:S(2)}) %collective-permute-start.34) | collective-permute-done | bytes 1179680 | tf_op jit(solution)/shard_map/ppermute | solution.py:264
  341.2 7.3 %forward.9 = (f32[96,16,192]{2,1,0:T(8,128)}, f32[96,16,192]{2,1,0:T(8,128)}) custom-call(s32[1]{0:T(128)} %bitcast.2.scalars, f32[4,2,3,4,24,128]{5,4,3,2,1,0:T(8,128)} %copy-done.13, f32[4,2,3,4,24,128]{5,4,3,2,1,0:T(8,128)} %collective-permute-done.34.far, f32[4,2,3,4,24,128]{5,4,3,2,1,0:T(8,128)} %copy-done.7, f32[4,2,3,4,24,128]{5,4,3,2,1,0:T(8,128)} %copy-done.16, ...), custom_call_target="tpu_custom_call" | custom-call | tf_op jit(solution)/shard_map/forward/pallas_call | solution.py:162
  355.5 24.7 %middle.1 = (f32[96,32,192]{2,1,0:T(8,128)}, f32[96,16,192]{2,1,0:T(8,128)}, f32[96,16,192]{2,1,0:T(8,128)}, f32[96,16,192]{2,1,0:T(8,128)}, f32[96,16,192]{2,1,...) custom-call(f32[96,192,192]{2,1,0:T(8,128)} %fusion.1.refs_0_, ...), custom_call_target="tpu_custom_call" | custom-call | tf_op jit(solution)/shard_map/middle/pallas_call | solution.py:196
  385.1 7.2 %inverse.11 = (f32[4,2,3,4,24,128]{5,4,3,2,1,0:T(8,128)}, f32[4,2,3,4,24,128]{5,4,3,2,1,0:T(8,128)}) custom-call(s32[1]{0:T(128)} %bitcast.2.scalars, f32[96,16,192]{2,1,0:T(8,128)} %get-tuple-element.312.keep_ref, f32[96,16,192]{2,1,0:T(8,128)} %copy-done.29, f32[4,2,3,4,24,128]{5,4,3,2,1,0:T(8,128)} %copy-done.7, f32[4,2,3,4,24,128]{5,4,3,2,1,0:T(8,128)} %copy-done.16, ...), custom_call_target="tpu_custom_call" | custom-call | tf_op jit(solution)/shard_map/inverse/pallas_call | solution.py:234
  395.1 7.3 %inverse.10 = (f32[4,2,3,4,24,128]{5,4,3,2,1,0:T(8,128)}, f32[4,2,3,4,24,128]{5,4,3,2,1,0:T(8,128)}) custom-call(s32[1]{0:T(128)} %bitcast.2.scalars, f32[96,16,192]{2,1,0:T(8,128)} %get-tuple-element.308.keep_ref, f32[96,16,192]{2,1,0:T(8,128)} %copy-done.28, f32[4,2,3,4,24,128]{5,4,3,2,1,0:T(8,128)} %copy-done.6, f32[4,2,3,4,24,128]{5,4,3,2,1,0:T(8,128)} %copy-done.14, ...), custom_call_target="tpu_custom_call" | custom-call | tf_op jit(solution)/shard_map/inverse/pallas_call | solution.py:234
  402.3 17.3 %collective-permute-done.45 = f32[4,2,3,4,24,128]{5,4,3,2,1,0:T(8,128)S(1)} collective-permute-done((f32[4,2,3,4,24,128]{5,4,3,2,1,0:T(8,128)}, f32[4,2,3,4,24,128]{5,4,3,2,1,0:T(8,128)S(1)}, u32[]{:S(2)}, u32[]{:S(2)}) %collective-permute-start.45) | collective-permute-done | bytes 1179680 | tf_op jit(solution)/shard_map/ppermute | solution.py:264
  432.8 7.2 %inverse.9 = (f32[4,2,3,4,24,128]{5,4,3,2,1,0:T(8,128)}, f32[4,2,3,4,24,128]{5,4,3,2,1,0:T(8,128)}) custom-call(s32[1]{0:T(128)} %bitcast.2.scalars, f32[96,16,192]{2,1,0:T(8,128)} %get-tuple-element.304.keep_ref, f32[96,16,192]{2,1,0:T(8,128)} %copy-done.27, f32[4,4,3,4,24,128]{5,4,3,2,1,0:T(8,128)} %copy-done.2, ...), custom_call_target="tpu_custom_call" | custom-call | tf_op jit(solution)/shard_map/inverse/pallas_call | solution.py:234
  440.0 7.8 %collective-permute-done.49 = f32[2,3,4,24,128]{4,3,2,1,0:T(8,128)S(1)} collective-permute-done((f32[2,3,4,24,128]{4,3,2,1,0:T(8,128)S(1)}, f32[2,3,4,24,128]{4,3,2,1,0:T(8,128)S(1)}, u32[]{:S(2)}, u32[]{:S(2)}) %collective-permute-start.49) | collective-permute-done | bytes 294944 | tf_op jit(solution)/shard_map/ppermute | solution.py:264
  458.3 7.1 %inverse.8 = (f32[4,2,3,4,24,128]{5,4,3,2,1,0:T(8,128)}, f32[4,2,3,4,24,128]{5,4,3,2,1,0:T(8,128)}) custom-call(s32[1]{0:T(128)} %bitcast.2.scalars, f32[96,16,192]{2,1,0:T(8,128)} %get-tuple-element.300.keep_ref, f32[96,16,192]{2,1,0:T(8,128)} %collective-permute-done.41.got_ref, f32[4,4,3,4,24,128]{5,4,3,2,1,0:T(8,128)} %copy-done.2, ...), custom_call_target="tpu_custom_call" | custom-call | tf_op jit(solution)/shard_map/inverse/pallas_call | solution.py:234
  475.7 7.4 %collective-permute-done.53 = f32[2,3,4,24,128]{4,3,2,1,0:T(8,128)} collective-permute-done((f32[2,3,4,24,128]{4,3,2,1,0:T(8,128)}, f32[2,3,4,24,128]{4,3,2,1,0:T(8,128)}, u32[]{:S(2)}, u32[]{:S(2)}) %collective-permute-start.53) | collective-permute-done | bytes 294944 | tf_op jit(solution)/shard_map/ppermute | solution.py:264
  493.5 7.1 %inverse.7 = (f32[4,2,3,4,24,128]{5,4,3,2,1,0:T(8,128)}, f32[4,2,3,4,24,128]{5,4,3,2,1,0:T(8,128)}) custom-call(s32[1]{0:T(128)} %bitcast.2.scalars, f32[96,32,192]{2,1,0:T(8,128)} %get-tuple-element.291.keep_ref, f32[96,32,192]{2,1,0:T(8,128)} %copy-done.5, f32[4,4,3,4,24,128]{5,4,3,2,1,0:T(8,128)} %copy-done.3, f32[4,4,3,4,24,128]{5,4,3,2,1,0:T(8,128)} %copy-done.4, ...), custom_call_target="tpu_custom_call" | custom-call | tf_op jit(solution)/shard_map/inverse/pallas_call | solution.py:234
  505.7 12.9 %collective-permute-done.58 = f32[2,3,4,24,128]{4,3,2,1,0:T(8,128)S(1)} collective-permute-done((f32[2,3,4,24,128]{4,3,2,1,0:T(8,128)S(1)}, f32[2,3,4,24,128]{4,3,2,1,0:T(8,128)S(1)}, u32[]{:S(2)}, u32[]{:S(2)}) %collective-permute-start.58) | collective-permute-done | bytes 294944 | tf_op jit(solution)/shard_map/ppermute | solution.py:264
  524.3 7.3 %inverse.6 = (f32[4,2,3,4,24,128]{5,4,3,2,1,0:T(8,128)}, f32[4,2,3,4,24,128]{5,4,3,2,1,0:T(8,128)}) custom-call(s32[1]{0:T(128)} %bitcast.2.scalars, f32[96,32,192]{2,1,0:T(8,128)} %get-tuple-element.291.keep_ref, f32[96,32,192]{2,1,0:T(8,128)} %copy-done.5, f32[4,4,3,4,24,128]{5,4,3,2,1,0:T(8,128)} %copy-done.3, f32[4,4,3,4,24,128]{5,4,3,2,1,0:T(8,128)} %copy-done.4, ...), custom_call_target="tpu_custom_call" | custom-call | tf_op jit(solution)/shard_map/inverse/pallas_call | solution.py:234
  537.1 12.5 %collective-permute-done.63 = f32[2,3,4,24,128]{4,3,2,1,0:T(8,128)S(1)} collective-permute-done((f32[2,3,4,24,128]{4,3,2,1,0:T(8,128)S(1)}, f32[2,3,4,24,128]{4,3,2,1,0:T(8,128)S(1)}, u32[]{:S(2)}, u32[]{:S(2)}) %collective-permute-start.63) | collective-permute-done | bytes 294944 | tf_op jit(solution)/shard_map/ppermute | solution.py:264
  568.6 13.1 %collective-permute-done.68 = f32[2,3,4,24,128]{4,3,2,1,0:T(8,128)S(1)} collective-permute-done((f32[2,3,4,24,128]{4,3,2,1,0:T(8,128)S(1)}, f32[2,3,4,24,128]{4,3,2,1,0:T(8,128)S(1)}, u32[]{:S(2)}, u32[]{:S(2)}) %collective-permute-start.68) | collective-permute-done | bytes 294944 | tf_op jit(solution)/shard_map/ppermute | solution.py:264
  599.4 13.1 %collective-permute-done.72 = f32[2,3,4,24,128]{4,3,2,1,0:T(8,128)S(1)} collective-permute-done((f32[2,3,4,24,128]{4,3,2,1,0:T(8,128)S(1)}, f32[2,3,4,24,128]{4,3,2,1,0:T(8,128)S(1)}, u32[]{:S(2)}, u32[]{:S(2)}) %collective-permute-start.72) | collective-permute-done | bytes 294944 | tf_op jit(solution)/shard_map/ppermute | solution.py:264
  (371 shorter events, 252.4 us)
Async XLA Ops:
  23.9 29.9 %collective-permute-start.8 = (f32[2,8,3,4,24,128]{5,4,3,2,1,0:T(8,128)}, f32[2,8,3,4,24,128]{5,4,3,2,1,0:T(8,128)}, u32[]{:S(2)}, u32[]{:S(2)}) collective-permute-start(f32[2,8,3,4,24,128]{5,4,3,2,1,0:T(8,128)} %get-tuple-element.200), channel_id=1, source_target_pairs={{0,8},{8,0},{16,24},{24,16},{1,9},{9,1},{17,25},{25,17},{2,10},{10... | collective-permute-start | bytes 7077896 | tf_op jit(solution)/shard_map/ppermute | solution.py:264
  38.1 47.3 %collective-permute-start.5 = (f32[4,3,4,24,128]{4,3,2,1,0:T(8,128)}, f32[4,3,4,24,128]{4,3,2,1,0:T(8,128)S(1)}, u32[]{:S(2)}, u32[]{:S(2)}) collective-permute-start(f32[4,3,4,24,128]{4,3,2,1,0:T(8,128)} %get-tuple-element.189), channel_id=1, source_target_pairs={{0,2},{1,3},{2,0},{3,1},{4,6},{5,7},{6,4},{7,5},{8,10},{9,11},{10,... | collective-permute-start | bytes 1769480 | tf_op jit(solution)/shard_map/ppermute | solution.py:264
  38.3 47.2 %collective-permute-start.6 = (f32[4,3,4,24,128]{4,3,2,1,0:T(8,128)}, f32[4,3,4,24,128]{4,3,2,1,0:T(8,128)S(1)}, u32[]{:S(2)}, u32[]{:S(2)}) collective-permute-start(f32[4,3,4,24,128]{4,3,2,1,0:T(8,128)} %get-tuple-element.190), channel_id=1, source_target_pairs={{0,4},{1,5},{2,6},{3,7},{4,0},{5,1},{6,2},{7,3},{8,12},{9,13},{10,... | collective-permute-start | bytes 1769480 | tf_op jit(solution)/shard_map/ppermute | solution.py:264
  51.1 40.7 %collective-permute-start.7 = (f32[4,3,4,24,128]{4,3,2,1,0:T(8,128)S(1)}, f32[4,3,4,24,128]{4,3,2,1,0:T(8,128)S(1)}, u32[]{:S(2)}, u32[]{:S(2)}) collective-permute-start(f32[4,3,4,24,128]{4,3,2,1,0:T(8,128)S(1)} %copy-done.49), channel_id=1, source_target_pairs={{0,6},{1,7},{2,4},{3,5},{4,2},{5,3},{6,0},{7,1},{8,14},{9,15},{10,... | collective-permute-start | bytes 1769480 | tf_op jit(solution)/shard_map/ppermute | solution.py:264
  92.0 60.0 %collective-permute-start.15 = (f32[4,4,3,4,24,128]{5,4,3,2,1,0:T(8,128)S(1)}, f32[4,4,3,4,24,128]{5,4,3,2,1,0:T(8,128)}, u32[]{:S(2)}, u32[]{:S(2)}) collective-permute-start(f32[4,4,3,4,24,128]{5,4,3,2,1,0:T(8,128)S(1)} %pad_maximum_fusion.near), channel_id=1, source_target_pairs={{0,1},{1,0},{2,3},{3,2},{4,5},{5,4},{6,7},{7,6},{8,9},{9,8},{10,11... | collective-permute-start | bytes 7077896 | tf_op jit(solution)/shard_map/ppermute | solution.py:264
  92.9 41.8 %collective-permute-start.10 = (f32[8,3,4,24,128]{4,3,2,1,0:T(8,128)}, f32[8,3,4,24,128]{4,3,2,1,0:T(8,128)S(1)}, u32[]{:S(2)}, u32[]{:S(2)}) collective-permute-start(f32[8,3,4,24,128]{4,3,2,1,0:T(8,128)} %get-tuple-element.204), channel_id=1, source_target_pairs={{0,16},{8,24},{16,0},{24,8},{1,17},{9,25},{17,1},{25,9},{2,18},{10... | collective-permute-start | bytes 3538952 | tf_op jit(solution)/shard_map/ppermute | solution.py:264
  94.2 37.0 %collective-permute-start.12 = (f32[6,3,4,24,128]{4,3,2,1,0:T(8,128)}, f32[6,3,4,24,128]{4,3,2,1,0:T(8,128)S(1)}, u32[]{:S(2)}, u32[]{:S(2)}) collective-permute-start(f32[6,3,4,24,128]{4,3,2,1,0:T(8,128)} %get-tuple-element.207), channel_id=1, source_target_pairs={{0,4},{1,5},{2,6},{3,7},{4,0},{5,1},{6,2},{7,3},{8,12},{9,13},{10,... | collective-permute-start | bytes 2654216 | tf_op jit(solution)/shard_map/ppermute | solution.py:264
  94.2 39.5 %collective-permute-start.11 = (f32[6,3,4,24,128]{4,3,2,1,0:T(8,128)}, f32[6,3,4,24,128]{4,3,2,1,0:T(8,128)S(1)}, u32[]{:S(2)}, u32[]{:S(2)}) collective-permute-start(f32[6,3,4,24,128]{4,3,2,1,0:T(8,128)} %get-tuple-element.206), channel_id=1, source_target_pairs={{0,2},{1,3},{2,0},{3,1},{4,6},{5,7},{6,4},{7,5},{8,10},{9,11},{10,... | collective-permute-start | bytes 2654216 | tf_op jit(solution)/shard_map/ppermute | solution.py:264
  100.0 45.1 %collective-permute-start.13 = (f32[2,3,4,24,128]{4,3,2,1,0:T(8,128)S(1)}, f32[2,3,4,24,128]{4,3,2,1,0:T(8,128)S(1)}, u32[]{:S(2)}, u32[]{:S(2)}) collective-permute-start(f32[2,3,4,24,128]{4,3,2,1,0:T(8,128)S(1)} %copy-done.63), channel_id=1, source_target_pairs={{0,6},{1,7},{2,4},{3,5},{4,2},{5,3},{6,0},{7,1},{8,14},{9,15},{10,... | collective-permute-start | bytes 884744 | tf_op jit(solution)/shard_map/ppermute | solution.py:264
  152.8 31.7 %collective-permute-start.16 = (f32[6,3,4,24,128]{4,3,2,1,0:T(8,128)}, f32[6,3,4,24,128]{4,3,2,1,0:T(8,128)S(1)}, u32[]{:S(2)}, u32[]{:S(2)}) collective-permute-start(f32[6,3,4,24,128]{4,3,2,1,0:T(8,128)} %get-tuple-element.216), channel_id=1, source_target_pairs={{0,2},{1,3},{2,0},{3,1},{4,6},{5,7},{6,4},{7,5},{8,10},{9,11},{10,... | collective-permute-start | bytes 2654216 | tf_op jit(solution)/shard_map/ppermute | solution.py:264
  155.7 57.3 %collective-permute-start.21 = (f32[4,4,3,4,24,128]{5,4,3,2,1,0:T(8,128)S(1)}, f32[4,4,3,4,24,128]{5,4,3,2,1,0:T(8,128)S(1)}, u32[]{:S(2)}, u32[]{:S(2)}) collective-permute-start(f32[4,4,3,4,24,128]{5,4,3,2,1,0:T(8,128)S(1)} %pad_maximum_fusion.1.first), channel_id=1, source_target_pairs={{0,16},{8,24},{16,0},{24,8},{1,17},{9,25},{17,1},{25,9},{2,18},{10... | collective-permute-start | bytes 7077896 | tf_op jit(solution)/shard_map/ppermute | solution.py:264
  157.1 53.8 %collective-permute-start.20 = (f32[4,2,3,4,24,128]{5,4,3,2,1,0:T(8,128)S(1)}, f32[4,2,3,4,24,128]{5,4,3,2,1,0:T(8,128)S(1)}, u32[]{:S(2)}, u32[]{:S(2)}) collective-permute-start(f32[4,2,3,4,24,128]{5,4,3,2,1,0:T(8,128)S(1)} %pad_maximum_fusion.3.near), channel_id=1, source_target_pairs={{0,1},{1,0},{2,3},{3,2},{4,5},{5,4},{6,7},{7,6},{8,9},{9,8},{10,11... | collective-permute-start | bytes 3538952 | tf_op jit(solution)/shard_map/ppermute | solution.py:264
  158.1 42.5 %collective-permute-start.17 = (f32[6,3,4,24,128]{4,3,2,1,0:T(8,128)S(1)}, f32[6,3,4,24,128]{4,3,2,1,0:T(8,128)S(1)}, u32[]{:S(2)}, u32[]{:S(2)}) collective-permute-start(f32[6,3,4,24,128]{4,3,2,1,0:T(8,128)S(1)} %copy-done.48), channel_id=1, source_target_pairs={{0,4},{1,5},{2,6},{3,7},{4,0},{5,1},{6,2},{7,3},{8,12},{9,13},{10,... | collective-permute-start | bytes 2654216 | tf_op jit(solution)/shard_map/ppermute | solution.py:264
  159.4 51.6 %collective-permute-start.18 = (f32[2,3,4,24,128]{4,3,2,1,0:T(8,128)S(1)}, f32[2,3,4,24,128]{4,3,2,1,0:T(8,128)S(1)}, u32[]{:S(2)}, u32[]{:S(2)}) collective-permute-start(f32[2,3,4,24,128]{4,3,2,1,0:T(8,128)S(1)} %copy-done.62), channel_id=1, source_target_pairs={{0,6},{1,7},{2,4},{3,5},{4,2},{5,3},{6,0},{7,1},{8,14},{9,15},{10,... | collective-permute-start | bytes 884744 | tf_op jit(solution)/shard_map/ppermute | solution.py:264
  214.4 59.5 %collective-permute-start.26 = (f32[4,4,3,4,24,128]{5,4,3,2,1,0:T(8,128)S(1)}, f32[4,4,3,4,24,128]{5,4,3,2,1,0:T(8,128)}, u32[]{:S(2)}, u32[]{:S(2)}) collective-permute-start(f32[4,4,3,4,24,128]{5,4,3,2,1,0:T(8,128)S(1)} %pad_maximum_fusion.2.first), channel_id=1, source_target_pairs={{0,16},{8,24},{16,0},{24,8},{1,17},{9,25},{17,1},{25,9},{2,18},{10... | collective-permute-start | bytes 7077896 | tf_op jit(solution)/shard_map/ppermute | solution.py:264
  214.8 40.6 %collective-permute-start.23 = (f32[6,3,4,24,128]{4,3,2,1,0:T(8,128)S(1)}, f32[6,3,4,24,128]{4,3,2,1,0:T(8,128)S(1)}, u32[]{:S(2)}, u32[]{:S(2)}) collective-permute-start(f32[6,3,4,24,128]{4,3,2,1,0:T(8,128)S(1)} %get-tuple-element.238), channel_id=1, source_target_pairs={{0,4},{1,5},{2,6},{3,7},{4,0},{5,1},{6,2},{7,3},{8,12},{9,13},{10,... | collective-permute-start | bytes 2654216 | tf_op jit(solution)/shard_map/ppermute | solution.py:264
  219.2 54.7 %collective-permute-start.27 = (f32[4,2,3,4,24,128]{5,4,3,2,1,0:T(8,128)}, f32[4,2,3,4,24,128]{5,4,3,2,1,0:T(8,128)}, u32[]{:S(2)}, u32[]{:S(2)}) collective-permute-start(f32[4,2,3,4,24,128]{5,4,3,2,1,0:T(8,128)} %pad_maximum_fusion.4.near), channel_id=1, source_target_pairs={{0,1},{1,0},{2,3},{3,2},{4,5},{5,4},{6,7},{7,6},{8,9},{9,8},{10,11... | collective-permute-start | bytes 3538952 | tf_op jit(solution)/shard_map/ppermute | solution.py:264
  219.5 52.3 %collective-permute-start.22 = (f32[6,3,4,24,128]{4,3,2,1,0:T(8,128)}, f32[6,3,4,24,128]{4,3,2,1,0:T(8,128)}, u32[]{:S(2)}, u32[]{:S(2)}) collective-permute-start(f32[6,3,4,24,128]{4,3,2,1,0:T(8,128)} %get-tuple-element.237), channel_id=1, source_target_pairs={{0,2},{1,3},{2,0},{3,1},{4,6},{5,7},{6,4},{7,5},{8,10},{9,11},{10,... | collective-permute-start | bytes 2654216 | tf_op jit(solution)/shard_map/ppermute | solution.py:264
  274.0 38.9 %collective-permute-start.33 = (f32[96,32,192]{2,1,0:T(8,128)}, f32[96,32,192]{2,1,0:T(8,128)}, u32[]{:S(2)}, u32[]{:S(2)}) collective-permute-start(f32[96,32,192]{2,1,0:T(8,128)} %get-tuple-element.269), channel_id=1, source_target_pairs={{0,8},{8,0},{16,24},{24,16},{1,9},{9,1},{17,25},{25,17},{2,10},{10... | collective-permute-start | bytes 7077896 | tf_op jit(solution)/shard_map/ppermute | solution.py:264
  276.5 36.4 %collective-permute-start.32 = (f32[4,2,3,4,24,128]{5,4,3,2,1,0:T(8,128)S(1)}, f32[4,2,3,4,24,128]{5,4,3,2,1,0:T(8,128)S(1)}, u32[]{:S(2)}, u32[]{:S(2)}) collective-permute-start(f32[4,2,3,4,24,128]{5,4,3,2,1,0:T(8,128)S(1)} %pad_maximum_fusion.6.first), channel_id=1, source_target_pairs={{0,16},{8,24},{16,0},{24,8},{1,17},{9,25},{17,1},{25,9},{2,18},{10... | collective-permute-start | bytes 3538952 | tf_op jit(solution)/shard_map/ppermute | solution.py:264
  278.7 34.2 %collective-permute-start.31 = (f32[4,2,3,4,24,128]{5,4,3,2,1,0:T(8,128)S(1)}, f32[4,2,3,4,24,128]{5,4,3,2,1,0:T(8,128)S(1)}, u32[]{:S(2)}, u32[]{:S(2)}) collective-permute-start(f32[4,2,3,4,24,128]{5,4,3,2,1,0:T(8,128)S(1)} %pad_maximum_fusion.5.near), channel_id=1, source_target_pairs={{0,1},{1,0},{2,3},{3,2},{4,5},{5,4},{6,7},{7,6},{8,9},{9,8},{10,11... | collective-permute-start | bytes 3538952 | tf_op jit(solution)/shard_map/ppermute | solution.py:264
  322.5 28.6 %collective-permute-start.37 = (f32[96,16,192]{2,1,0:T(8,128)}, f32[96,16,192]{2,1,0:T(8,128)S(1)}, u32[]{:S(2)}, u32[]{:S(2)}) collective-permute-start(f32[96,16,192]{2,1,0:T(8,128)} %get-tuple-element.288), channel_id=1, source_target_pairs={{0,8},{8,0},{16,24},{24,16},{1,9},{9,1},{17,25},{25,17},{2,10},{10... | collective-permute-start | bytes 3538952 | tf_op jit(solution)/shard_map/ppermute | solution.py:264
  392.3 27.4 %collective-permute-start.45 = (f32[4,2,3,4,24,128]{5,4,3,2,1,0:T(8,128)}, f32[4,2,3,4,24,128]{5,4,3,2,1,0:T(8,128)S(1)}, u32[]{:S(2)}, u32[]{:S(2)}) collective-permute-start(f32[4,2,3,4,24,128]{5,4,3,2,1,0:T(8,128)} %get-tuple-element.315), channel_id=1, source_target_pairs={{0,1},{1,0},{2,3},{3,2},{4,5},{5,4},{6,7},{7,6},{8,9},{9,8},{10,11... | collective-permute-start | bytes 3538952 | tf_op jit(solution)/shard_map/ppermute | solution.py:264
  393.3 30.3 %collective-permute-start.42 = (f32[96,16,192]{2,1,0:T(8,128)}, f32[96,16,192]{2,1,0:T(8,128)S(1)}, u32[]{:S(2)}, u32[]{:S(2)}) collective-permute-start(f32[96,16,192]{2,1,0:T(8,128)} %get-tuple-element.305), channel_id=1, source_target_pairs={{0,8},{8,0},{16,24},{24,16},{1,9},{9,1},{17,25},{25,17},{2,10},{10... | collective-permute-start | bytes 3538952 | tf_op jit(solution)/shard_map/ppermute | solution.py:264
  419.6 28.2 %collective-permute-start.46 = (f32[4,2,3,4,24,128]{5,4,3,2,1,0:T(8,128)}, f32[4,2,3,4,24,128]{5,4,3,2,1,0:T(8,128)S(1)}, u32[]{:S(2)}, u32[]{:S(2)}) collective-permute-start(f32[4,2,3,4,24,128]{5,4,3,2,1,0:T(8,128)} %get-tuple-element.317), channel_id=1, source_target_pairs={{0,1},{1,0},{2,3},{3,2},{4,5},{5,4},{6,7},{7,6},{8,9},{9,8},{10,11... | collective-permute-start | bytes 3538952 | tf_op jit(solution)/shard_map/ppermute | solution.py:264
  423.5 30.7 %collective-permute-start.41 = (f32[96,16,192]{2,1,0:T(8,128)}, f32[96,16,192]{2,1,0:T(8,128)}, u32[]{:S(2)}, u32[]{:S(2)}) collective-permute-start(f32[96,16,192]{2,1,0:T(8,128)} %get-tuple-element.301), channel_id=1, source_target_pairs={{0,8},{8,0},{16,24},{24,16},{1,9},{9,1},{17,25},{25,17},{2,10},{10... | collective-permute-start | bytes 3538952 | tf_op jit(solution)/shard_map/ppermute | solution.py:264
  430.2 61.6 %collective-permute-start.40 = (f32[96,32,192]{2,1,0:T(8,128)}, f32[96,32,192]{2,1,0:T(8,128)S(1)}, u32[]{:S(2)}, u32[]{:S(2)}) collective-permute-start(f32[96,32,192]{2,1,0:T(8,128)} %get-tuple-element.292), channel_id=1, source_target_pairs={{0,8},{8,0},{16,24},{24,16},{1,9},{9,1},{17,25},{25,17},{2,10},{10... | collective-permute-start | bytes 7077896 | tf_op jit(solution)/shard_map/ppermute | solution.py:264
  447.8 35.2 %collective-permute-start.50 = (f32[4,2,3,4,24,128]{5,4,3,2,1,0:T(8,128)}, f32[4,2,3,4,24,128]{5,4,3,2,1,0:T(8,128)}, u32[]{:S(2)}, u32[]{:S(2)}) collective-permute-start(f32[4,2,3,4,24,128]{5,4,3,2,1,0:T(8,128)} %get-tuple-element.321), channel_id=1, source_target_pairs={{0,1},{1,0},{2,3},{3,2},{4,5},{5,4},{6,7},{7,6},{8,9},{9,8},{10,11... | collective-permute-start | bytes 3538952 | tf_op jit(solution)/shard_map/ppermute | solution.py:264
  483.0 35.6 %collective-permute-start.55 = (f32[4,2,3,4,24,128]{5,4,3,2,1,0:T(8,128)}, f32[4,2,3,4,24,128]{5,4,3,2,1,0:T(8,128)S(1)}, u32[]{:S(2)}, u32[]{:S(2)}) collective-permute-start(f32[4,2,3,4,24,128]{5,4,3,2,1,0:T(8,128)} %get-tuple-element.329), channel_id=1, source_target_pairs={{0,1},{1,0},{2,3},{3,2},{4,5},{5,4},{6,7},{7,6},{8,9},{9,8},{10,11... | collective-permute-start | bytes 3538952 | tf_op jit(solution)/shard_map/ppermute | solution.py:264
  491.8 26.8 %collective-permute-start.58 = (f32[2,3,4,24,128]{4,3,2,1,0:T(8,128)S(1)}, f32[2,3,4,24,128]{4,3,2,1,0:T(8,128)S(1)}, u32[]{:S(2)}, u32[]{:S(2)}) collective-permute-start(f32[2,3,4,24,128]{4,3,2,1,0:T(8,128)S(1)} %get-tuple-element.387), channel_id=1, source_target_pairs={{0,6},{1,7},{2,4},{3,5},{4,2},{5,3},{6,0},{7,1},{8,14},{9,15},{10,... | collective-permute-start | bytes 884744 | tf_op jit(solution)/shard_map/ppermute | solution.py:264
  518.6 31.0 %collective-permute-start.60 = (f32[4,2,3,4,24,128]{5,4,3,2,1,0:T(8,128)}, f32[4,2,3,4,24,128]{5,4,3,2,1,0:T(8,128)S(1)}, u32[]{:S(2)}, u32[]{:S(2)}) collective-permute-start(f32[4,2,3,4,24,128]{5,4,3,2,1,0:T(8,128)} %get-tuple-element.338), channel_id=1, source_target_pairs={{0,1},{1,0},{2,3},{3,2},{4,5},{5,4},{6,7},{7,6},{8,9},{9,8},{10,11... | collective-permute-start | bytes 3538952 | tf_op jit(solution)/shard_map/ppermute | solution.py:264
  549.7 32.0 %collective-permute-start.65 = (f32[4,2,3,4,24,128]{5,4,3,2,1,0:T(8,128)S(1)}, f32[4,2,3,4,24,128]{5,4,3,2,1,0:T(8,128)S(1)}, u32[]{:S(2)}, u32[]{:S(2)}) collective-permute-start(f32[4,2,3,4,24,128]{5,4,3,2,1,0:T(8,128)S(1)} %copy-done.64), channel_id=1, source_target_pairs={{0,1},{1,0},{2,3},{3,2},{4,5},{5,4},{6,7},{7,6},{8,9},{9,8},{10,11... | collective-permute-start | bytes 3538952 | tf_op jit(solution)/shard_map/ppermute | solution.py:264
  (114 other events, 1043.1 us)

commit v3 on v2

--- a/solution.py
+++ b/solution.py
@@ -15,7 +15,8 @@
 SPLIT = (4, 2, 2, 2, 2)
 PARTS = ((0,), (1, 2), (3, 4))
 BACK = 2
-VMEM_LIMIT = 56 * 1024 * 1024
+VMEM_LIMIT = 16 * 1024 * 1024
+PACK_LIMIT = 56 * 1024 * 1024
 
 
 def wave_squared(modes, length):
@@ -83,7 +84,7 @@
             out_specs=[spec, spec],
         ),
         out_shape=[shape, shape],
-        compiler_params=pltpu.CompilerParams(vmem_limit_bytes=VMEM_LIMIT),
+        compiler_params=pltpu.CompilerParams(vmem_limit_bytes=PACK_LIMIT),
         name="pack",
     )(scalars, stored, stored)
 
@@ -413,18 +414,22 @@
     got0 = over_core(give0)
     keep1, give1 = forward(near1, far1, first1, 0, second1, 0, flag, lower, upper, to_modes)
     near4, far3, second2, first3, got0, keep1, give1 = sync(near4, far3, second2, first3, got0, keep1, give1)
-    near4 = jnp.stack(near4)
-    far4 = over_x(near4)
+    cut = SPLIT[4] // 2
+    near4 = [jnp.stack([piece[at : at + cut] for piece in near4]) for at in (0, cut)]
+    far4 = [over_x(near4[0])]
+    far4.append(over_x(near4[1]))
     second3 = over_y(first3)
     got1 = over_core(give1)
     keep2, give2 = forward(near2, far2, first1, SPLIT[1], second1, SPLIT[1], flag, lower, upper, to_modes)
     got2 = over_core(give2)
     keep3, give3 = forward(near3, far3, first2, 0, second2, 0, flag, lower, upper, to_modes)
     got3 = over_core(give3)
-    keep4, give4 = forward(near4, far4, first3, 0, second3, 0, flag, lower, upper, to_modes)
+    keep4, give4 = forward(near4[0], far4[0], first3, 0, second3, 0, flag, lower, upper, to_modes)
     got4 = over_core(give4)
-
-    spectra = [keep0, keep1, keep2, keep3, keep4, got0, got1, got2, got3, got4]
+    keep5, give5 = forward(near4[1], far4[1], first3, cut, second3, cut, flag, lower, upper, to_modes)
+    got5 = over_core(give5)
+
+    spectra = [keep0, keep1, keep2, keep3, keep4, keep5, got0, got1, got2, got3, got4, got5]
     filtered = middle(spectra, kernel, forth, back)
 
     orbit = [
@@ -434,18 +439,20 @@
         (first2, 0, second2, 0),
         (first3, 0, second3, 0),
     ]
-    back_got = [over_core(values) for values in filtered[chunks:]]
-    queue = [(j, skip) for j in range(chunks) for skip in range(0, SPLIT[j], BACK)]
-    queue.reverse()
+    back_got = [over_core(values) for values in filtered[chunks + 1 :]]
+    queue = [(j, skip, BACK) for j in range(chunks - 1) for skip in range(0, SPLIT[j], BACK)]
+    queue = [(chunks, 0, cut), (chunks - 1, 0, cut)] + queue[::-1]
+    orbit.append((first3, cut, second3, cut))
+    starts.append(starts[-1] + cut)
     result, home, sums = None, None, None
     for turn in range(len(queue) + 2):
         near = far = got = pieces = None
         if turn < len(queue):
-            j, skip = queue[turn]
+            j, skip, count = queue[turn]
             first, at, second, there = orbit[j]
             orbitals = first, at + skip, second, there + skip
             near, far = inverse(
-                filtered[j], back_got[j], skip, BACK, *orbitals, flag, lower_back, upper_back, to_planes
+                filtered[j], back_got[j], skip, count, *orbitals, flag, lower_back, upper_back, to_planes
             )
         if turn:
             near, far, sums, home, result = sync(near, far, sums, home, result)
@@ -455,12 +462,12 @@
             pieces = [sums[0][d] + sums[1][d] for d in range(layers)]
             pieces = [over_z(piece, d) if d else piece for d, piece in enumerate(pieces)]
         if home is not None:
-            j, skip = queue[turn - 2]
+            j, skip, count = queue[turn - 2]
             kept, sent = jnp.stack(home[:picks]), jnp.stack(home[picks:])
             own = jnp.where(here, kept, sent)
             other = over_core(jnp.where(here, sent, kept))
             index = jnp.arange(picks, dtype=jnp.int32) ^ first_bit
-            place = jnp.concatenate([index, row_blocks(starts[j] + skip, BACK)])
+            place = jnp.concatenate([index, row_blocks(starts[j] + skip, count)])
             result = unpack(own, other, place, (picks,) + bands.shape[1:], result)
         sums = None if far is None else (near, got)
         home = pieces

time: 632 us -> 602 us (0.953)
  the two profiles are of different devices: /device:TPU:9 before, /device:TPU:0 now
where the time goes in v3:
time: 602 us; the launch traced here: 592 us
  waiting for transfers between devices  269 us (45%)
  Pallas kernels  126 us (21%)
  starting transfers between devices  92.6 us (15%)
  local copies, waits for them, and re-layouts  51.8 us (9%)
  other arithmetic  50.1 us (8%)
    ppermute x83, waiting for transfers between devices, swap(): return lax.ppermute(values, axis, [(i, flip(i)) for i in range(size)])  269 us
    ppermute x83, starting transfers between devices, swap(): return lax.ppermute(values, axis, [(i, flip(i)) for i in range(size)])  92.6 us
    pallas_call x7, Pallas kernels, inverse(): pl.pallas_call(inverse_body, grid_spec=pltpu.PrefetchScalarGridSpec(num_s...  33.2 us
    pallas_call x6, Pallas kernels, forward(): pl.pallas_call(forward_body, grid_spec=pltpu.PrefetchScalarGridSpec(num_s...  32.2 us
    unnamed x142, local copies, waits for them, and re-layouts  31.8 us
    pallas_call x4, Pallas kernels, pack(): pl.pallas_call(pack_body, grid_spec=pltpu.PrefetchScalarGridSpec(num_scal...  22.2 us
    pallas_call x1, Pallas kernels, middle(): pl.pallas_call(lambda *refs: middle_body(count, *refs), grid=(deep // blo...  20.3 us
    pallas_call x7, Pallas kernels, unpack(): pl.pallas_call(unpack_body, grid_spec=pltpu.PrefetchScalarGridSpec(num_sc...  18.1 us
  transfers between devices with their start and end apart: 83, of which 28 were waited for; matrix products, arithmetic and copies ran while one was open for 11% of the time, Pallas kernels for 16%

profile of v3, /device:TPU:0, one launch (start us, length us, event | category | flops | bytes accessed | tf_op | source)
XLA Modules:
  0.0 592.4 jit_solution(325727047995270837)
XLA Ops:
  17.0 6.4 %pack.6 = (f32[2,8,3,4,24,128]{5,4,3,2,1,0:T(8,128)}, f32[2,8,3,4,24,128]{5,4,3,2,1,0:T(8,128)}) custom-call(s32[4]{0:T(128)} %get-tuple-element.209.scalars, f32[4,24,192,192]{3,2,1,0:T(8,128)} %give_ref.6, f32[4,24,192,192]{3,2,1,0:T(8,128)} %give_ref.6), custom_call_target="tpu_custom_call" | custom-call | tf_op jit(solution)/shard_map/pack/pallas_call | solution.py:75
  23.6 8.3 %pack.7 = (f32[2,8,3,4,24,128]{5,4,3,2,1,0:T(8,128)}, f32[2,8,3,4,24,128]{5,4,3,2,1,0:T(8,128)}) custom-call(s32[4]{0:T(128)} %get-tuple-element.211.scalars, f32[2,24,192,192]{3,2,1,0:T(8,128)} %give_ref.7, f32[2,24,192,192]{3,2,1,0:T(8,128)} %give_ref.7), custom_call_target="tpu_custom_call" | custom-call | tf_op jit(solution)/shard_map/pack/pallas_call | solution.py:75
  45.2 7.2 %collective-permute-done.3 = f32[4,3,4,24,128]{4,3,2,1,0:T(8,128)} collective-permute-done((f32[4,3,4,24,128]{4,3,2,1,0:T(8,128)}, f32[4,3,4,24,128]{4,3,2,1,0:T(8,128)}, u32[]{:S(2)}, u32[]{:S(2)}) %collective-permute-start.3) | collective-permute-done | bytes 589856 | tf_op jit(solution)/shard_map/ppermute | solution.py:265
  63.1 9.2 %collective-permute-done.4 = f32[4,3,4,24,128]{4,3,2,1,0:T(8,128)S(1)} collective-permute-done((f32[4,3,4,24,128]{4,3,2,1,0:T(8,128)S(1)}, f32[4,3,4,24,128]{4,3,2,1,0:T(8,128)S(1)}, u32[]{:S(2)}, u32[]{:S(2)}) %collective-permute-start.4) | collective-permute-done | bytes 589856 | tf_op jit(solution)/shard_map/ppermute | solution.py:265
  75.8 11.6 %collective-permute-done.9 = f32[8,3,4,24,128]{4,3,2,1,0:T(8,128)S(1)} collective-permute-done((f32[8,3,4,24,128]{4,3,2,1,0:T(8,128)S(1)}, f32[8,3,4,24,128]{4,3,2,1,0:T(8,128)S(1)}, u32[]{:S(2)}, u32[]{:S(2)}) %collective-permute-start.9) | collective-permute-done | bytes 1179680 | tf_op jit(solution)/shard_map/ppermute | solution.py:265
  107.0 38.4 %collective-permute-done.12 = f32[6,3,4,24,128]{4,3,2,1,0:T(8,128)S(1)} collective-permute-done((f32[6,3,4,24,128]{4,3,2,1,0:T(8,128)}, f32[6,3,4,24,128]{4,3,2,1,0:T(8,128)S(1)}, u32[]{:S(2)}, u32[]{:S(2)}) %collective-permute-start.12) | collective-permute-done | bytes 884768 | tf_op jit(solution)/shard_map/ppermute | solution.py:265
  149.4 18.6 %collective-permute-done.14 = f32[4,3,4,24,128]{4,3,2,1,0:T(8,128)S(1)} collective-permute-done((f32[4,3,4,24,128]{4,3,2,1,0:T(8,128)S(1)}, f32[4,3,4,24,128]{4,3,2,1,0:T(8,128)S(1)}, u32[]{:S(2)}, u32[]{:S(2)}) %collective-permute-start.14) | collective-permute-done | bytes 589856 | tf_op jit(solution)/shard_map/ppermute | solution.py:265
  179.3 20.0 %collective-permute-done.16 = f32[6,3,4,24,128]{4,3,2,1,0:T(8,128)} collective-permute-done((f32[6,3,4,24,128]{4,3,2,1,0:T(8,128)}, f32[6,3,4,24,128]{4,3,2,1,0:T(8,128)}, u32[]{:S(2)}, u32[]{:S(2)}) %collective-permute-start.16) | collective-permute-done | bytes 884768 | tf_op jit(solution)/shard_map/ppermute | solution.py:265
  202.9 9.6 %fusion.1.refs_0_ = f32[96,192,192]{2,1,0:T(8,128)} fusion(f32[192]{0:T(256)S(1)} %fusion.52, f32[96,192]{1,0:T(8,128)S(1)} %broadcast_add_fusion), kind=kLoop, calls=%fused_computation.6 | loop fusion | flops 35389440 | bytes 14230272 | tf_op jit(solution)/shard_map/div | solution.py:385
  212.5 5.0 sine_add_fusion
  228.5 23.3 %collective-permute-done.23 = f32[6,3,4,24,128]{4,3,2,1,0:T(8,128)S(1)} collective-permute-done((f32[6,3,4,24,128]{4,3,2,1,0:T(8,128)S(1)}, f32[6,3,4,24,128]{4,3,2,1,0:T(8,128)S(1)}, u32[]{:S(2)}, u32[]{:S(2)}) %collective-permute-start.23) | collective-permute-done | bytes 884768 | tf_op jit(solution)/shard_map/ppermute | solution.py:265
  261.5 10.7 %forward.6 = (f32[96,32,192]{2,1,0:T(8,128)S(1)}, f32[96,32,192]{2,1,0:T(8,128)S(1)}) custom-call(s32[1]{0:T(128)} %bitcast.2.scalars, f32[4,4,3,4,24,128]{5,4,3,2,1,0:T(8,128)S(1)} %copy-done.15, f32[4,4,3,4,24,128]{5,4,3,2,1,0:T(8,128)} %collective-permute-done.15.far, f32[4,4,3,4,24,128]{5,4,3,2,1,0:T(8,128)S(1)} %copy-done.3, ...), custom_call_target="tpu_custom_call" | custom-call | tf_op jit(solution)/shard_map/forward/pallas_call | solution.py:163
  285.2 12.3 %collective-permute-done.28 = f32[2,3,4,24,128]{4,3,2,1,0:T(8,128)S(1)} collective-permute-done((f32[2,3,4,24,128]{4,3,2,1,0:T(8,128)S(1)}, f32[2,3,4,24,128]{4,3,2,1,0:T(8,128)S(1)}, u32[]{:S(2)}, u32[]{:S(2)}) %collective-permute-start.28) | collective-permute-done | bytes 294944 | tf_op jit(solution)/shard_map/ppermute | solution.py:265
  299.0 5.8 forward.7
  312.7 6.0 %forward.8 = (f32[96,16,192]{2,1,0:T(8,128)S(1)}, f32[96,16,192]{2,1,0:T(8,128)S(1)}) custom-call(s32[1]{0:T(128)} %bitcast.2.scalars, f32[4,2,3,4,24,128]{5,4,3,2,1,0:T(8,128)} %pad_maximum_fusion.4.near, f32[4,2,3,4,24,128]{5,4,3,2,1,0:T(8,128)} %collective-permute-done.27.far, f32[4,4,3,4,24,128]{5,4,3,2,1,0:T(8,128)S(1)} %pad_maximum_fusion.2.first, ...), custom_call_target="tpu_custom_call" | custom-call | tf_op jit(solution)/shard_map/forward/pallas_call | solution.py:163
  321.6 5.3 forward.9
  328.5 10.3 %collective-permute-done.35.second = f32[4,2,3,4,24,128]{5,4,3,2,1,0:T(8,128)S(1)} collective-permute-done((f32[4,2,3,4,24,128]{5,4,3,2,1,0:T(8,128)S(1)}, f32[4,2,3,4,24,128]{5,4,3,2,1,0:T(8,128)S(1)}, u32[]{:S(2)}, u32[]{:S(2)}) %collective-permute-start.35) | collective-permute-done | bytes 1179680 | tf_op jit(solution)/shard_map/ppermute | solution.py:265
  350.4 20.3 %middle.1 = (f32[96,32,192]{2,1,0:T(8,128)S(1)}, f32[96,16,192]{2,1,0:T(8,128)S(1)}, f32[96,16,192]{2,1,0:T(8,128)S(1)}, f32[96,16,192]{2,1,0:T(8,128)S(1)}, f32...) custom-call(f32[96,192,192]{2,1,0:T(8,128)} %fusion.1.refs_0_, ...), custom_call_target="tpu_custom_call" | custom-call | tf_op jit(solution)/shard_map/middle/pallas_call | solution.py:197
  380.8 12.3 %collective-permute-done.48 = f32[4,1,3,4,24,128]{5,4,3,2,1,0:T(8,128)S(1)} collective-permute-done((f32[4,1,3,4,24,128]{5,4,3,2,1,0:T(8,128)S(1)}, f32[4,1,3,4,24,128]{5,4,3,2,1,0:T(8,128)S(1)}, u32[]{:S(2)}, u32[]{:S(2)}) %collective-permute-start.48) | collective-permute-done | bytes 589856 | tf_op jit(solution)/shard_map/ppermute | solution.py:265
  398.7 5.6 inverse.11
  404.3 7.0 %collective-permute-done.51 = f32[1,3,4,24,128]{4,3,2,1,0:T(8,128)S(1)} collective-permute-done((f32[1,3,4,24,128]{4,3,2,1,0:T(8,128)S(1)}, f32[1,3,4,24,128]{4,3,2,1,0:T(8,128)S(1)}, u32[]{:S(2)}, u32[]{:S(2)}) %collective-permute-start.51) | collective-permute-done | bytes 147488 | tf_op jit(solution)/shard_map/ppermute | solution.py:265
  428.3 5.6 inverse.10
  448.3 5.7 inverse.9
  456.2 14.9 %collective-permute-done.60 = f32[2,3,4,24,128]{4,3,2,1,0:T(8,128)S(1)} collective-permute-done((f32[2,3,4,24,128]{4,3,2,1,0:T(8,128)S(1)}, f32[2,3,4,24,128]{4,3,2,1,0:T(8,128)S(1)}, u32[]{:S(2)}, u32[]{:S(2)}) %collective-permute-start.60) | collective-permute-done | bytes 294944 | tf_op jit(solution)/shard_map/ppermute | solution.py:265
  476.5 6.3 %inverse.8 = (f32[4,2,3,4,24,128]{5,4,3,2,1,0:T(8,128)S(1)}, f32[4,2,3,4,24,128]{5,4,3,2,1,0:T(8,128)}) custom-call(s32[1]{0:T(128)} %bitcast.2.scalars, f32[96,32,192]{2,1,0:T(8,128)S(1)} %copy-done.10, f32[96,32,192]{2,1,0:T(8,128)} %collective-permute-done.42.got_ref, f32[4,4,3,4,24,128]{5,4,3,2,1,0:T(8,128)S(1)} %copy-done.4, ...), custom_call_target="tpu_custom_call" | custom-call | tf_op jit(solution)/shard_map/inverse/pallas_call | solution.py:235
  485.3 13.2 %collective-permute-done.65 = f32[2,3,4,24,128]{4,3,2,1,0:T(8,128)S(1)} collective-permute-done((f32[2,3,4,24,128]{4,3,2,1,0:T(8,128)S(1)}, f32[2,3,4,24,128]{4,3,2,1,0:T(8,128)S(1)}, u32[]{:S(2)}, u32[]{:S(2)}) %collective-permute-start.65) | collective-permute-done | bytes 294944 | tf_op jit(solution)/shard_map/ppermute | solution.py:265
  510.2 5.7 inverse.7
  519.8 10.0 %collective-permute-done.70 = f32[2,3,4,24,128]{4,3,2,1,0:T(8,128)} collective-permute-done((f32[2,3,4,24,128]{4,3,2,1,0:T(8,128)}, f32[2,3,4,24,128]{4,3,2,1,0:T(8,128)}, u32[]{:S(2)}, u32[]{:S(2)}) %collective-permute-start.70) | collective-permute-done | bytes 294944 | tf_op jit(solution)/shard_map/ppermute | solution.py:265
  540.2 4.9 collective-permute-done.76
  545.1 14.6 %collective-permute-done.75 = f32[2,3,4,24,128]{4,3,2,1,0:T(8,128)S(1)} collective-permute-done((f32[2,3,4,24,128]{4,3,2,1,0:T(8,128)S(1)}, f32[2,3,4,24,128]{4,3,2,1,0:T(8,128)S(1)}, u32[]{:S(2)}, u32[]{:S(2)}) %collective-permute-start.75) | collective-permute-done | bytes 294944 | tf_op jit(solution)/shard_map/ppermute | solution.py:265
  567.0 4.9 collective-permute-done.80
  571.9 15.6 %collective-permute-done.79 = f32[2,3,4,24,128]{4,3,2,1,0:T(8,128)S(1)} collective-permute-done((f32[2,3,4,24,128]{4,3,2,1,0:T(8,128)S(1)}, f32[2,3,4,24,128]{4,3,2,1,0:T(8,128)S(1)}, u32[]{:S(2)}, u32[]{:S(2)}) %collective-permute-start.79) | collective-permute-done | bytes 294944 | tf_op jit(solution)/shard_map/ppermute | solution.py:265
  (405 shorter events, 235.3 us)
Async XLA Ops:
  23.4 34.3 %collective-permute-start.8 = (f32[2,8,3,4,24,128]{5,4,3,2,1,0:T(8,128)}, f32[2,8,3,4,24,128]{5,4,3,2,1,0:T(8,128)}, u32[]{:S(2)}, u32[]{:S(2)}) collective-permute-start(f32[2,8,3,4,24,128]{5,4,3,2,1,0:T(8,128)} %get-tuple-element.215), channel_id=1, source_target_pairs={{0,8},{8,0},{16,24},{24,16},{1,9},{9,1},{17,25},{25,17},{2,10},{10... | collective-permute-start | bytes 7077896 | tf_op jit(solution)/shard_map/ppermute | solution.py:265
  31.9 28.5 %collective-permute-start.1 = (f32[2,8,3,4,24,128]{5,4,3,2,1,0:T(8,128)}, f32[2,8,3,4,24,128]{5,4,3,2,1,0:T(8,128)S(1)}, u32[]{:S(2)}, u32[]{:S(2)}) collective-permute-start(f32[2,8,3,4,24,128]{5,4,3,2,1,0:T(8,128)} %get-tuple-element.213), channel_id=1, source_target_pairs={{0,8},{8,0},{16,24},{24,16},{1,9},{9,1},{17,25},{25,17},{2,10},{10... | collective-permute-start | bytes 7077896 | tf_op jit(solution)/shard_map/ppermute | solution.py:265
  39.1 51.3 %collective-permute-start.5 = (f32[4,3,4,24,128]{4,3,2,1,0:T(8,128)}, f32[4,3,4,24,128]{4,3,2,1,0:T(8,128)S(1)}, u32[]{:S(2)}, u32[]{:S(2)}) collective-permute-start(f32[4,3,4,24,128]{4,3,2,1,0:T(8,128)} %get-tuple-element.204), channel_id=1, source_target_pairs={{0,2},{1,3},{2,0},{3,1},{4,6},{5,7},{6,4},{7,5},{8,10},{9,11},{10,... | collective-permute-start | bytes 1769480 | tf_op jit(solution)/shard_map/ppermute | solution.py:265
  40.7 49.6 %collective-permute-start.6 = (f32[4,3,4,24,128]{4,3,2,1,0:T(8,128)}, f32[4,3,4,24,128]{4,3,2,1,0:T(8,128)S(1)}, u32[]{:S(2)}, u32[]{:S(2)}) collective-permute-start(f32[4,3,4,24,128]{4,3,2,1,0:T(8,128)} %get-tuple-element.205), channel_id=1, source_target_pairs={{0,4},{1,5},{2,6},{3,7},{4,0},{5,1},{6,2},{7,3},{8,12},{9,13},{10,... | collective-permute-start | bytes 1769480 | tf_op jit(solution)/shard_map/ppermute | solution.py:265
  52.4 37.9 %collective-permute-start.7 = (f32[4,3,4,24,128]{4,3,2,1,0:T(8,128)S(1)}, f32[4,3,4,24,128]{4,3,2,1,0:T(8,128)S(1)}, u32[]{:S(2)}, u32[]{:S(2)}) collective-permute-start(f32[4,3,4,24,128]{4,3,2,1,0:T(8,128)S(1)} %copy-done.62), channel_id=1, source_target_pairs={{0,6},{1,7},{2,4},{3,5},{4,2},{5,3},{6,0},{7,1},{8,14},{9,15},{10,... | collective-permute-start | bytes 1769480 | tf_op jit(solution)/shard_map/ppermute | solution.py:265
  60.4 26.9 %collective-permute-start.9 = (f32[8,3,4,24,128]{4,3,2,1,0:T(8,128)S(1)}, f32[8,3,4,24,128]{4,3,2,1,0:T(8,128)S(1)}, u32[]{:S(2)}, u32[]{:S(2)}) collective-permute-start(f32[8,3,4,24,128]{4,3,2,1,0:T(8,128)S(1)} %fusion.7), channel_id=1, source_target_pairs={{0,1},{1,0},{2,3},{3,2},{4,5},{5,4},{6,7},{7,6},{8,9},{9,8},{10,11... | collective-permute-start | bytes 3538952 | tf_op jit(solution)/shard_map/ppermute | solution.py:265
  90.6 77.4 %collective-permute-start.15 = (f32[4,4,3,4,24,128]{5,4,3,2,1,0:T(8,128)S(1)}, f32[4,4,3,4,24,128]{5,4,3,2,1,0:T(8,128)}, u32[]{:S(2)}, u32[]{:S(2)}) collective-permute-start(f32[4,4,3,4,24,128]{5,4,3,2,1,0:T(8,128)S(1)} %pad_maximum_fusion.near), channel_id=1, source_target_pairs={{0,1},{1,0},{2,3},{3,2},{4,5},{5,4},{6,7},{7,6},{8,9},{9,8},{10,11... | collective-permute-start | bytes 7077896 | tf_op jit(solution)/shard_map/ppermute | solution.py:265
  92.4 53.1 %collective-permute-start.11 = (f32[6,3,4,24,128]{4,3,2,1,0:T(8,128)}, f32[6,3,4,24,128]{4,3,2,1,0:T(8,128)S(1)}, u32[]{:S(2)}, u32[]{:S(2)}) collective-permute-start(f32[6,3,4,24,128]{4,3,2,1,0:T(8,128)} %get-tuple-element.221), channel_id=1, source_target_pairs={{0,2},{1,3},{2,0},{3,1},{4,6},{5,7},{6,4},{7,5},{8,10},{9,11},{10,... | collective-permute-start | bytes 2654216 | tf_op jit(solution)/shard_map/ppermute | solution.py:265
  96.3 49.0 %collective-permute-start.12 = (f32[6,3,4,24,128]{4,3,2,1,0:T(8,128)}, f32[6,3,4,24,128]{4,3,2,1,0:T(8,128)S(1)}, u32[]{:S(2)}, u32[]{:S(2)}) collective-permute-start(f32[6,3,4,24,128]{4,3,2,1,0:T(8,128)} %get-tuple-element.222), channel_id=1, source_target_pairs={{0,4},{1,5},{2,6},{3,7},{4,0},{5,1},{6,2},{7,3},{8,12},{9,13},{10,... | collective-permute-start | bytes 2654216 | tf_op jit(solution)/shard_map/ppermute | solution.py:265
  97.3 49.7 %collective-permute-start.10 = (f32[8,3,4,24,128]{4,3,2,1,0:T(8,128)}, f32[8,3,4,24,128]{4,3,2,1,0:T(8,128)S(1)}, u32[]{:S(2)}, u32[]{:S(2)}) collective-permute-start(f32[8,3,4,24,128]{4,3,2,1,0:T(8,128)} %get-tuple-element.219), channel_id=1, source_target_pairs={{0,16},{8,24},{16,0},{24,8},{1,17},{9,25},{17,1},{25,9},{2,18},{10... | collective-permute-start | bytes 3538952 | tf_op jit(solution)/shard_map/ppermute | solution.py:265
  102.8 46.6 %collective-permute-start.13 = (f32[2,3,4,24,128]{4,3,2,1,0:T(8,128)}, f32[2,3,4,24,128]{4,3,2,1,0:T(8,128)S(1)}, u32[]{:S(2)}, u32[]{:S(2)}) collective-permute-start(f32[2,3,4,24,128]{4,3,2,1,0:T(8,128)} %get-tuple-element.223), channel_id=1, source_target_pairs={{0,6},{1,7},{2,4},{3,5},{4,2},{5,3},{6,0},{7,1},{8,14},{9,15},{10,... | collective-permute-start | bytes 884744 | tf_op jit(solution)/shard_map/ppermute | solution.py:265
  168.8 30.5 %collective-permute-start.16 = (f32[6,3,4,24,128]{4,3,2,1,0:T(8,128)}, f32[6,3,4,24,128]{4,3,2,1,0:T(8,128)}, u32[]{:S(2)}, u32[]{:S(2)}) collective-permute-start(f32[6,3,4,24,128]{4,3,2,1,0:T(8,128)} %get-tuple-element.231), channel_id=1, source_target_pairs={{0,2},{1,3},{2,0},{3,1},{4,6},{5,7},{6,4},{7,5},{8,10},{9,11},{10,... | collective-permute-start | bytes 2654216 | tf_op jit(solution)/shard_map/ppermute | solution.py:265
  168.8 31.5 %collective-permute-start.17 = (f32[6,3,4,24,128]{4,3,2,1,0:T(8,128)}, f32[6,3,4,24,128]{4,3,2,1,0:T(8,128)}, u32[]{:S(2)}, u32[]{:S(2)}) collective-permute-start(f32[6,3,4,24,128]{4,3,2,1,0:T(8,128)} %get-tuple-element.232), channel_id=1, source_target_pairs={{0,4},{1,5},{2,6},{3,7},{4,0},{5,1},{6,2},{7,3},{8,12},{9,13},{10,... | collective-permute-start | bytes 2654216 | tf_op jit(solution)/shard_map/ppermute | solution.py:265
  171.7 48.2 %collective-permute-start.18 = (f32[2,3,4,24,128]{4,3,2,1,0:T(8,128)}, f32[2,3,4,24,128]{4,3,2,1,0:T(8,128)S(1)}, u32[]{:S(2)}, u32[]{:S(2)}) collective-permute-start(f32[2,3,4,24,128]{4,3,2,1,0:T(8,128)} %get-tuple-element.233), channel_id=1, source_target_pairs={{0,6},{1,7},{2,4},{3,5},{4,2},{5,3},{6,0},{7,1},{8,14},{9,15},{10,... | collective-permute-start | bytes 884744 | tf_op jit(solution)/shard_map/ppermute | solution.py:265
  174.9 45.0 %collective-permute-start.20 = (f32[4,2,3,4,24,128]{5,4,3,2,1,0:T(8,128)S(1)}, f32[4,2,3,4,24,128]{5,4,3,2,1,0:T(8,128)S(1)}, u32[]{:S(2)}, u32[]{:S(2)}) collective-permute-start(f32[4,2,3,4,24,128]{5,4,3,2,1,0:T(8,128)S(1)} %pad_maximum_fusion.3.near), channel_id=1, source_target_pairs={{0,1},{1,0},{2,3},{3,2},{4,5},{5,4},{6,7},{7,6},{8,9},{9,8},{10,11... | collective-permute-start | bytes 3538952 | tf_op jit(solution)/shard_map/ppermute | solution.py:265
  176.7 43.2 %collective-permute-start.21 = (f32[4,4,3,4,24,128]{5,4,3,2,1,0:T(8,128)S(1)}, f32[4,4,3,4,24,128]{5,4,3,2,1,0:T(8,128)S(1)}, u32[]{:S(2)}, u32[]{:S(2)}) collective-permute-start(f32[4,4,3,4,24,128]{5,4,3,2,1,0:T(8,128)S(1)} %pad_maximum_fusion.1.first), channel_id=1, source_target_pairs={{0,16},{8,24},{16,0},{24,8},{1,17},{9,25},{17,1},{25,9},{2,18},{10... | collective-permute-start | bytes 7077896 | tf_op jit(solution)/shard_map/ppermute | solution.py:265
  221.8 54.3 %collective-permute-start.26 = (f32[4,4,3,4,24,128]{5,4,3,2,1,0:T(8,128)S(1)}, f32[4,4,3,4,24,128]{5,4,3,2,1,0:T(8,128)}, u32[]{:S(2)}, u32[]{:S(2)}) collective-permute-start(f32[4,4,3,4,24,128]{5,4,3,2,1,0:T(8,128)S(1)} %pad_maximum_fusion.2.first), channel_id=1, source_target_pairs={{0,16},{8,24},{16,0},{24,8},{1,17},{9,25},{17,1},{25,9},{2,18},{10... | collective-permute-start | bytes 7077896 | tf_op jit(solution)/shard_map/ppermute | solution.py:265
  223.2 28.7 %collective-permute-start.23 = (f32[6,3,4,24,128]{4,3,2,1,0:T(8,128)S(1)}, f32[6,3,4,24,128]{4,3,2,1,0:T(8,128)S(1)}, u32[]{:S(2)}, u32[]{:S(2)}) collective-permute-start(f32[6,3,4,24,128]{4,3,2,1,0:T(8,128)S(1)} %get-tuple-element.253), channel_id=1, source_target_pairs={{0,4},{1,5},{2,6},{3,7},{4,0},{5,1},{6,2},{7,3},{8,12},{9,13},{10,... | collective-permute-start | bytes 2654216 | tf_op jit(solution)/shard_map/ppermute | solution.py:265
  225.7 50.4 %collective-permute-start.27 = (f32[4,2,3,4,24,128]{5,4,3,2,1,0:T(8,128)}, f32[4,2,3,4,24,128]{5,4,3,2,1,0:T(8,128)}, u32[]{:S(2)}, u32[]{:S(2)}) collective-permute-start(f32[4,2,3,4,24,128]{5,4,3,2,1,0:T(8,128)} %pad_maximum_fusion.4.near), channel_id=1, source_target_pairs={{0,1},{1,0},{2,3},{3,2},{4,5},{5,4},{6,7},{7,6},{8,9},{9,8},{10,11... | collective-permute-start | bytes 3538952 | tf_op jit(solution)/shard_map/ppermute | solution.py:265
  228.5 45.4 %collective-permute-start.22 = (f32[6,3,4,24,128]{4,3,2,1,0:T(8,128)}, f32[6,3,4,24,128]{4,3,2,1,0:T(8,128)}, u32[]{:S(2)}, u32[]{:S(2)}) collective-permute-start(f32[6,3,4,24,128]{4,3,2,1,0:T(8,128)} %get-tuple-element.252), channel_id=1, source_target_pairs={{0,2},{1,3},{2,0},{3,1},{4,6},{5,7},{6,4},{7,5},{8,10},{9,11},{10,... | collective-permute-start | bytes 2654216 | tf_op jit(solution)/shard_map/ppermute | solution.py:265
  276.1 33.5 %collective-permute-start.33 = (f32[96,32,192]{2,1,0:T(8,128)S(1)}, f32[96,32,192]{2,1,0:T(8,128)S(1)}, u32[]{:S(2)}, u32[]{:S(2)}) collective-permute-start(f32[96,32,192]{2,1,0:T(8,128)S(1)} %get-tuple-element.284), channel_id=1, source_target_pairs={{0,8},{8,0},{16,24},{24,16},{1,9},{9,1},{17,25},{25,17},{2,10},{10... | collective-permute-start | bytes 7077896 | tf_op jit(solution)/shard_map/ppermute | solution.py:265
  277.4 30.3 %collective-permute-start.31 = (f32[4,2,3,4,24,128]{5,4,3,2,1,0:T(8,128)S(1)}, f32[4,2,3,4,24,128]{5,4,3,2,1,0:T(8,128)S(1)}, u32[]{:S(2)}, u32[]{:S(2)}) collective-permute-start(f32[4,2,3,4,24,128]{5,4,3,2,1,0:T(8,128)S(1)} %pad_maximum_fusion.5.near), channel_id=1, source_target_pairs={{0,1},{1,0},{2,3},{3,2},{4,5},{5,4},{6,7},{7,6},{8,9},{9,8},{10,11... | collective-permute-start | bytes 3538952 | tf_op jit(solution)/shard_map/ppermute | solution.py:265
  281.5 28.1 %collective-permute-start.32 = (f32[4,2,3,4,24,128]{5,4,3,2,1,0:T(8,128)S(1)}, f32[4,2,3,4,24,128]{5,4,3,2,1,0:T(8,128)S(1)}, u32[]{:S(2)}, u32[]{:S(2)}) collective-permute-start(f32[4,2,3,4,24,128]{5,4,3,2,1,0:T(8,128)S(1)} %pad_maximum_fusion.6.first), channel_id=1, source_target_pairs={{0,16},{8,24},{16,0},{24,8},{1,17},{9,25},{17,1},{25,9},{2,18},{10... | collective-permute-start | bytes 3538952 | tf_op jit(solution)/shard_map/ppermute | solution.py:265
  311.4 27.3 %collective-permute-start.35 = (f32[4,2,3,4,24,128]{5,4,3,2,1,0:T(8,128)S(1)}, f32[4,2,3,4,24,128]{5,4,3,2,1,0:T(8,128)S(1)}, u32[]{:S(2)}, u32[]{:S(2)}) collective-permute-start(f32[4,2,3,4,24,128]{5,4,3,2,1,0:T(8,128)S(1)} %pad_maximum_fusion.7.first), channel_id=1, source_target_pairs={{0,16},{8,24},{16,0},{24,8},{1,17},{9,25},{17,1},{25,9},{2,18},{10... | collective-permute-start | bytes 3538952 | tf_op jit(solution)/shard_map/ppermute | solution.py:265
  373.3 25.4 %collective-permute-start.45 = (f32[96,16,192]{2,1,0:T(8,128)S(1)}, f32[96,16,192]{2,1,0:T(8,128)S(1)}, u32[]{:S(2)}, u32[]{:S(2)}) collective-permute-start(f32[96,16,192]{2,1,0:T(8,128)S(1)} %get-tuple-element.326), channel_id=1, source_target_pairs={{0,8},{8,0},{16,24},{24,16},{1,9},{9,1},{17,25},{25,17},{2,10},{10... | collective-permute-start | bytes 3538952 | tf_op jit(solution)/shard_map/ppermute | solution.py:265
  411.3 28.3 %collective-permute-start.53 = (f32[4,2,3,4,24,128]{5,4,3,2,1,0:T(8,128)}, f32[4,2,3,4,24,128]{5,4,3,2,1,0:T(8,128)}, u32[]{:S(2)}, u32[]{:S(2)}) collective-permute-start(f32[4,2,3,4,24,128]{5,4,3,2,1,0:T(8,128)} %get-tuple-element.342), channel_id=1, source_target_pairs={{0,1},{1,0},{2,3},{3,2},{4,5},{5,4},{6,7},{7,6},{8,9},{9,8},{10,11... | collective-permute-start | bytes 3538952 | tf_op jit(solution)/shard_map/ppermute | solution.py:265
  416.0 30.2 %collective-permute-start.43 = (f32[96,16,192]{2,1,0:T(8,128)}, f32[96,16,192]{2,1,0:T(8,128)}, u32[]{:S(2)}, u32[]{:S(2)}) collective-permute-start(f32[96,16,192]{2,1,0:T(8,128)} %get-tuple-element.318), channel_id=1, source_target_pairs={{0,8},{8,0},{16,24},{24,16},{1,9},{9,1},{17,25},{25,17},{2,10},{10... | collective-permute-start | bytes 3538952 | tf_op jit(solution)/shard_map/ppermute | solution.py:265
  417.4 56.1 %collective-permute-start.42 = (f32[96,32,192]{2,1,0:T(8,128)}, f32[96,32,192]{2,1,0:T(8,128)}, u32[]{:S(2)}, u32[]{:S(2)}) collective-permute-start(f32[96,32,192]{2,1,0:T(8,128)} %get-tuple-element.309), channel_id=1, source_target_pairs={{0,8},{8,0},{16,24},{24,16},{1,9},{9,1},{17,25},{25,17},{2,10},{10... | collective-permute-start | bytes 7077896 | tf_op jit(solution)/shard_map/ppermute | solution.py:265
  439.5 31.6 %collective-permute-start.58 = (f32[4,2,3,4,24,128]{5,4,3,2,1,0:T(8,128)S(1)}, f32[4,2,3,4,24,128]{5,4,3,2,1,0:T(8,128)S(1)}, u32[]{:S(2)}, u32[]{:S(2)}) collective-permute-start(f32[4,2,3,4,24,128]{5,4,3,2,1,0:T(8,128)S(1)} %get-tuple-element.350), channel_id=1, source_target_pairs={{0,1},{1,0},{2,3},{3,2},{4,5},{5,4},{6,7},{7,6},{8,9},{9,8},{10,11... | collective-permute-start | bytes 3538952 | tf_op jit(solution)/shard_map/ppermute | solution.py:265
  471.1 27.4 %collective-permute-start.63 = (f32[4,2,3,4,24,128]{5,4,3,2,1,0:T(8,128)S(1)}, f32[4,2,3,4,24,128]{5,4,3,2,1,0:T(8,128)S(1)}, u32[]{:S(2)}, u32[]{:S(2)}) collective-permute-start(f32[4,2,3,4,24,128]{5,4,3,2,1,0:T(8,128)S(1)} %get-tuple-element.359), channel_id=1, source_target_pairs={{0,1},{1,0},{2,3},{3,2},{4,5},{5,4},{6,7},{7,6},{8,9},{9,8},{10,11... | collective-permute-start | bytes 3538952 | tf_op jit(solution)/shard_map/ppermute | solution.py:265
  498.5 31.3 %collective-permute-start.68 = (f32[4,2,3,4,24,128]{5,4,3,2,1,0:T(8,128)}, f32[4,2,3,4,24,128]{5,4,3,2,1,0:T(8,128)}, u32[]{:S(2)}, u32[]{:S(2)}) collective-permute-start(f32[4,2,3,4,24,128]{5,4,3,2,1,0:T(8,128)} %get-tuple-element.368), channel_id=1, source_target_pairs={{0,1},{1,0},{2,3},{3,2},{4,5},{5,4},{6,7},{7,6},{8,9},{9,8},{10,11... | collective-permute-start | bytes 3538952 | tf_op jit(solution)/shard_map/ppermute | solution.py:265
  529.9 29.9 %collective-permute-start.73 = (f32[4,2,3,4,24,128]{5,4,3,2,1,0:T(8,128)S(1)}, f32[4,2,3,4,24,128]{5,4,3,2,1,0:T(8,128)S(1)}, u32[]{:S(2)}, u32[]{:S(2)}) collective-permute-start(f32[4,2,3,4,24,128]{5,4,3,2,1,0:T(8,128)S(1)} %get-tuple-element.377), channel_id=1, source_target_pairs={{0,1},{1,0},{2,3},{3,2},{4,5},{5,4},{6,7},{7,6},{8,9},{9,8},{10,11... | collective-permute-start | bytes 3538952 | tf_op jit(solution)/shard_map/ppermute | solution.py:265
  (124 other events, 1165.7 us)

commit v4 on v3

--- a/solution.py
+++ b/solution.py
@@ -180,7 +180,12 @@
     forth, back = halves(forth_ref[...]), halves(back_ref[...])
     for k in range(kernel_ref.shape[0]):
         rows = jnp.concatenate([r[k] for r in ins], axis=0)
-        spectrum = multiply(forth, halves(rows)) * kernel_ref[k]
+        half, tail = rows.shape[0] // 2, rows.shape[1] - LANES
+        top = kernel_ref[k, :half]
+        first_row = lax.broadcasted_iota(jnp.int32, top.shape, 0) == 0
+        table = jnp.concatenate([top, jnp.where(first_row, kernel_ref[k, half : half + 1], top)], axis=0)
+        table = jnp.concatenate([table, table[:, :tail]], axis=1)
+        spectrum = multiply(forth, halves(rows)) * table
         filtered = multiply(back, halves(spectrum))
         start = 0
         for out in outs:
@@ -197,7 +202,7 @@
     return pl.pallas_call(
         lambda *refs: middle_body(count, *refs),
         grid=(deep // block,),
-        in_specs=[pl.BlockSpec((block, points, points), lambda k: (k, 0, 0)), whole, whole] + parts,
+        in_specs=[pl.BlockSpec((block,) + kernel.shape[1:], lambda k: (k, 0, 0)), whole, whole] + parts,
         out_specs=parts,
         out_shape=[jax.ShapeDtypeStruct(a.shape, jnp.float32) for a in spectra],
         compiler_params=pltpu.CompilerParams(vmem_limit_bytes=VMEM_LIMIT),
@@ -284,7 +289,14 @@
     all_modes = jnp.arange(points, dtype=jnp.int32)
     mode_of = (core_of[:, None] * half_rows + jnp.arange(half_rows, dtype=jnp.int32)).reshape(-1)
 
-    squares = wave_squared(all_modes, points)
+    tail = points - LANES
+    low = jnp.arange(half_rows, dtype=jnp.int32)
+    row_modes = jnp.concatenate([low, jnp.where(low == 0, half_rows, points - low)])
+    near_columns = jnp.arange(tail, dtype=jnp.int32) + 1
+    rest = jnp.arange(LANES - tail, dtype=jnp.int32)
+    column_modes = jnp.concatenate([near_columns, jnp.where(rest == 0, 0, rest + tail), points - near_columns])
+    row_squares = wave_squared(jnp.arange(half_rows + 2 * STEP, dtype=jnp.int32), points)
+    column_squares = wave_squared(column_modes[:LANES], points)
     own_squares = wave_squared(c * half_rows + jnp.arange(half_rows, dtype=jnp.int32), points)
 
     first_bit = z % picks
@@ -378,21 +390,22 @@
     second0 = over_y(first0)
     far1 = over_x(near1)
     ready = choose_targets(3, keep, got, carried2)
-    own_squares, squares, all_modes, mode_of, plane_of = after(
-        (own_squares, squares, all_modes, mode_of, plane_of), near2[1]
+    own_squares, row_squares, column_squares, all_modes, row_modes, column_modes, mode_of, plane_of = after(
+        (own_squares, row_squares, column_squares, all_modes, row_modes, column_modes, mode_of, plane_of), near2[1]
     )
-    kernel = screened(own_squares[:, None, None] + squares[None, :, None] + squares[None, None, :])
+    kernel = screened(own_squares[:, None, None] + row_squares[None, :, None] + column_squares[None, None, :])
     kernel = kernel / float(points * points * points)
-    columns = cas_matrix(all_modes, all_modes, points)
+    columns = cas_matrix(all_modes, column_modes, points)
+    columns_back = cas_matrix(column_modes, all_modes, points)
     empty = jnp.zeros((points - LANES, points), jnp.float32)
     lower = jnp.concatenate([columns, empty], axis=0)
     upper = jnp.concatenate([columns[:LANES], empty, columns[LANES:]], axis=0)
-    lower_back = jnp.concatenate([columns, empty.T], axis=1)
-    upper_back = jnp.concatenate([columns[:, :LANES], empty.T, columns[:, LANES:]], axis=1)
+    lower_back = jnp.concatenate([columns_back, empty.T], axis=1)
+    upper_back = jnp.concatenate([columns_back[:, :LANES], empty.T, columns_back[:, LANES:]], axis=1)
     to_modes = cas_matrix(mode_of, plane_of, points)
     to_planes = cas_matrix(plane_of, mode_of, points)
-    forth = cas_matrix(all_modes, mode_of, points)
-    back = cas_matrix(mode_of, all_modes, points)
+    forth = cas_matrix(row_modes, mode_of, points)
+    back = cas_matrix(mode_of, row_modes, points)
     matrices = lower, upper, lower_back, upper_back, to_modes, to_planes, forth, back
     ready, carried2, near2, first1, far1, second0, kernel, matrices = sync(
         ready, carried2, near2, first1, far1, second0, kernel, matrices

time: 602 us -> 600 us (level)
  waiting for transfers between devices: 269 us -> 287 us
  other arithmetic: 50.1 us -> 36.3 us
    ppermute x83, waiting for transfers between devices: 269 us -> 287 us  [swap(): return lax.ppermute(values, axis, [(i, flip(i)) for i in range(size)])]
    unnamed x142 -> x130, local copies, waits for them, and re-layouts: 31.8 us -> 32.8 us
  transfers between devices with their start and end apart: 83 -> 83, of which waited for: 28 -> 29; matrix products, arithmetic and copies ran while one was open for 11% -> 8% of each run, Pallas kernels for 16% -> 16%
where the time goes in v4:
time: 600 us; the launch traced here: 590 us
  waiting for transfers between devices  287 us (48%)
  Pallas kernels  124 us (21%)
  starting transfers between devices  92.7 us (15%)
  local copies, waits for them, and re-layouts  46.9 us (8%)
  other arithmetic  36.3 us (6%)
    ppermute x83, waiting for transfers between devices, swap(): return lax.ppermute(values, axis, [(i, flip(i)) for i in range(size)])  287 us
    ppermute x83, starting transfers between devices, swap(): return lax.ppermute(values, axis, [(i, flip(i)) for i in range(size)])  92.7 us
    pallas_call x7, Pallas kernels, inverse(): pl.pallas_call(inverse_body, grid_spec=pltpu.PrefetchScalarGridSpec(num_s...  33.1 us
    unnamed x130, local copies, waits for them, and re-layouts  32.8 us
    pallas_call x6, Pallas kernels, forward(): pl.pallas_call(forward_body, grid_spec=pltpu.PrefetchScalarGridSpec(num_s...  31.3 us
    pallas_call x4, Pallas kernels, pack(): pl.pallas_call(pack_body, grid_spec=pltpu.PrefetchScalarGridSpec(num_scal...  22.2 us
    pallas_call x1, Pallas kernels, middle(): pl.pallas_call(lambda *refs: middle_body(count, *refs), grid=(deep // blo...  19.4 us
    pallas_call x7, Pallas kernels, unpack(): pl.pallas_call(unpack_body, grid_spec=pltpu.PrefetchScalarGridSpec(num_sc...  18.1 us
  transfers between devices with their start and end apart: 83, of which 29 were waited for; matrix products, arithmetic and copies ran while one was open for 8% of the time, Pallas kernels for 16%

profile of v4, /device:TPU:0, one launch (start us, length us, event | category | flops | bytes accessed | tf_op | source)
XLA Modules:
  0.0 589.8 jit_solution(1950054452039003466)
XLA Ops:
  17.0 6.4 %pack.6 = (f32[2,8,3,4,24,128]{5,4,3,2,1,0:T(8,128)}, f32[2,8,3,4,24,128]{5,4,3,2,1,0:T(8,128)}) custom-call(s32[4]{0:T(128)} %get-tuple-element.212.scalars, f32[4,24,192,192]{3,2,1,0:T(8,128)} %give_ref.6, f32[4,24,192,192]{3,2,1,0:T(8,128)} %give_ref.6), custom_call_target="tpu_custom_call" | custom-call | tf_op jit(solution)/shard_map/pack/pallas_call | solution.py:75
  23.6 8.3 %pack.7 = (f32[2,8,3,4,24,128]{5,4,3,2,1,0:T(8,128)}, f32[2,8,3,4,24,128]{5,4,3,2,1,0:T(8,128)}) custom-call(s32[4]{0:T(128)} %get-tuple-element.214.scalars, f32[2,24,192,192]{3,2,1,0:T(8,128)} %give_ref.7, f32[2,24,192,192]{3,2,1,0:T(8,128)} %give_ref.7), custom_call_target="tpu_custom_call" | custom-call | tf_op jit(solution)/shard_map/pack/pallas_call | solution.py:75
  45.5 7.1 %collective-permute-done.3 = f32[4,3,4,24,128]{4,3,2,1,0:T(8,128)} collective-permute-done((f32[4,3,4,24,128]{4,3,2,1,0:T(8,128)}, f32[4,3,4,24,128]{4,3,2,1,0:T(8,128)}, u32[]{:S(2)}, u32[]{:S(2)}) %collective-permute-start.3) | collective-permute-done | bytes 589856 | tf_op jit(solution)/shard_map/ppermute | solution.py:270
  62.7 9.8 %collective-permute-done.4 = f32[4,3,4,24,128]{4,3,2,1,0:T(8,128)S(1)} collective-permute-done((f32[4,3,4,24,128]{4,3,2,1,0:T(8,128)S(1)}, f32[4,3,4,24,128]{4,3,2,1,0:T(8,128)S(1)}, u32[]{:S(2)}, u32[]{:S(2)}) %collective-permute-start.4) | collective-permute-done | bytes 589856 | tf_op jit(solution)/shard_map/ppermute | solution.py:270
  73.9 13.7 %collective-permute-done.9 = f32[8,3,4,24,128]{4,3,2,1,0:T(8,128)S(1)} collective-permute-done((f32[8,3,4,24,128]{4,3,2,1,0:T(8,128)S(1)}, f32[8,3,4,24,128]{4,3,2,1,0:T(8,128)S(1)}, u32[]{:S(2)}, u32[]{:S(2)}) %collective-permute-start.9) | collective-permute-done | bytes 1179680 | tf_op jit(solution)/shard_map/ppermute | solution.py:270
  91.3 5.3 collective-permute-start.11
  104.7 40.7 %collective-permute-done.12 = f32[6,3,4,24,128]{4,3,2,1,0:T(8,128)S(1)} collective-permute-done((f32[6,3,4,24,128]{4,3,2,1,0:T(8,128)S(1)}, f32[6,3,4,24,128]{4,3,2,1,0:T(8,128)S(1)}, u32[]{:S(2)}, u32[]{:S(2)}) %collective-permute-start.12) | collective-permute-done | bytes 884768 | tf_op jit(solution)/shard_map/ppermute | solution.py:270
  146.9 22.1 %collective-permute-done.14 = f32[4,3,4,24,128]{4,3,2,1,0:T(8,128)S(1)} collective-permute-done((f32[4,3,4,24,128]{4,3,2,1,0:T(8,128)S(1)}, f32[4,3,4,24,128]{4,3,2,1,0:T(8,128)S(1)}, u32[]{:S(2)}, u32[]{:S(2)}) %collective-permute-start.14) | collective-permute-done | bytes 589856 | tf_op jit(solution)/shard_map/ppermute | solution.py:270
  178.2 21.4 %collective-permute-done.16 = f32[6,3,4,24,128]{4,3,2,1,0:T(8,128)S(1)} collective-permute-done((f32[6,3,4,24,128]{4,3,2,1,0:T(8,128)S(1)}, f32[6,3,4,24,128]{4,3,2,1,0:T(8,128)S(1)}, u32[]{:S(2)}, u32[]{:S(2)}) %collective-permute-start.16) | collective-permute-done | bytes 884768 | tf_op jit(solution)/shard_map/ppermute | solution.py:270
  224.4 25.0 %collective-permute-done.23 = f32[6,3,4,24,128]{4,3,2,1,0:T(8,128)S(1)} collective-permute-done((f32[6,3,4,24,128]{4,3,2,1,0:T(8,128)S(1)}, f32[6,3,4,24,128]{4,3,2,1,0:T(8,128)S(1)}, u32[]{:S(2)}, u32[]{:S(2)}) %collective-permute-start.23) | collective-permute-done | bytes 884768 | tf_op jit(solution)/shard_map/ppermute | solution.py:270
  261.7 9.9 %forward.6 = (f32[96,32,192]{2,1,0:T(8,128)S(1)}, f32[96,32,192]{2,1,0:T(8,128)S(1)}) custom-call(s32[1]{0:T(128)} %bitcast.2.scalars, f32[4,4,3,4,24,128]{5,4,3,2,1,0:T(8,128)S(1)} %copy-done.15, f32[4,4,3,4,24,128]{5,4,3,2,1,0:T(8,128)S(1)} %copy-done.24, f32[4,4,3,4,24,128]{5,4,3,2,1,0:T(8,128)S(1)} %copy-done.3, f32[4,4,3,4,24,128]{5,4,3,2,1,0:T(8,128)S(1)} %copy-done.6, ...), custom_call_target="tpu_custom_call" | custom-call | tf_op jit(solution)/shard_map/forward/pallas_call | solution.py:163
  283.0 12.2 %collective-permute-done.28 = f32[2,3,4,24,128]{4,3,2,1,0:T(8,128)S(1)} collective-permute-done((f32[2,3,4,24,128]{4,3,2,1,0:T(8,128)S(1)}, f32[2,3,4,24,128]{4,3,2,1,0:T(8,128)S(1)}, u32[]{:S(2)}, u32[]{:S(2)}) %collective-permute-start.28) | collective-permute-done | bytes 294944 | tf_op jit(solution)/shard_map/ppermute | solution.py:270
  297.9 5.8 forward.7
  312.6 6.0 %forward.8 = (f32[96,16,192]{2,1,0:T(8,128)S(1)}, f32[96,16,192]{2,1,0:T(8,128)S(1)}) custom-call(s32[1]{0:T(128)} %bitcast.2.scalars, f32[4,2,3,4,24,128]{5,4,3,2,1,0:T(8,128)} %pad_maximum_fusion.4.near, f32[4,2,3,4,24,128]{5,4,3,2,1,0:T(8,128)} %collective-permute-done.27.far, f32[4,4,3,4,24,128]{5,4,3,2,1,0:T(8,128)S(1)} %pad_maximum_fusion.2.first, ...), custom_call_target="tpu_custom_call" | custom-call | tf_op jit(solution)/shard_map/forward/pallas_call | solution.py:163
  320.6 5.3 forward.9
  327.6 10.4 %collective-permute-done.35.second = f32[4,2,3,4,24,128]{5,4,3,2,1,0:T(8,128)S(1)} collective-permute-done((f32[4,2,3,4,24,128]{5,4,3,2,1,0:T(8,128)S(1)}, f32[4,2,3,4,24,128]{5,4,3,2,1,0:T(8,128)S(1)}, u32[]{:S(2)}, u32[]{:S(2)}) %collective-permute-start.35) | collective-permute-done | bytes 1179680 | tf_op jit(solution)/shard_map/ppermute | solution.py:270
  349.6 19.4 %middle.1 = (f32[96,32,192]{2,1,0:T(8,128)S(1)}, f32[96,16,192]{2,1,0:T(8,128)S(1)}, f32[96,16,192]{2,1,0:T(8,128)S(1)}, f32[96,16,192]{2,1,0:T(8,128)S(1)}, f32...) custom-call(f32[96,104,128]{2,1,0:T(8,128)} %fusion.1.refs_0_, ...), custom_call_target="tpu_custom_call" | custom-call | tf_op jit(solution)/shard_map/middle/pallas_call | solution.py:202
  379.0 12.3 %collective-permute-done.48 = f32[4,1,3,4,24,128]{5,4,3,2,1,0:T(8,128)S(1)} collective-permute-done((f32[4,1,3,4,24,128]{5,4,3,2,1,0:T(8,128)S(1)}, f32[4,1,3,4,24,128]{5,4,3,2,1,0:T(8,128)S(1)}, u32[]{:S(2)}, u32[]{:S(2)}) %collective-permute-start.48) | collective-permute-done | bytes 589856 | tf_op jit(solution)/shard_map/ppermute | solution.py:270
  396.6 5.6 inverse.11
  402.2 7.5 %collective-permute-done.51 = f32[1,3,4,24,128]{4,3,2,1,0:T(8,128)S(1)} collective-permute-done((f32[1,3,4,24,128]{4,3,2,1,0:T(8,128)S(1)}, f32[1,3,4,24,128]{4,3,2,1,0:T(8,128)S(1)}, u32[]{:S(2)}, u32[]{:S(2)}) %collective-permute-start.51) | collective-permute-done | bytes 147488 | tf_op jit(solution)/shard_map/ppermute | solution.py:270
  414.7 5.3 collective-permute-done.56
  425.3 5.6 inverse.10
  446.5 5.7 inverse.9
  454.4 13.7 %collective-permute-done.60 = f32[2,3,4,24,128]{4,3,2,1,0:T(8,128)S(1)} collective-permute-done((f32[2,3,4,24,128]{4,3,2,1,0:T(8,128)S(1)}, f32[2,3,4,24,128]{4,3,2,1,0:T(8,128)S(1)}, u32[]{:S(2)}, u32[]{:S(2)}) %collective-permute-start.60) | collective-permute-done | bytes 294944 | tf_op jit(solution)/shard_map/ppermute | solution.py:270
  473.7 6.3 %inverse.8 = (f32[4,2,3,4,24,128]{5,4,3,2,1,0:T(8,128)S(1)}, f32[4,2,3,4,24,128]{5,4,3,2,1,0:T(8,128)}) custom-call(s32[1]{0:T(128)} %bitcast.2.scalars, f32[96,32,192]{2,1,0:T(8,128)S(1)} %copy-done.10, f32[96,32,192]{2,1,0:T(8,128)} %collective-permute-done.42.got_ref, f32[4,4,3,4,24,128]{5,4,3,2,1,0:T(8,128)S(1)} %copy-done.4, ...), custom_call_target="tpu_custom_call" | custom-call | tf_op jit(solution)/shard_map/inverse/pallas_call | solution.py:240
  482.4 14.5 %collective-permute-done.65 = f32[2,3,4,24,128]{4,3,2,1,0:T(8,128)S(1)} collective-permute-done((f32[2,3,4,24,128]{4,3,2,1,0:T(8,128)S(1)}, f32[2,3,4,24,128]{4,3,2,1,0:T(8,128)S(1)}, u32[]{:S(2)}, u32[]{:S(2)}) %collective-permute-start.65) | collective-permute-done | bytes 294944 | tf_op jit(solution)/shard_map/ppermute | solution.py:270
  508.5 5.7 inverse.7
  518.2 8.8 %collective-permute-done.70 = f32[2,3,4,24,128]{4,3,2,1,0:T(8,128)} collective-permute-done((f32[2,3,4,24,128]{4,3,2,1,0:T(8,128)}, f32[2,3,4,24,128]{4,3,2,1,0:T(8,128)}, u32[]{:S(2)}, u32[]{:S(2)}) %collective-permute-start.70) | collective-permute-done | bytes 294944 | tf_op jit(solution)/shard_map/ppermute | solution.py:270
  537.7 4.9 collective-permute-done.76
  542.6 15.6 %collective-permute-done.75 = f32[2,3,4,24,128]{4,3,2,1,0:T(8,128)S(1)} collective-permute-done((f32[2,3,4,24,128]{4,3,2,1,0:T(8,128)S(1)}, f32[2,3,4,24,128]{4,3,2,1,0:T(8,128)S(1)}, u32[]{:S(2)}, u32[]{:S(2)}) %collective-permute-start.75) | collective-permute-done | bytes 294944 | tf_op jit(solution)/shard_map/ppermute | solution.py:270
  565.5 4.9 collective-permute-done.80
  570.4 14.5 %collective-permute-done.79 = f32[2,3,4,24,128]{4,3,2,1,0:T(8,128)S(1)} collective-permute-done((f32[2,3,4,24,128]{4,3,2,1,0:T(8,128)S(1)}, f32[2,3,4,24,128]{4,3,2,1,0:T(8,128)S(1)}, u32[]{:S(2)}, u32[]{:S(2)}) %collective-permute-start.79) | collective-permute-done | bytes 294944 | tf_op jit(solution)/shard_map/ppermute | solution.py:270
  (406 shorter events, 227.3 us)
Async XLA Ops:
  23.4 34.5 %collective-permute-start.8 = (f32[2,8,3,4,24,128]{5,4,3,2,1,0:T(8,128)}, f32[2,8,3,4,24,128]{5,4,3,2,1,0:T(8,128)}, u32[]{:S(2)}, u32[]{:S(2)}) collective-permute-start(f32[2,8,3,4,24,128]{5,4,3,2,1,0:T(8,128)} %get-tuple-element.218), channel_id=1, source_target_pairs={{0,8},{8,0},{16,24},{24,16},{1,9},{9,1},{17,25},{25,17},{2,10},{10... | collective-permute-start | bytes 7077896 | tf_op jit(solution)/shard_map/ppermute | solution.py:270
  31.8 28.9 %collective-permute-start.1 = (f32[2,8,3,4,24,128]{5,4,3,2,1,0:T(8,128)}, f32[2,8,3,4,24,128]{5,4,3,2,1,0:T(8,128)S(1)}, u32[]{:S(2)}, u32[]{:S(2)}) collective-permute-start(f32[2,8,3,4,24,128]{5,4,3,2,1,0:T(8,128)} %get-tuple-element.216), channel_id=1, source_target_pairs={{0,8},{8,0},{16,24},{24,16},{1,9},{9,1},{17,25},{25,17},{2,10},{10... | collective-permute-start | bytes 7077896 | tf_op jit(solution)/shard_map/ppermute | solution.py:270
  39.4 49.8 %collective-permute-start.5 = (f32[4,3,4,24,128]{4,3,2,1,0:T(8,128)}, f32[4,3,4,24,128]{4,3,2,1,0:T(8,128)S(1)}, u32[]{:S(2)}, u32[]{:S(2)}) collective-permute-start(f32[4,3,4,24,128]{4,3,2,1,0:T(8,128)} %get-tuple-element.207), channel_id=1, source_target_pairs={{0,2},{1,3},{2,0},{3,1},{4,6},{5,7},{6,4},{7,5},{8,10},{9,11},{10,... | collective-permute-start | bytes 1769480 | tf_op jit(solution)/shard_map/ppermute | solution.py:270
  41.1 48.2 %collective-permute-start.6 = (f32[4,3,4,24,128]{4,3,2,1,0:T(8,128)}, f32[4,3,4,24,128]{4,3,2,1,0:T(8,128)S(1)}, u32[]{:S(2)}, u32[]{:S(2)}) collective-permute-start(f32[4,3,4,24,128]{4,3,2,1,0:T(8,128)} %get-tuple-element.208), channel_id=1, source_target_pairs={{0,4},{1,5},{2,6},{3,7},{4,0},{5,1},{6,2},{7,3},{8,12},{9,13},{10,... | collective-permute-start | bytes 1769480 | tf_op jit(solution)/shard_map/ppermute | solution.py:270
  52.6 36.6 %collective-permute-start.7 = (f32[4,3,4,24,128]{4,3,2,1,0:T(8,128)S(1)}, f32[4,3,4,24,128]{4,3,2,1,0:T(8,128)S(1)}, u32[]{:S(2)}, u32[]{:S(2)}) collective-permute-start(f32[4,3,4,24,128]{4,3,2,1,0:T(8,128)S(1)} %copy-done.59), channel_id=1, source_target_pairs={{0,6},{1,7},{2,4},{3,5},{4,2},{5,3},{6,0},{7,1},{8,14},{9,15},{10,... | collective-permute-start | bytes 1769480 | tf_op jit(solution)/shard_map/ppermute | solution.py:270
  60.7 26.9 %collective-permute-start.9 = (f32[8,3,4,24,128]{4,3,2,1,0:T(8,128)S(1)}, f32[8,3,4,24,128]{4,3,2,1,0:T(8,128)S(1)}, u32[]{:S(2)}, u32[]{:S(2)}) collective-permute-start(f32[8,3,4,24,128]{4,3,2,1,0:T(8,128)S(1)} %fusion.7), channel_id=1, source_target_pairs={{0,1},{1,0},{2,3},{3,2},{4,5},{5,4},{6,7},{7,6},{8,9},{9,8},{10,11... | collective-permute-start | bytes 3538952 | tf_op jit(solution)/shard_map/ppermute | solution.py:270
  89.5 79.5 %collective-permute-start.15 = (f32[4,4,3,4,24,128]{5,4,3,2,1,0:T(8,128)S(1)}, f32[4,4,3,4,24,128]{5,4,3,2,1,0:T(8,128)S(1)}, u32[]{:S(2)}, u32[]{:S(2)}) collective-permute-start(f32[4,4,3,4,24,128]{5,4,3,2,1,0:T(8,128)S(1)} %pad_maximum_fusion.near), channel_id=1, source_target_pairs={{0,1},{1,0},{2,3},{3,2},{4,5},{5,4},{6,7},{7,6},{8,9},{9,8},{10,11... | collective-permute-start | bytes 7077896 | tf_op jit(solution)/shard_map/ppermute | solution.py:270
  91.3 54.2 %collective-permute-start.11 = (f32[6,3,4,24,128]{4,3,2,1,0:T(8,128)S(1)}, f32[6,3,4,24,128]{4,3,2,1,0:T(8,128)S(1)}, u32[]{:S(2)}, u32[]{:S(2)}) collective-permute-start(f32[6,3,4,24,128]{4,3,2,1,0:T(8,128)S(1)} %get-tuple-element.224), channel_id=1, source_target_pairs={{0,2},{1,3},{2,0},{3,1},{4,6},{5,7},{6,4},{7,5},{8,10},{9,11},{10,... | collective-permute-start | bytes 2654216 | tf_op jit(solution)/shard_map/ppermute | solution.py:270
  96.6 48.8 %collective-permute-start.12 = (f32[6,3,4,24,128]{4,3,2,1,0:T(8,128)S(1)}, f32[6,3,4,24,128]{4,3,2,1,0:T(8,128)S(1)}, u32[]{:S(2)}, u32[]{:S(2)}) collective-permute-start(f32[6,3,4,24,128]{4,3,2,1,0:T(8,128)S(1)} %get-tuple-element.225), channel_id=1, source_target_pairs={{0,4},{1,5},{2,6},{3,7},{4,0},{5,1},{6,2},{7,3},{8,12},{9,13},{10,... | collective-permute-start | bytes 2654216 | tf_op jit(solution)/shard_map/ppermute | solution.py:270
  97.7 48.7 %collective-permute-start.10 = (f32[8,3,4,24,128]{4,3,2,1,0:T(8,128)S(1)}, f32[8,3,4,24,128]{4,3,2,1,0:T(8,128)S(1)}, u32[]{:S(2)}, u32[]{:S(2)}) collective-permute-start(f32[8,3,4,24,128]{4,3,2,1,0:T(8,128)S(1)} %get-tuple-element.222), channel_id=1, source_target_pairs={{0,16},{8,24},{16,0},{24,8},{1,17},{9,25},{17,1},{25,9},{2,18},{10... | collective-permute-start | bytes 3538952 | tf_op jit(solution)/shard_map/ppermute | solution.py:270
  100.8 46.1 %collective-permute-start.13 = (f32[2,3,4,24,128]{4,3,2,1,0:T(8,128)S(1)}, f32[2,3,4,24,128]{4,3,2,1,0:T(8,128)S(1)}, u32[]{:S(2)}, u32[]{:S(2)}) collective-permute-start(f32[2,3,4,24,128]{4,3,2,1,0:T(8,128)S(1)} %get-tuple-element.226), channel_id=1, source_target_pairs={{0,6},{1,7},{2,4},{3,5},{4,2},{5,3},{6,0},{7,1},{8,14},{9,15},{10,... | collective-permute-start | bytes 884744 | tf_op jit(solution)/shard_map/ppermute | solution.py:270
  169.0 30.6 %collective-permute-start.16 = (f32[6,3,4,24,128]{4,3,2,1,0:T(8,128)S(1)}, f32[6,3,4,24,128]{4,3,2,1,0:T(8,128)S(1)}, u32[]{:S(2)}, u32[]{:S(2)}) collective-permute-start(f32[6,3,4,24,128]{4,3,2,1,0:T(8,128)S(1)} %get-tuple-element.234), channel_id=1, source_target_pairs={{0,2},{1,3},{2,0},{3,1},{4,6},{5,7},{6,4},{7,5},{8,10},{9,11},{10,... | collective-permute-start | bytes 2654216 | tf_op jit(solution)/shard_map/ppermute | solution.py:270
  169.2 32.2 %collective-permute-start.17 = (f32[6,3,4,24,128]{4,3,2,1,0:T(8,128)S(1)}, f32[6,3,4,24,128]{4,3,2,1,0:T(8,128)S(1)}, u32[]{:S(2)}, u32[]{:S(2)}) collective-permute-start(f32[6,3,4,24,128]{4,3,2,1,0:T(8,128)S(1)} %get-tuple-element.235), channel_id=1, source_target_pairs={{0,4},{1,5},{2,6},{3,7},{4,0},{5,1},{6,2},{7,3},{8,12},{9,13},{10,... | collective-permute-start | bytes 2654216 | tf_op jit(solution)/shard_map/ppermute | solution.py:270
  172.0 37.9 %collective-permute-start.18 = (f32[2,3,4,24,128]{4,3,2,1,0:T(8,128)S(1)}, f32[2,3,4,24,128]{4,3,2,1,0:T(8,128)S(1)}, u32[]{:S(2)}, u32[]{:S(2)}) collective-permute-start(f32[2,3,4,24,128]{4,3,2,1,0:T(8,128)S(1)} %get-tuple-element.236), channel_id=1, source_target_pairs={{0,6},{1,7},{2,4},{3,5},{4,2},{5,3},{6,0},{7,1},{8,14},{9,15},{10,... | collective-permute-start | bytes 884744 | tf_op jit(solution)/shard_map/ppermute | solution.py:270
  173.9 39.9 %collective-permute-start.21 = (f32[4,4,3,4,24,128]{5,4,3,2,1,0:T(8,128)S(1)}, f32[4,4,3,4,24,128]{5,4,3,2,1,0:T(8,128)S(1)}, u32[]{:S(2)}, u32[]{:S(2)}) collective-permute-start(f32[4,4,3,4,24,128]{5,4,3,2,1,0:T(8,128)S(1)} %pad_maximum_fusion.1.first), channel_id=1, source_target_pairs={{0,16},{8,24},{16,0},{24,8},{1,17},{9,25},{17,1},{25,9},{2,18},{10... | collective-permute-start | bytes 7077896 | tf_op jit(solution)/shard_map/ppermute | solution.py:270
  175.6 34.3 %collective-permute-start.20 = (f32[4,2,3,4,24,128]{5,4,3,2,1,0:T(8,128)S(1)}, f32[4,2,3,4,24,128]{5,4,3,2,1,0:T(8,128)S(1)}, u32[]{:S(2)}, u32[]{:S(2)}) collective-permute-start(f32[4,2,3,4,24,128]{5,4,3,2,1,0:T(8,128)S(1)} %pad_maximum_fusion.3.near), channel_id=1, source_target_pairs={{0,1},{1,0},{2,3},{3,2},{4,5},{5,4},{6,7},{7,6},{8,9},{9,8},{10,11... | collective-permute-start | bytes 3538952 | tf_op jit(solution)/shard_map/ppermute | solution.py:270
  215.2 60.4 %collective-permute-start.26 = (f32[4,4,3,4,24,128]{5,4,3,2,1,0:T(8,128)S(1)}, f32[4,4,3,4,24,128]{5,4,3,2,1,0:T(8,128)}, u32[]{:S(2)}, u32[]{:S(2)}) collective-permute-start(f32[4,4,3,4,24,128]{5,4,3,2,1,0:T(8,128)S(1)} %pad_maximum_fusion.2.first), channel_id=1, source_target_pairs={{0,16},{8,24},{16,0},{24,8},{1,17},{9,25},{17,1},{25,9},{2,18},{10... | collective-permute-start | bytes 7077896 | tf_op jit(solution)/shard_map/ppermute | solution.py:270
  218.6 30.8 %collective-permute-start.23 = (f32[6,3,4,24,128]{4,3,2,1,0:T(8,128)S(1)}, f32[6,3,4,24,128]{4,3,2,1,0:T(8,128)S(1)}, u32[]{:S(2)}, u32[]{:S(2)}) collective-permute-start(f32[6,3,4,24,128]{4,3,2,1,0:T(8,128)S(1)} %get-tuple-element.259), channel_id=1, source_target_pairs={{0,4},{1,5},{2,6},{3,7},{4,0},{5,1},{6,2},{7,3},{8,12},{9,13},{10,... | collective-permute-start | bytes 2654216 | tf_op jit(solution)/shard_map/ppermute | solution.py:270
  219.8 55.7 %collective-permute-start.27 = (f32[4,2,3,4,24,128]{5,4,3,2,1,0:T(8,128)}, f32[4,2,3,4,24,128]{5,4,3,2,1,0:T(8,128)}, u32[]{:S(2)}, u32[]{:S(2)}) collective-permute-start(f32[4,2,3,4,24,128]{5,4,3,2,1,0:T(8,128)} %pad_maximum_fusion.4.near), channel_id=1, source_target_pairs={{0,1},{1,0},{2,3},{3,2},{4,5},{5,4},{6,7},{7,6},{8,9},{9,8},{10,11... | collective-permute-start | bytes 3538952 | tf_op jit(solution)/shard_map/ppermute | solution.py:270
  224.4 49.0 %collective-permute-start.22 = (f32[6,3,4,24,128]{4,3,2,1,0:T(8,128)}, f32[6,3,4,24,128]{4,3,2,1,0:T(8,128)}, u32[]{:S(2)}, u32[]{:S(2)}) collective-permute-start(f32[6,3,4,24,128]{4,3,2,1,0:T(8,128)} %get-tuple-element.258), channel_id=1, source_target_pairs={{0,2},{1,3},{2,0},{3,1},{4,6},{5,7},{6,4},{7,5},{8,10},{9,11},{10,... | collective-permute-start | bytes 2654216 | tf_op jit(solution)/shard_map/ppermute | solution.py:270
  275.5 33.3 %collective-permute-start.33 = (f32[96,32,192]{2,1,0:T(8,128)S(1)}, f32[96,32,192]{2,1,0:T(8,128)S(1)}, u32[]{:S(2)}, u32[]{:S(2)}) collective-permute-start(f32[96,32,192]{2,1,0:T(8,128)S(1)} %get-tuple-element.290), channel_id=1, source_target_pairs={{0,8},{8,0},{16,24},{24,16},{1,9},{9,1},{17,25},{25,17},{2,10},{10... | collective-permute-start | bytes 7077896 | tf_op jit(solution)/shard_map/ppermute | solution.py:270
  276.8 29.3 %collective-permute-start.31 = (f32[4,2,3,4,24,128]{5,4,3,2,1,0:T(8,128)S(1)}, f32[4,2,3,4,24,128]{5,4,3,2,1,0:T(8,128)S(1)}, u32[]{:S(2)}, u32[]{:S(2)}) collective-permute-start(f32[4,2,3,4,24,128]{5,4,3,2,1,0:T(8,128)S(1)} %pad_maximum_fusion.5.near), channel_id=1, source_target_pairs={{0,1},{1,0},{2,3},{3,2},{4,5},{5,4},{6,7},{7,6},{8,9},{9,8},{10,11... | collective-permute-start | bytes 3538952 | tf_op jit(solution)/shard_map/ppermute | solution.py:270
  280.7 28.1 %collective-permute-start.32 = (f32[4,2,3,4,24,128]{5,4,3,2,1,0:T(8,128)S(1)}, f32[4,2,3,4,24,128]{5,4,3,2,1,0:T(8,128)S(1)}, u32[]{:S(2)}, u32[]{:S(2)}) collective-permute-start(f32[4,2,3,4,24,128]{5,4,3,2,1,0:T(8,128)S(1)} %pad_maximum_fusion.6.first), channel_id=1, source_target_pairs={{0,16},{8,24},{16,0},{24,8},{1,17},{9,25},{17,1},{25,9},{2,18},{10... | collective-permute-start | bytes 3538952 | tf_op jit(solution)/shard_map/ppermute | solution.py:270
  310.6 27.3 %collective-permute-start.35 = (f32[4,2,3,4,24,128]{5,4,3,2,1,0:T(8,128)S(1)}, f32[4,2,3,4,24,128]{5,4,3,2,1,0:T(8,128)S(1)}, u32[]{:S(2)}, u32[]{:S(2)}) collective-permute-start(f32[4,2,3,4,24,128]{5,4,3,2,1,0:T(8,128)S(1)} %pad_maximum_fusion.7.first), channel_id=1, source_target_pairs={{0,16},{8,24},{16,0},{24,8},{1,17},{9,25},{17,1},{25,9},{2,18},{10... | collective-permute-start | bytes 3538952 | tf_op jit(solution)/shard_map/ppermute | solution.py:270
  409.8 28.3 %collective-permute-start.53 = (f32[4,2,3,4,24,128]{5,4,3,2,1,0:T(8,128)}, f32[4,2,3,4,24,128]{5,4,3,2,1,0:T(8,128)}, u32[]{:S(2)}, u32[]{:S(2)}) collective-permute-start(f32[4,2,3,4,24,128]{5,4,3,2,1,0:T(8,128)} %get-tuple-element.348), channel_id=1, source_target_pairs={{0,1},{1,0},{2,3},{3,2},{4,5},{5,4},{6,7},{7,6},{8,9},{9,8},{10,11... | collective-permute-start | bytes 3538952 | tf_op jit(solution)/shard_map/ppermute | solution.py:270
  412.9 30.1 %collective-permute-start.43 = (f32[96,16,192]{2,1,0:T(8,128)}, f32[96,16,192]{2,1,0:T(8,128)}, u32[]{:S(2)}, u32[]{:S(2)}) collective-permute-start(f32[96,16,192]{2,1,0:T(8,128)} %get-tuple-element.324), channel_id=1, source_target_pairs={{0,8},{8,0},{16,24},{24,16},{1,9},{9,1},{17,25},{25,17},{2,10},{10... | collective-permute-start | bytes 3538952 | tf_op jit(solution)/shard_map/ppermute | solution.py:270
  414.4 57.5 %collective-permute-start.42 = (f32[96,32,192]{2,1,0:T(8,128)}, f32[96,32,192]{2,1,0:T(8,128)}, u32[]{:S(2)}, u32[]{:S(2)}) collective-permute-start(f32[96,32,192]{2,1,0:T(8,128)} %get-tuple-element.315), channel_id=1, source_target_pairs={{0,8},{8,0},{16,24},{24,16},{1,9},{9,1},{17,25},{25,17},{2,10},{10... | collective-permute-start | bytes 7077896 | tf_op jit(solution)/shard_map/ppermute | solution.py:270
  438.0 30.1 %collective-permute-start.58 = (f32[4,2,3,4,24,128]{5,4,3,2,1,0:T(8,128)S(1)}, f32[4,2,3,4,24,128]{5,4,3,2,1,0:T(8,128)S(1)}, u32[]{:S(2)}, u32[]{:S(2)}) collective-permute-start(f32[4,2,3,4,24,128]{5,4,3,2,1,0:T(8,128)S(1)} %get-tuple-element.356), channel_id=1, source_target_pairs={{0,1},{1,0},{2,3},{3,2},{4,5},{5,4},{6,7},{7,6},{8,9},{9,8},{10,11... | collective-permute-start | bytes 3538952 | tf_op jit(solution)/shard_map/ppermute | solution.py:270
  468.1 28.8 %collective-permute-start.63 = (f32[4,2,3,4,24,128]{5,4,3,2,1,0:T(8,128)S(1)}, f32[4,2,3,4,24,128]{5,4,3,2,1,0:T(8,128)S(1)}, u32[]{:S(2)}, u32[]{:S(2)}) collective-permute-start(f32[4,2,3,4,24,128]{5,4,3,2,1,0:T(8,128)S(1)} %get-tuple-element.365), channel_id=1, source_target_pairs={{0,1},{1,0},{2,3},{3,2},{4,5},{5,4},{6,7},{7,6},{8,9},{9,8},{10,11... | collective-permute-start | bytes 3538952 | tf_op jit(solution)/shard_map/ppermute | solution.py:270
  496.9 30.1 %collective-permute-start.68 = (f32[4,2,3,4,24,128]{5,4,3,2,1,0:T(8,128)}, f32[4,2,3,4,24,128]{5,4,3,2,1,0:T(8,128)}, u32[]{:S(2)}, u32[]{:S(2)}) collective-permute-start(f32[4,2,3,4,24,128]{5,4,3,2,1,0:T(8,128)} %get-tuple-element.374), channel_id=1, source_target_pairs={{0,1},{1,0},{2,3},{3,2},{4,5},{5,4},{6,7},{7,6},{8,9},{9,8},{10,11... | collective-permute-start | bytes 3538952 | tf_op jit(solution)/shard_map/ppermute | solution.py:270
  501.7 25.3 %collective-permute-start.70 = (f32[2,3,4,24,128]{4,3,2,1,0:T(8,128)}, f32[2,3,4,24,128]{4,3,2,1,0:T(8,128)}, u32[]{:S(2)}, u32[]{:S(2)}) collective-permute-start(f32[2,3,4,24,128]{4,3,2,1,0:T(8,128)} %get-tuple-element.420), channel_id=1, source_target_pairs={{0,4},{1,5},{2,6},{3,7},{4,0},{5,1},{6,2},{7,3},{8,12},{9,13},{10,... | collective-permute-start | bytes 884744 | tf_op jit(solution)/shard_map/ppermute | solution.py:270
  527.0 31.3 %collective-permute-start.73 = (f32[4,2,3,4,24,128]{5,4,3,2,1,0:T(8,128)S(1)}, f32[4,2,3,4,24,128]{5,4,3,2,1,0:T(8,128)S(1)}, u32[]{:S(2)}, u32[]{:S(2)}) collective-permute-start(f32[4,2,3,4,24,128]{5,4,3,2,1,0:T(8,128)S(1)} %get-tuple-element.383), channel_id=1, source_target_pairs={{0,1},{1,0},{2,3},{3,2},{4,5},{5,4},{6,7},{7,6},{8,9},{9,8},{10,11... | collective-permute-start | bytes 3538952 | tf_op jit(solution)/shard_map/ppermute | solution.py:270
  (123 other events, 1191.7 us)
